TPU v7x, 128 devices: a whole 4x4x4 slice. The times are simulated.
128 devices in a mesh: group: 4 (over z), dev: 32 (over x, y, core).
Axes of the slice: x: 4, y: 4, z: 4, core: 2. Of those that a mesh axis runs over, the one named last changes fastest.
Arguments:
- prompt_cache: bfloat16 [128, 2048, 576], P('group', 'dev'), may hold values from -6 to 6
- assignment: int32 [4, 32], P('group'), may hold values from 0 to 31, each once within a row
- resident_cache: bfloat16 [384, 512, 576], P(('group', 'dev')), may hold values from -6 to 6
- resident_len: int32 [128, 3], P(('group', 'dev')), may hold values from 1 to 512, 1024 in all within a row
- queries: bfloat16 [512, 128, 576], P(('group', 'dev')), may hold values from -240 to 240
- new_latent: bfloat16 [512, 576], P(('group', 'dev')), may hold values from -6 to 6
- residual: bfloat16 [512, 7168], P(('group', 'dev')), may hold values from -4 to 4
- w_uv: bfloat16 [128, 512, 128], P('dev'), may hold values from -0.25 to 0.25
- w_out: bfloat16 [16384, 7168], P('dev'), may hold values from -0.125 to 0.125
- norm_gain: bfloat16 [7168], replicated, may hold values from 0.25 to 1.75
- w_router: bfloat16 [7168, 32], replicated, may hold values from -0.125 to 0.125
- expert_ids: int32 [512, 8], replicated, may hold values from 0 to 31, all different within a row; in each aligned block of 512 rows (0 to 511, 512 to 1023, ...) at most 192 rows name the same one
- w_gate: bfloat16 [128, 7168, 256], P(('group', 'dev')), may hold values from -0.0625 to 0.0625
- w_up: bfloat16 [128, 7168, 256], P(('group', 'dev')), may hold values from -0.0625 to 0.0625
- w_down: bfloat16 [128, 256, 7168], P(('group', 'dev')), may hold values from -0.375 to 0.375
Outputs:
- layer_out: bfloat16 [512, 7168], P(('group', 'dev'))
Inputs may be any that keep to these rules, and one draw needn't show every extreme that they name: Each group's row of assignment names each of the 32 decode devices of that group once. `resident_len`: each device's 3 lengths sum to 1024. `expert_ids`: each row names 8 different experts; no expert is named by more than 192 rows.
All inputs are finite; a program needn't handle non-finite values.
Results may differ from a plain program's by a relative error of at most 0.033.
Values may be sent and summed in bfloat16 or wider, within the bound.
No kernel may reach another device: no remote copies, remote signals or barrier semaphores. Data moves between devices by JAX's collectives and lax.ppermute only.
A program may use at most 128 MiB of HBM per device.

v0:
```python
import jax
import jax.numpy as jnp
from jax import lax
from jax.sharding import PartitionSpec as P

LAT = 512
ROPE = 64
NOPE = 128
EXP_G = 8


def attend(query_row, cache_block, valid_mask, own_entry):
    scale_factor = (NOPE + ROPE) ** (-0.5)
    scores = (
        jnp.einsum("hc,kc->hk", query_row, cache_block, preferred_element_type=jnp.float32)
        * scale_factor
    )
    scores = jnp.where(valid_mask[None, :], scores, -jnp.inf)
    own_score = (
        jnp.einsum("hc,c->h", query_row, own_entry, preferred_element_type=jnp.float32)
        * scale_factor
    )
    maximum = jnp.maximum(jnp.max(scores, axis=1), own_score)
    exponent = jnp.exp(scores - maximum[:, None])
    own_exponent = jnp.exp(own_score - maximum)
    totals = jnp.sum(exponent, axis=1) + own_exponent
    weights = (exponent / totals[:, None]).astype(jnp.bfloat16)
    own_weight = (own_exponent / totals).astype(jnp.bfloat16)
    context = jnp.einsum(
        "hk,kl->hl", weights, cache_block[:, :LAT], preferred_element_type=jnp.float32
    )
    context = (
        context
        + own_weight.astype(jnp.float32)[:, None] * own_entry[:LAT].astype(jnp.float32)[None, :]
    )
    return context.astype(jnp.bfloat16)


def norm_rows(hidden, norm_gain):
    hidden_wide = hidden.astype(jnp.float32)
    scale_rows = lax.rsqrt(jnp.mean(hidden_wide * hidden_wide, axis=1, keepdims=True) + 1e-06)
    return (hidden_wide * scale_rows * norm_gain.astype(jnp.float32)[None, :]).astype(jnp.bfloat16)


def slot_table(flat_ids, which, capacity, top_count):
    matches = (flat_ids == which).astype(jnp.int32)
    slot_ranks = jnp.cumsum(matches) - matches
    row_flat = jnp.arange(flat_ids.shape[0], dtype=jnp.int32) // top_count
    hits = (slot_ranks[None, :] == jnp.arange(capacity, dtype=jnp.int32)[:, None]).astype(
        jnp.int32
    ) * matches[None, :]
    return (
        matches,
        slot_ranks,
        hits,
        jnp.sum(hits * row_flat[None, :], axis=1),
        jnp.sum(hits, axis=1),
    )


def per_device(
    prompt_cache,
    assignment,
    resident_cache,
    resident_len,
    queries,
    new_latent,
    residual,
    w_uv,
    w_out,
    norm_gain,
    w_router,
    expert_ids,
    w_gate,
    w_up,
    w_down,
):
    dev_count = lax.axis_size("dev")
    group_count = lax.axis_size("group")
    group_index = lax.axis_index("group")
    dev_index = lax.axis_index("dev")
    rows_dev = queries.shape[0]
    owners = assignment[0]
    owner_match = (owners[None, :] == jnp.arange(dev_count, dtype=jnp.int32)[:, None]).astype(
        jnp.int32
    )
    inverse = jnp.sum(owner_match * jnp.arange(dev_count, dtype=jnp.int32)[None, :], axis=1)
    outgoing = jnp.take(prompt_cache, inverse, axis=0)
    received = lax.all_to_all(outgoing, "dev", split_axis=0, concat_axis=1, tiled=True)
    prompt_mask = jnp.arange(received.shape[1], dtype=jnp.int32) >= 0
    context_new = attend(queries[0], received[0], prompt_mask, new_latent[0])
    slot_iota = jnp.arange(resident_cache.shape[1], dtype=jnp.int32)
    old_masks = slot_iota[None, :] < resident_len[0][:, None]
    context_old = jax.vmap(attend)(queries[1:], resident_cache, old_masks, new_latent[1:])
    context = jnp.concatenate([context_new[None], context_old], axis=0)
    context_heads = lax.all_to_all(context, "dev", split_axis=1, concat_axis=0, tiled=True)
    group_rows = context_heads.shape[0]
    attn_values = jnp.einsum(
        "rhl,hlv->rhv", context_heads, w_uv, preferred_element_type=jnp.float32
    ).astype(jnp.bfloat16)
    partial_value = jnp.dot(
        attn_values.reshape(group_rows, -1), w_out, preferred_element_type=jnp.float32
    )
    own_start = dev_index * rows_dev
    own_block = lax.dynamic_slice_in_dim(partial_value, own_start, rows_dev, 0) + residual.astype(
        jnp.float32
    )
    partial_value = lax.dynamic_update_slice_in_dim(partial_value, own_block, own_start, 0)
    attn_total = lax.psum(partial_value.astype(jnp.bfloat16), "dev")
    normed = norm_rows(attn_total, norm_gain)
    group_ids = lax.dynamic_slice_in_dim(expert_ids, group_index * group_rows, group_rows, 0)
    logits = jnp.dot(normed, w_router, preferred_element_type=jnp.float32)
    affinity = jax.nn.sigmoid(logits)
    picked = jnp.take_along_axis(affinity, group_ids, axis=1)
    gate_values = (2.5 * picked / jnp.sum(picked, axis=1, keepdims=True)).astype(jnp.bfloat16)
    all_normed, all_gates = (
        lax.all_gather(normed, "group", axis=0, tiled=True),
        lax.all_gather(gate_values, "group", axis=0, tiled=True),
    )
    total_rows = expert_ids.shape[0]
    top_count = expert_ids.shape[1]
    expert_count = EXP_G * group_count
    capacity = 3 * total_rows * top_count // (2 * expert_count)
    slices_per = dev_count // EXP_G
    expert = group_index * EXP_G + dev_index // slices_per
    flat_ids = expert_ids.reshape(total_rows * top_count)
    matches, slot_ranks, hits, slot_rows, filled = slot_table(flat_ids, expert, capacity, top_count)
    slot_gates = jnp.sum(
        hits.astype(jnp.float32)
        * all_gates.reshape(total_rows * top_count).astype(jnp.float32)[None, :],
        axis=1,
    )
    inputs = jnp.take(all_normed, slot_rows, axis=0) * filled[:, None].astype(jnp.bfloat16)
    gate_proj = jnp.dot(inputs, w_gate[0], preferred_element_type=jnp.float32)
    up_proj = jnp.dot(inputs, w_up[0], preferred_element_type=jnp.float32)
    activation = (jax.nn.silu(gate_proj) * up_proj).astype(jnp.bfloat16)
    scaled = (
        jnp.dot(activation, w_down[0], preferred_element_type=jnp.float32) * slot_gates[:, None]
    )
    row_matches = matches.reshape(total_rows, top_count)
    row_slot = jnp.sum(slot_ranks.reshape(total_rows, top_count) * row_matches, axis=1)
    row_has = jnp.sum(row_matches, axis=1)
    moe_rows = lax.psum_scatter(
        jnp.take(scaled, row_slot, axis=0) * row_has[:, None].astype(jnp.float32),
        ("group", "dev"),
        scatter_dimension=0,
        tiled=True,
    )
    own_hidden = lax.dynamic_slice_in_dim(attn_total, own_start, rows_dev, 0)
    return (own_hidden.astype(jnp.float32) + moe_rows).astype(jnp.bfloat16)


def solution(mesh):
    return jax.shard_map(
        per_device,
        mesh=mesh,
        in_specs=(
            P("group", "dev", None),
            P("group", None),
            P(("group", "dev"), None, None),
            P(("group", "dev"), None),
            P(("group", "dev"), None, None),
            P(("group", "dev"), None),
            P(("group", "dev"), None),
            P("dev", None, None),
            P("dev", None),
            P(),
            P(),
            P(),
            P(("group", "dev"), None, None),
            P(("group", "dev"), None, None),
            P(("group", "dev"), None, None),
        ),
        out_specs=P(("group", "dev"), None),
        check_vma=False,
    )
```

profile of v0, /device:TPU:1, one launch (start us, length us, event | category | flops | bytes accessed | tf_op | source)
XLA Modules:
  0.0 504.4 jit_solution(7817163631492629072)
XLA Ops:
  8.3 2.4 gather_fusion
  10.7 3.6 broadcast_select_fusion
  14.2 8.7 %all-to-all-start = ((bf16[32,64,576]{2,1,0:T(8,128)(2,1)}), bf16[32,64,576]{2,1,0:T(8,128)(2,1)S(1)}, u32[]{:S(2)}, u32[]{:S(2)}) async-start(bf16[32,64,576]{2,1,0:T(8,128)(2,1)} %broadcast_select_fusion), calls=%async_computation | async-start | bytes 5242880 | tf_op jit(solution)/shard_map/all_to_all | solution.py:89
  23.3 2.3 fusion.75
  25.9 1.4 fusion.19
  27.3 29.5 %all-to-all-done = bf16[32,64,576]{2,1,0:T(8,128)(2,1)S(1)} async-done(((bf16[32,64,576]{2,1,0:T(8,128)(2,1)}), bf16[32,64,576]{2,1,0:T(8,128)(2,1)S(1)}, u32[]{:S(2)}, u32[]{:S(2)}) %all-to-all-start) | async-done | bytes 2359328 | tf_op jit(solution)/shard_map/all_to_all | solution.py:89
  59.2 1.2 copy.50
  60.4 4.5 all-to-all-start.1
  65.0 11.7 %all-to-all-done.1 = bf16[4,128,512]{2,0,1:T(4,128)(2,1)S(1)} async-done(((bf16[4,128,512]{2,0,1:T(4,128)(2,1)}), bf16[4,128,512]{2,0,1:T(4,128)(2,1)S(1)}, u32[]{:S(2)}, u32[]{:S(2)}) %all-to-all-start.1) | async-done | bytes 524320 | tf_op jit(solution)/shard_map/all_to_all | solution.py:96
  77.4 4.3 fusion.78
  81.8 1.5 convert_element_type.125
  83.4 104.1 %all-reduce.4.cloned.1.call-done = bf16[128,7168]{1,0:T(8,128)(2,1)} async-done(((bf16[128,7168]{1,0:T(8,128)(2,1)}), bf16[128,7168]{1,0:T(8,128)(2,1)}) %all-reduce.4.cloned.1.call-update) | async-done | bytes 1835024 | tf_op jit(solution)/shard_map/psum | solution.py:109
  187.5 1.9 fusion
  189.4 3.4 fusion.2
  196.4 7.0 %gather_fusion.3 = f32[1024]{0:T(1024)S(1)} fusion(f32[128,32]{0,1:T(8,128)S(1)} %fusion.41, s32[1024]{0:T(1024)S(1)} %reshape.222), kind=kCustom, calls=%fused_computation.3 | custom fusion | bytes 16384 | tf_op jit(solution)/shard_map/jit(take_along_axis)/gather | solution.py:114
  203.6 9.5 %all_gather.7 = bf16[512,8]{0,1:T(8,128)(2,1)S(1)} all-gather(bf16[128,8]{0,1:T(8,128)(2,1)S(1)} %divide_convert_fusion.4), channel_id=1, replica_groups=mesh['group'=4,'dev'=32] {'group'}, dimensions={0}, use_global_device_ids=true | all-gather | bytes 10240 | tf_op jit(solution)/shard_map/all_gather | solution.py:118
  214.0 53.6 %all-gather.2.cloned.1.call-done = bf16[512,7168]{1,0:T(8,128)(2,1)} async-done(((bf16[128,7168]{1,0:T(8,128)(2,1)}), bf16[512,7168]{1,0:T(8,128)(2,1)}) %all-gather.2.cloned.1.call-update) | async-done | bytes 7340048 | tf_op jit(solution)/shard_map/all_gather | solution.py:117
  267.6 10.4 %gather_fusion.1 = bf16[192,7168]{1,0:T(8,128)(2,1)} fusion(bf16[512,7168]{1,0:T(8,128)(2,1)} %all-gather.2.cloned.1.call-done, s32[1024]{0:T(1024)S(1)} %pad_clamp_fusion.1), kind=kCustom, calls=%fused_computation.1 | custom fusion | bytes 5505792 | tf_op jit(solution)/shard_map/jit(_take)/gather | solution.py:133
  278.0 3.8 fusion.6
  281.8 9.4 %convolution_multiply_fusion = f32[192,7168]{1,0:T(8,128)} fusion(bf16[1,256,7168]{2,1,0:T(8,128)(2,1)} %param.29, f32[192]{0:T(256)S(1)} %fusion.10, bf16[1,7168,256]{2,1,0:T(8,128)(2,1)} %param.28, f32[192,256]{1,0:T(8,128)S(1)} %fusion.6, bf16[192,7168]{1,0:T(8,128)(2,1)} %gather_fusion.1, pred[192]{0:T(512)(128)(4,1)S(1)} %compare_and_fusion, ...), kind=kOutput, calls=%fused_computation.5 | convolution fusion | flops 1413709824 | bytes 15795520 | tf_op jit(solution)/shard_map/dot_general | solution.py:138
  291.3 16.8 %gather_fusion.2 = f32[512,7168]{1,0:T(8,128)} fusion(f32[192,7168]{1,0:T(8,128)} %convolution_multiply_fusion, s32[1024]{0:T(1024)S(1)} %pad_clamp_fusion), kind=kCustom, calls=%fused_computation.2 | custom fusion | bytes 29362176 | tf_op jit(solution)/shard_map/jit(_take)/gather | solution.py:144
  308.1 13.8 %select_multiply_fusion = f32[512,7168]{1,0:T(8,128)} fusion(f32[512,7168]{1,0:T(8,128)} %gather_fusion.2, f32[512]{0:T(512)S(1)} %convert_element_type.141, pred[512]{0:T(512)(128)(4,1)S(1)} %compare_and_fusion.1), kind=kLoop, calls=%fused_computation.4 | loop fusion | flops 7340032 | bytes 29362688 | tf_op jit(solution)/shard_map/mul | solution.py:144
  321.9 174.3 %all-reduce.6.cloned.1.call-done = f32[512,7168]{1,0:T(8,128)} async-done(((f32[512,7168]{1,0:T(8,128)}), f32[512,7168]{1,0:T(8,128)}) %all-reduce.6.cloned.1.call-update) | async-done | bytes 14680080
  496.2 1.7 fusion.58
  (91 shorter events, 10.0 us)
Async XLA Ops:
  6.5 1.8 copy-start
  14.2 8.7 %copy-start.11 = (s32[1,3]{1,0:T(1,128)S(1)}, s32[1,3]{1,0:T(1,128)}, u32[]{:S(2)}) copy-start(s32[1,3]{1,0:T(1,128)} %param.18) | copy-start | bytes 40
  14.2 8.8 %copy-start.9 = (bf16[4,576]{1,0:T(4,128)(2,1)S(1)}, bf16[4,576]{1,0:T(4,128)(2,1)}, u32[]{:S(2)}) copy-start(bf16[4,576]{1,0:T(4,128)(2,1)} %param.20) | copy-start | bytes 13828
  14.2 8.8 %copy-start.3 = (bf16[4,128,576]{1,2,0:T(8,128)(2,1)S(1)}, bf16[4,128,576]{1,2,0:T(8,128)(2,1)}, u32[]{:S(2)}) copy-start(bf16[4,128,576]{1,2,0:T(8,128)(2,1)} %param.19) | copy-start | bytes 1769476
  14.2 42.6 %all-to-all-start = ((bf16[32,64,576]{2,1,0:T(8,128)(2,1)}), bf16[32,64,576]{2,1,0:T(8,128)(2,1)S(1)}, u32[]{:S(2)}, u32[]{:S(2)}) async-start(bf16[32,64,576]{2,1,0:T(8,128)(2,1)} %broadcast_select_fusion), calls=%async_computation | async-start | bytes 5242880 | tf_op jit(solution)/shard_map/all_to_all | solution.py:89
  23.0 2.9 copy-start.12
  58.2 1.0 copy-start.6
  59.2 17.8 %copy-start.4 = (bf16[4,512,128]{2,1,0:T(8,128)(2,1)S(1)}, bf16[4,512,128]{2,1,0:T(8,128)(2,1)}, u32[]{:S(2)}) copy-start(bf16[4,512,128]{2,1,0:T(8,128)(2,1)} %param.22) | copy-start | bytes 1572868
  60.4 16.3 %all-to-all-start.1 = ((bf16[4,128,512]{2,0,1:T(4,128)(2,1)}), bf16[4,128,512]{2,0,1:T(4,128)(2,1)S(1)}, u32[]{:S(2)}, u32[]{:S(2)}) async-start(bf16[4,128,512]{2,0,1:T(4,128)(2,1)} %copy.50), calls=%async_computation.1 | async-start | bytes 1048576 | tf_op jit(solution)/shard_map/all_to_all | solution.py:96
  65.0 122.5 %all-reduce.4.cloned.1.call-start = ((), (), s32[]{:S(2)}) async-start(), calls=%async_computation.2 | async-start | bytes 3670016 | tf_op jit(solution)/shard_map/psum | solution.py:109
  77.4 4.3 copy-start.7
  81.8 1.6 copy-start.10
  83.3 184.3 %all-gather.2.cloned.1.call-start = ((), (), s32[]{:S(2)}) async-start(), calls=%async_computation.3 | async-start | bytes 9175040 | tf_op jit(solution)/shard_map/all_gather | solution.py:117
  189.4 3.5 copy-start.8
  189.4 6.2 %copy-start.5 = (bf16[7168,32]{0,1:T(8,128)(2,1)S(1)}, bf16[7168,32]{0,1:T(8,128)(2,1)}, u32[]{:S(2)}) copy-start(bf16[7168,32]{0,1:T(8,128)(2,1)} %param.25) | copy-start | bytes 1376260
  192.8 2.8 copy-start.2
  192.9 303.3 %all-reduce.6.cloned.1.call-start = ((), (), s32[]{:S(2)}) async-start(), calls=%async_computation.4 | async-start | bytes 29360128
  321.9 176.0 %copy-start.1 = (bf16[32,64,576]{2,1,0:T(8,128)(2,1)S(1)}, bf16[32,64,576]{2,1,0:T(8,128)(2,1)}, u32[]{:S(2)}) copy-start(bf16[32,64,576]{2,1,0:T(8,128)(2,1)} %param.15) | copy-start | bytes 7077892
Sparse Core Ops, SparseCore 0:
  83.4 103.9 all-reduce.3
  193.0 74.5 all-gather.1
  322.0 174.1 all-reduce.5
where the time goes:
time: 505 us; the launch traced here: 504 us
  waiting for transfers between devices  373 us (74%)
  local copies, waits for them, and re-layouts  41 us (8%)
  other arithmetic  29.7 us (6%)
  matrix products  24.1 us (5%)
  between operations  13.5 us (3%)
  starting transfers between devices  13.4 us (3%)
  blocking collectives  9.48 us (2%)
    unnamed x4, waiting for transfers between devices  174 us
    psum x1, waiting for transfers between devices, per_device(): attn_total = lax.psum(partial_value.astype(jnp.bfloat16), 'dev')  104 us
    all_gather x1, waiting for transfers between devices, per_device(): lax.all_gather(normed, 'group', axis=0, tiled=True)  53.6 us
    all_to_all x1, waiting for transfers between devices, per_device(): lax.all_to_all(outgoing, 'dev', split_axis=0, concat_axis=1, tiled=True)  29.5 us
    gather x1, local copies, waits for them, and re-layouts, per_device(): jnp.take(scaled, row_slot, axis=0) * row_has[:, None].astype(jnp.float32)  16.8 us
    mul x1, other arithmetic, per_device(): jnp.take(scaled, row_slot, axis=0) * row_has[:, None].astype(jnp.float32)  13.8 us
    all_to_all x1, waiting for transfers between devices, per_device(): lax.all_to_all(context, 'dev', split_axis=1, concat_axis=0, tiled=True)  11.7 us
    gather x1, local copies, waits for them, and re-layouts, per_device(): jnp.take(all_normed, slot_rows, axis=0)  10.4 us
  transfers between devices with their start and end apart: 5, of which 5 were waited for; matrix products, arithmetic and copies ran while one was open for 3% of the time, Pallas kernels for 0%

commit v1 on v0

v1 whole, which is shorter than its diff:
```python
import functools

import jax
import jax.numpy as jnp
from jax import lax
from jax.experimental import pallas as pl
from jax.experimental.pallas import tpu as pltpu
from jax.sharding import Mesh, PartitionSpec as P

LAT = 512
ROPE = 64
NOPE = 128
D = 7168
CAP = 192
NZ, NX, NY, NC = 4, 4, 4, 2
NXY = NX * NY
NDEV = NXY * NC
EXP_G = 8
CHUNK = D // NDEV
LANES = 256
GROUP = 4
BLK = CHUNK * GROUP
STEPS = NXY // GROUP
ROWS = 128
ALL_ROWS = ROWS * NZ
F32 = jnp.float32
BF16 = jnp.bfloat16
VMEM = 48 * 1024 * 1024


def attend(query_row, cache_block, valid_mask, own_entry):
    scale_factor = (NOPE + ROPE) ** (-0.5)
    scores = jnp.einsum("hc,kc->hk", query_row, cache_block, preferred_element_type=F32) * scale_factor
    if valid_mask is not None:
        scores = jnp.where(valid_mask[None, :], scores, -jnp.inf)
    own_score = jnp.einsum("hc,c->h", query_row, own_entry, preferred_element_type=F32) * scale_factor
    maximum = jnp.maximum(jnp.max(scores, axis=1), own_score)
    exponent = jnp.exp(scores - maximum[:, None])
    own_exponent = jnp.exp(own_score - maximum)
    totals = jnp.sum(exponent, axis=1) + own_exponent
    weights = (exponent / totals[:, None]).astype(BF16)
    own_weight = (own_exponent / totals).astype(BF16)
    context = jnp.einsum("hk,kl->hl", weights, cache_block[:, :LAT], preferred_element_type=F32)
    context = context + own_weight.astype(F32)[:, None] * own_entry[:LAT].astype(F32)[None, :]
    return context.astype(BF16)


def project_kernel(half_ref, attn_ref, place_ref, res_ref, w_ref, out_ref):
    acc = jnp.dot(attn_ref[...], w_ref[...], preferred_element_type=F32)
    acc = acc + jnp.dot(place_ref[...], res_ref[...], preferred_element_type=F32)
    for g in range(GROUP):
        part = acc[:, g * CHUNK : (g + 1) * CHUNK]
        out_ref[g, :, :CHUNK] = part.astype(out_ref.dtype)
        out_ref[g, :, CHUNK:] = jnp.zeros((ROWS, LANES - CHUNK), out_ref.dtype)


def project(half, attn, place, res, w_out, dtype):
    depth = attn.shape[1]
    return pl.pallas_call(
        project_kernel,
        grid_spec=pltpu.PrefetchScalarGridSpec(
            num_scalar_prefetch=1,
            grid=(STEPS,),
            in_specs=[
                pl.BlockSpec((ROWS, depth), lambda i, h: (0, 0)),
                pl.BlockSpec((ROWS, 16), lambda i, h: (0, 0)),
                pl.BlockSpec((16, BLK), lambda i, h: (0, h[0] * STEPS + i)),
                pl.BlockSpec((depth, BLK), lambda i, h: (0, h[0] * STEPS + i)),
            ],
            out_specs=pl.BlockSpec((GROUP, ROWS, LANES), lambda i, h: (i, 0, 0)),
        ),
        out_shape=jax.ShapeDtypeStruct((NXY, ROWS, LANES), dtype),
        compiler_params=pltpu.CompilerParams(vmem_limit_bytes=VMEM),
        cost_estimate=pl.CostEstimate(
            flops=2 * ROWS * depth * D // 2, bytes_accessed=depth * D + 2 * ROWS * D, transcendentals=0
        ),
        name="project",
    )(half, attn, place, res, w_out)


def gate_up_step(y_ref, wg_ref, wu_ref, gate, up, stats):
    for g in range(GROUP):
        rows = y_ref[g, :, :CHUNK]
        gate = gate + jnp.dot(rows, wg_ref[g * CHUNK : (g + 1) * CHUNK, :], preferred_element_type=F32)
        up = up + jnp.dot(rows, wu_ref[g * CHUNK : (g + 1) * CHUNK, :], preferred_element_type=F32)
        stats = stats + y_ref[g, :, CHUNK:].astype(F32)
    return gate, up, stats


def first_kernel(half_ref, y_ref, wg_ref, wu_ref, gate_ref, up_ref, stats_ref):
    @pl.when(pl.program_id(0) == 0)
    def _():
        gate_ref[...] = jnp.zeros_like(gate_ref)
        up_ref[...] = jnp.zeros_like(up_ref)
        stats_ref[...] = jnp.zeros_like(stats_ref)

    gate, up, stats = gate_up_step(y_ref, wg_ref, wu_ref, gate_ref[...], up_ref[...], stats_ref[...])
    gate_ref[...] = gate
    up_ref[...] = up
    stats_ref[...] = stats


def first_half(half, y, w_gate, w_up):
    hidden = w_gate.shape[1]
    acc = pl.BlockSpec((CAP, hidden), lambda i, h: (0, 0))
    return pl.pallas_call(
        first_kernel,
        grid_spec=pltpu.PrefetchScalarGridSpec(
            num_scalar_prefetch=1,
            grid=(STEPS,),
            in_specs=[
                pl.BlockSpec((GROUP, CAP, LANES), lambda i, h: (i, 0, 0)),
                pl.BlockSpec((BLK, hidden), lambda i, h: (h[0] * STEPS + i, 0)),
                pl.BlockSpec((BLK, hidden), lambda i, h: (h[0] * STEPS + i, 0)),
            ],
            out_specs=[acc, acc, pl.BlockSpec((CAP, LANES - CHUNK), lambda i, h: (0, 0))],
        ),
        out_shape=[
            jax.ShapeDtypeStruct((CAP, hidden), F32),
            jax.ShapeDtypeStruct((CAP, hidden), F32),
            jax.ShapeDtypeStruct((CAP, LANES - CHUNK), F32),
        ],
        compiler_params=pltpu.CompilerParams(vmem_limit_bytes=VMEM),
        cost_estimate=pl.CostEstimate(
            flops=2 * CAP * D * hidden, bytes_accessed=2 * D * hidden + CAP * D, transcendentals=0
        ),
        name="gate_up_first",
    )(half, y, w_gate, w_up)


def down_step(act, gates, wd_ref, out_ref):
    acc = jnp.dot(act, wd_ref[...], preferred_element_type=F32) * gates
    for g in range(GROUP):
        out_ref[g, :, :CHUNK] = acc[:, g * CHUNK : (g + 1) * CHUNK].astype(out_ref.dtype)
        out_ref[g, :, CHUNK:] = jnp.zeros((CAP, LANES - CHUNK), out_ref.dtype)


def second_kernel(
    half_ref, y_ref, wg_ref, wu_ref, wd_ref, gate0_ref, up0_ref, stats0_ref, mine_ref,
    act_ref, gates_ref, out_ref, gate_acc, up_acc, stats_acc,
):
    step = pl.program_id(0)

    @pl.when(step == 0)
    def _():
        gate_acc[...] = gate0_ref[...]
        up_acc[...] = up0_ref[...]
        stats_acc[...] = stats0_ref[...]

    @pl.when(step < STEPS)
    def _():
        gate, up, stats = gate_up_step(y_ref, wg_ref, wu_ref, gate_acc[...], up_acc[...], stats_acc[...])
        gate_acc[...] = gate
        up_acc[...] = up
        stats_acc[...] = stats

    @pl.when(step == STEPS - 1)
    def _():
        stats = stats_acc[...]
        square = stats[:, 16:17] + stats[:, 17:18]
        scale = lax.rsqrt(square * (1.0 / D) + 1e-6)
        affinity = jax.nn.sigmoid((stats[:, 0:8] + stats[:, 8:16]) * scale)
        own = jnp.sum(affinity * mine_ref[...], axis=1, keepdims=True)
        gates = 2.5 * own / jnp.sum(affinity, axis=1, keepdims=True)
        gates_ref[...] = jnp.broadcast_to(gates.astype(BF16).astype(F32), gates_ref.shape)
        gate = gate_acc[...] * scale
        up = up_acc[...] * scale
        act_ref[...] = (gate * jax.nn.sigmoid(gate) * up).astype(BF16)

    @pl.when(step >= STEPS)
    def _():
        down_step(act_ref[...], gates_ref[:, :1], wd_ref, out_ref)


def second_half(half, y, w_gate, w_up, w_down, gate, up, stats, mine):
    hidden = w_gate.shape[1]
    fixed = lambda i, h: (0, 0)
    return pl.pallas_call(
        second_kernel,
        grid_spec=pltpu.PrefetchScalarGridSpec(
            num_scalar_prefetch=1,
            grid=(2 * STEPS,),
            in_specs=[
                pl.BlockSpec((GROUP, CAP, LANES), lambda i, h: (jnp.minimum(i, STEPS - 1), 0, 0)),
                pl.BlockSpec((BLK, hidden), lambda i, h: (h[0] * STEPS + jnp.minimum(i, STEPS - 1), 0)),
                pl.BlockSpec((BLK, hidden), lambda i, h: (h[0] * STEPS + jnp.minimum(i, STEPS - 1), 0)),
                pl.BlockSpec((hidden, BLK), lambda i, h: (0, h[0] * STEPS + jnp.maximum(i - STEPS, 0))),
                pl.BlockSpec((CAP, hidden), fixed),
                pl.BlockSpec((CAP, hidden), fixed),
                pl.BlockSpec((CAP, LANES - CHUNK), fixed),
                pl.BlockSpec((CAP, EXP_G), fixed),
            ],
            out_specs=[
                pl.BlockSpec((CAP, hidden), fixed),
                pl.BlockSpec((CAP, 128), fixed),
                pl.BlockSpec((GROUP, CAP, LANES), lambda i, h: (jnp.maximum(i - STEPS, 0), 0, 0)),
            ],
            scratch_shapes=[
                pltpu.VMEM((CAP, hidden), F32),
                pltpu.VMEM((CAP, hidden), F32),
                pltpu.VMEM((CAP, LANES - CHUNK), F32),
            ],
        ),
        out_shape=[
            jax.ShapeDtypeStruct((CAP, hidden), BF16),
            jax.ShapeDtypeStruct((CAP, 128), F32),
            jax.ShapeDtypeStruct((NXY, CAP, LANES), BF16),
        ],
        compiler_params=pltpu.CompilerParams(vmem_limit_bytes=VMEM),
        cost_estimate=pl.CostEstimate(
            flops=3 * CAP * D * hidden, bytes_accessed=3 * D * hidden + 2 * CAP * D, transcendentals=0
        ),
        name="gate_up_second",
    )(half, y, w_gate, w_up, w_down, gate, up, stats, mine)


def down_kernel(half_ref, act_ref, gates_ref, wd_ref, out_ref):
    down_step(act_ref[...], gates_ref[:, :1], wd_ref, out_ref)


def down_half(half, act, gates, w_down):
    hidden = act.shape[1]
    return pl.pallas_call(
        down_kernel,
        grid_spec=pltpu.PrefetchScalarGridSpec(
            num_scalar_prefetch=1,
            grid=(STEPS,),
            in_specs=[
                pl.BlockSpec((CAP, hidden), lambda i, h: (0, 0)),
                pl.BlockSpec((CAP, 128), lambda i, h: (0, 0)),
                pl.BlockSpec((hidden, BLK), lambda i, h: (0, h[0] * STEPS + i)),
            ],
            out_specs=pl.BlockSpec((GROUP, CAP, LANES), lambda i, h: (i, 0, 0)),
        ),
        out_shape=jax.ShapeDtypeStruct((NXY, CAP, LANES), F32),
        compiler_params=pltpu.CompilerParams(vmem_limit_bytes=VMEM),
        cost_estimate=pl.CostEstimate(
            flops=CAP * D * hidden, bytes_accessed=D * hidden + 2 * CAP * D, transcendentals=0
        ),
        name="down_own",
    )(half, act, gates, w_down)


def split_pair(values):
    high = lax.reduce_precision(values, 8, 7)
    low = lax.reduce_precision(values - high, 8, 7)
    return high.astype(BF16), low.astype(BF16)


def swap_cores(values):
    return lax.ppermute(values, "c", [(0, 1), (1, 0)])


def per_device(
    prompt_cache,
    assignment,
    resident_cache,
    resident_len,
    queries,
    new_latent,
    residual,
    w_uv,
    w_out,
    norm_gain,
    w_router,
    expert_ids,
    w_gate,
    w_up,
    w_down,
):
    plane = lax.axis_index("z")
    core = lax.axis_index("c")
    place_xy = lax.axis_index("x") * NY + lax.axis_index("y")
    dev_index = place_xy * NC + core
    rows_dev = queries.shape[0]
    own_half = jnp.reshape(core, (1,)).astype(jnp.int32)
    other_half = 1 - own_half
    chunk = core * NXY + place_xy

    owners = assignment[0]
    dev_iota = jnp.arange(NDEV, dtype=jnp.int32)
    inverse = jnp.sum((owners[None, :] == dev_iota[:, None]).astype(jnp.int32) * dev_iota[None, :], axis=1)
    outgoing = prompt_cache.at[inverse].get(mode="promise_in_bounds")
    received = lax.all_to_all(outgoing, ("x", "y", "c"), 0, 0, tiled=True)

    ids_plane = expert_ids - plane * EXP_G
    named = jnp.any(expert_ids[:, :, None] == jnp.arange(NZ * EXP_G, dtype=jnp.int32)[None, None, :], axis=1)
    lower = (jnp.arange(ALL_ROWS)[:, None] > jnp.arange(ALL_ROWS)[None, :]).astype(BF16)
    ranks = jnp.dot(lower, named.astype(BF16), preferred_element_type=F32).astype(jnp.int32)
    ranks = jnp.where(named, ranks, -1)
    plane_ranks = lax.dynamic_slice_in_dim(ranks, plane * EXP_G, EXP_G, 1)
    slots = (plane_ranks.T[:, None, :] == jnp.arange(CAP, dtype=jnp.int32)[None, :, None]).astype(BF16)
    table = jnp.broadcast_to(slots[:, None], (EXP_G, 2, CAP, ALL_ROWS)).reshape(NXY * CAP, ALL_ROWS)
    own_expert = place_xy // 2
    own_slots = lax.dynamic_index_in_dim(slots, own_expert, 0, keepdims=False)
    slot_ids = jnp.dot(own_slots, ids_plane.astype(BF16), preferred_element_type=F32)
    mine = (slot_ids == own_expert.astype(F32)).astype(F32)
    group_ids = lax.dynamic_slice_in_dim(expert_ids, plane * ROWS, ROWS, 0)
    picks = (group_ids[:, :, None] == jnp.arange(NZ * EXP_G, dtype=jnp.int32)[None, None, :]).astype(F32)
    gain_chunk = lax.dynamic_slice_in_dim(norm_gain, chunk * CHUNK, CHUNK, 0).astype(F32)
    router_chunk = lax.dynamic_slice_in_dim(w_router, chunk * CHUNK, CHUNK, 0)
    row_iota = jnp.arange(ROWS, dtype=jnp.int32)
    place = (row_iota[:, None] == dev_index * rows_dev + jnp.arange(16, dtype=jnp.int32)[None, :]) & (
        jnp.arange(16) < rows_dev
    )[None, :]
    place = place.astype(BF16)
    res = jnp.pad(residual, ((0, 16 - rows_dev), (0, 0)))

    slot_iota = jnp.arange(resident_cache.shape[1], dtype=jnp.int32)
    old_masks = slot_iota[None, :] < resident_len[0][:, None]
    context_old = jax.vmap(attend)(queries[1:], resident_cache, old_masks, new_latent[1:])
    prompt = received.reshape(-1, received.shape[-1])
    context_new = attend(queries[0], prompt, None, new_latent[0])
    context = jnp.concatenate([context_new[None], context_old], axis=0)

    heads = w_uv.shape[0]
    context = context.reshape(rows_dev, NDEV, heads, LAT).transpose(1, 2, 0, 3)
    context = context.reshape(NDEV, heads * rows_dev, LAT)
    context = lax.all_to_all(context, ("x", "y", "c"), 0, 0, tiled=True)
    context = context.reshape(NDEV, heads, rows_dev, LAT)
    attn = jnp.einsum("shrl,hlv->srhv", context, w_uv, preferred_element_type=F32).astype(BF16)
    attn = attn.reshape(ROWS, -1)

    partial_other = project(other_half, attn, place, res, w_out, BF16)
    partial_got = swap_cores(partial_other)
    partial_own = project(own_half, attn, place, res, w_out, F32)
    partial = (partial_own + partial_got.astype(F32)).astype(BF16)
    partial = lax.all_to_all(partial, ("x", "y"), 0, 0, tiled=True)
    hidden = jnp.sum(partial[:, :, :CHUNK].astype(F32), axis=0).astype(BF16)

    hidden_wide = hidden.astype(F32)
    square = jnp.sum(hidden_wide * hidden_wide, axis=1, keepdims=True)
    scaled = (hidden_wide * gain_chunk[None, :]).astype(BF16)
    logits = jnp.dot(scaled, router_chunk, preferred_element_type=F32)
    picked = jnp.sum(picks * logits[:, None, :], axis=2)
    picked_high, picked_low = split_pair(picked)
    square_high, square_low = split_pair(square)
    spare = jnp.zeros((ROWS, LANES - CHUNK - 18), BF16)
    packed = jnp.concatenate([scaled, picked_high, picked_low, square_high, square_low, spare], axis=1)

    packed = jnp.broadcast_to(packed[None], (NZ, ROWS, LANES))
    packed = lax.all_to_all(packed, "z", 0, 0, tiled=True).reshape(ALL_ROWS, LANES)
    slotted = jnp.dot(table, packed, preferred_element_type=F32).astype(BF16).reshape(NXY, CAP, LANES)
    slotted = lax.all_to_all(slotted, ("x", "y"), 0, 0, tiled=True)

    slotted_other = swap_cores(slotted)
    gate, up, stats = first_half(own_half, slotted, w_gate[0], w_up[0])
    act, gates, out_other = second_half(
        other_half, slotted_other, w_gate[0], w_up[0], w_down[0], gate, up, stats, mine
    )
    out_got = swap_cores(out_other)
    out_own = down_half(own_half, act, gates, w_down[0])
    out = (out_own + out_got.astype(F32)).astype(BF16)
    out = lax.all_to_all(out, ("x", "y"), 0, 0, tiled=True)

    moe = lax.dot_general(
        table, out.reshape(NXY * CAP, LANES), (((0,), (0,)), ((), ())), preferred_element_type=F32
    )[:, :CHUNK].reshape(NZ, ROWS, CHUNK)
    mask = (jnp.arange(NZ) == plane).astype(F32)
    total = (moe + mask[:, None, None] * hidden_wide[None]).astype(BF16)
    total = total.reshape(NZ * NDEV, rows_dev, CHUNK)
    total = lax.all_to_all(total, ("z", "x", "y", "c"), 0, 0, tiled=True)
    total = jnp.sum(total.reshape(NZ, NXY, NC, rows_dev, CHUNK).astype(F32), axis=0)
    return total.transpose(2, 1, 0, 3).reshape(rows_dev, D).astype(BF16)


def solution(mesh):
    grid = Mesh(mesh.devices.reshape(NZ, NX, NY, NC), ("z", "x", "y", "c"))
    dev = ("x", "y", "c")
    every = ("z", "x", "y", "c")
    return jax.shard_map(
        per_device,
        mesh=grid,
        in_specs=(
            P("z", dev, None),
            P("z", None),
            P(every, None, None),
            P(every, None),
            P(every, None, None),
            P(every, None),
            P(every, None),
            P(dev, None, None),
            P(dev, None),
            P(),
            P(),
            P(),
            P(every, None, None),
            P(every, None, None),
            P(every, None, None),
        ),
        out_specs=P(every, None),
        check_vma=False,
    )
```

time: 505 us -> 220 us (0.44)
  waiting for transfers between devices: 373 us -> 81.4 us
  blocking collectives: 9.48 us -> 39.7 us
  local copies, waits for them, and re-layouts: 41 us -> 15.1 us
  Pallas kernels: 0 us -> 21.9 us
  other arithmetic: 29.7 us -> 10.4 us
  starting transfers between devices: 13.4 us -> 32.1 us
  between operations: 13.5 us -> 0.45 us
  matrix products: 24.1 us -> 17.9 us
    unnamed x4 -> x0, waiting for transfers between devices: 174 us -> none
    psum x1 -> x0, waiting for transfers between devices: 104 us -> none  [per_device(): attn_total = lax.psum(partial_value.astype(jnp.bfloat16), 'dev')]
    all_gather x1 -> x0, waiting for transfers between devices: 53.6 us -> none  [per_device(): lax.all_gather(normed, 'group', axis=0, tiled=True)]
    all_to_all x2 -> x5, waiting for transfers between devices: 41.2 us -> 81.4 us  [the longest x1 30.2 us: per_device(): received = lax.all_to_all(outgoing, ('x', 'y', 'c'), 0, 0, tiled=True)]
    all_to_all x0 -> x2, blocking collectives: none -> 39.7 us  [the longest x1 23.2 us: per_device(): slotted = lax.all_to_all(slotted, ('x', 'y'), 0, 0, tiled=True)]
    gather x8 -> x1, local copies, waits for them, and re-layouts: 36.9 us -> 2.37 us  [per_device(): outgoing = prompt_cache.at[inverse].get(mode='promise_in_bounds')]
    pallas_call x0 -> x5, Pallas kernels: none -> 21.9 us  [the longest x2 7.65 us: project(): pl.pallas_call(project_kernel, grid_spec=pltpu.PrefetchScalarGridSpec(num...]
    all_to_all x2 -> x5, starting transfers between devices: 13.2 us -> 27.1 us  [the longest x1 8.77 us: per_device(): received = lax.all_to_all(outgoing, ('x', 'y', 'c'), 0, 0, tiled=True)]
  transfers between devices with their start and end apart: 5 -> 8, of which waited for: 5 -> 5; matrix products, arithmetic and copies ran while one was open for 3% -> 4% of each run, Pallas kernels for 0% -> 5%
where the time goes in v1:
time: 220 us; the launch traced here: 219 us
  waiting for transfers between devices  81.4 us (37%)
  blocking collectives  39.7 us (18%)
  starting transfers between devices  32.1 us (15%)
  Pallas kernels  21.9 us (10%)
  matrix products  17.9 us (8%)
  local copies, waits for them, and re-layouts  15.1 us (7%)
  other arithmetic  10.4 us (5%)
    all_to_all x1, waiting for transfers between devices, per_device(): received = lax.all_to_all(outgoing, ('x', 'y', 'c'), 0, 0, tiled=True)  30.2 us
    all_to_all x1, blocking collectives, per_device(): slotted = lax.all_to_all(slotted, ('x', 'y'), 0, 0, tiled=True)  23.2 us
    all_to_all x1, waiting for transfers between devices, per_device(): out = lax.all_to_all(out, ('x', 'y'), 0, 0, tiled=True)  21 us
    all_to_all x1, blocking collectives, per_device(): total = lax.all_to_all(total, ('z', 'x', 'y', 'c'), 0, 0, tiled=True)  16.5 us
    all_to_all x1, waiting for transfers between devices, per_device(): partial = lax.all_to_all(partial, ('x', 'y'), 0, 0, tiled=True)  14.9 us
    all_to_all x1, waiting for transfers between devices, per_device(): context = lax.all_to_all(context, ('x', 'y', 'c'), 0, 0, tiled=True)  11.6 us
    all_to_all x1, starting transfers between devices, per_device(): received = lax.all_to_all(outgoing, ('x', 'y', 'c'), 0, 0, tiled=True)  8.77 us
    pallas_call x2, Pallas kernels, project(): pl.pallas_call(project_kernel, grid_spec=pltpu.PrefetchScalarGridSpec(num...  7.65 us
  transfers between devices with their start and end apart: 8, of which 5 were waited for; matrix products, arithmetic and copies ran while one was open for 4% of the time, Pallas kernels for 5%

profile of v1, /device:TPU:1, one launch (start us, length us, event | category | flops | bytes accessed | tf_op | source)
XLA Modules:
  0.0 218.9 jit_solution(15289450706794009783)
XLA Ops:
  1.8 2.4 %gather_fusion = bf16[32,64,576]{2,1,0:T(8,128)(2,1)} fusion(bf16[32,64,576]{2,1,0:T(8,128)(2,1)S(1)} %copy-done, s32[1024]{0:T(1024)S(1)} %pad_clamp_fusion), kind=kCustom, calls=%fused_computation | custom fusion | bytes 4718720 | tf_op jit(solution)/shard_map/gather | solution.py:283
  4.1 8.8 %all-to-all-start = ((bf16[32,64,576]{2,1,0:T(8,128)(2,1)}), bf16[32,64,576]{2,1,0:T(8,128)(2,1)}, u32[]{:S(2)}, u32[]{:S(2)}) async-start(bf16[32,64,576]{2,1,0:T(8,128)(2,1)} %gather_fusion), calls=%async_computation | async-start | bytes 5242880 | tf_op jit(solution)/shard_map/all_to_all | solution.py:284
  13.2 2.3 %fusion.60 = (f32[3,128]{1,0:T(4,128)S(1)}, f32[3,128,512]{2,1,0:T(8,128)S(1)}) fusion(bf16[4,128,576]{1,2,0:T(8,128)(2,1)S(1)} %copy-done.3, bf16[3,512,576]{1,2,0:T(8,128)(2,1)} %param.17, pred[3,512]{1,0:T(4,128)(4,1)S(1)} %iota_compare_fusion.7), kind=kOutput, calls=%fused_computation.101 | convolution fusion | flops 227081856 | bytes 3148800 | tf_op jit(solution)/shard_map/vmap(hc,kc->hk)/dot_general | solution.py:33
  16.7 30.2 %all-to-all-done = bf16[32,64,576]{2,1,0:T(8,128)(2,1)} async-done(((bf16[32,64,576]{2,1,0:T(8,128)(2,1)}), bf16[32,64,576]{2,1,0:T(8,128)(2,1)}, u32[]{:S(2)}, u32[]{:S(2)}) %all-to-all-start) | async-done | bytes 2359328 | tf_op jit(solution)/shard_map/all_to_all | solution.py:284
  46.9 2.6 %fusion.61 = (f32[128]{0:T(128)S(1)}, f32[2048,128]{1,0:T(8,128)S(1)}) fusion(bf16[2048,576]{1,0:T(8,128)(2,1)} %bitcast.6, bf16[4,128,576]{1,2,0:T(8,128)(2,1)} %param.19), kind=kOutput, calls=%fused_computation.102 | convolution fusion | flops 302514048 | bytes 3817984 | tf_op jit(solution)/shard_map/hc,kc->hk/dot_general | solution.py:33
  50.8 2.1 fusion.16
  54.2 4.5 %all-to-all-start.1 = ((bf16[32,16,512]{2,1,0:T(8,128)(2,1)}), bf16[32,16,512]{2,1,0:T(8,128)(2,1)S(1)}, u32[]{:S(2)}, u32[]{:S(2)}) async-start(bf16[32,16,512]{2,1,0:T(8,128)(2,1)} %copy.77), calls=%async_computation.1 | async-start | bytes 1048576 | tf_op jit(solution)/shard_map/all_to_all | solution.py:319
  58.8 11.6 %all-to-all-done.1 = bf16[32,16,512]{2,1,0:T(8,128)(2,1)S(1)} async-done(((bf16[32,16,512]{2,1,0:T(8,128)(2,1)}), bf16[32,16,512]{2,1,0:T(8,128)(2,1)S(1)}, u32[]{:S(2)}, u32[]{:S(2)}) %all-to-all-start.1) | async-done | bytes 524320 | tf_op jit(solution)/shard_map/all_to_all | solution.py:319
  72.2 3.8 %project.3 = bf16[16,128,256]{2,1,0:T(8,128)(2,1)S(1)} custom-call(s32[1]{0:T(128)S(6)} %sub.50.half_ref, bf16[128,512]{1,0:T(8,128)(2,1)S(1)} %bitcast.92, bf16[128,16]{1,0:T(8,128)(2,1)S(1)} %fusion.38.place_ref, bf16[16,7168]{1,0:T(8,128)(2,1)S(1)} %pad.4.res_ref, bf16[512,7168]{1,0:T(8,128)(2,1)} %w_ref.3), custom_call_target="tpu_custom_call" | custom-call | flops 469762048 | bytes 5505024 | tf_op jit(solution)/shard_map/project/pallas_call | solution.py:59
  76.1 3.8 %project.2 = f32[16,128,256]{2,1,0:T(8,128)S(1)} custom-call(s32[1]{0:T(128)} %bitcast.2.half_ref, bf16[128,512]{1,0:T(8,128)(2,1)S(1)} %bitcast.93, bf16[128,16]{1,0:T(8,128)(2,1)S(1)} %fusion.38.place_ref, bf16[16,7168]{1,0:T(8,128)(2,1)S(1)} %pad.4.res_ref, bf16[512,7168]{1,0:T(8,128)(2,1)} %w_ref.3), custom_call_target="tpu_custom_call" | custom-call | flops 469762048 | bytes 5505024 | tf_op jit(solution)/shard_map/project/pallas_call | solution.py:59
  81.4 4.3 %all-to-all-start.2 = ((bf16[16,128,256]{2,1,0:T(8,128)(2,1)}), bf16[16,128,256]{2,1,0:T(8,128)(2,1)}, u32[]{:S(2)}, u32[]{:S(2)}) async-start(bf16[16,128,256]{2,1,0:T(8,128)(2,1)} %add_convert_fusion.1), calls=%async_computation.2 | async-start | bytes 2097152 | tf_op jit(solution)/shard_map/all_to_all | solution.py:328
  86.8 14.9 %all-to-all-done.2 = bf16[16,128,256]{2,1,0:T(8,128)(2,1)} async-done(((bf16[16,128,256]{2,1,0:T(8,128)(2,1)}), bf16[16,128,256]{2,1,0:T(8,128)(2,1)}, u32[]{:S(2)}, u32[]{:S(2)}) %all-to-all-start.2) | async-done | bytes 1048608 | tf_op jit(solution)/shard_map/all_to_all | solution.py:328
  105.6 5.0 %all-to-all-start.3 = ((bf16[4,128,256]{2,1,0:T(8,128)(2,1)}), bf16[4,128,256]{2,1,0:T(8,128)(2,1)}, u32[]{:S(2)}, u32[]{:S(2)}) async-start(bf16[4,128,256]{2,1,0:T(8,128)(2,1)} %broadcast_in_dim.23), calls=%async_computation.3 | async-start | bytes 524288 | tf_op jit(solution)/shard_map/all_to_all | solution.py:342
  112.6 3.7 %all-to-all-done.3 = bf16[4,128,256]{2,1,0:T(8,128)(2,1)} async-done(((bf16[4,128,256]{2,1,0:T(8,128)(2,1)}), bf16[4,128,256]{2,1,0:T(8,128)(2,1)}, u32[]{:S(2)}, u32[]{:S(2)}) %all-to-all-start.3) | async-done | bytes 262176 | tf_op jit(solution)/shard_map/all_to_all | solution.py:342
  118.1 2.1 convolution_convert_fusion
  120.2 23.2 %all_to_all.35.y_ref = bf16[16,192,256]{2,1,0:T(8,128)(2,1)} all-to-all(bf16[16,192,256]{2,1,0:T(8,128)(2,1)S(1)} %bitcast.102), channel_id=1, replica_groups=mesh['z'=4,'x'=4,'y'=4,'c'=2] {'x','y'}, dimensions={0} | all-to-all | bytes 3145728 | tf_op jit(solution)/shard_map/all_to_all | solution.py:344
  143.4 4.8 %collective-permute-start.1 = (bf16[16,192,256]{2,1,0:T(8,128)(2,1)}, bf16[16,192,256]{2,1,0:T(8,128)(2,1)}, u32[]{:S(2)}, u32[]{:S(2)}) collective-permute-start(bf16[16,192,256]{2,1,0:T(8,128)(2,1)} %all_to_all.35.y_ref), channel_id=1, source_target_pairs={{0,1},{1,0},{2,3},{3,2},{4,5},{5,4},{6,7},{7,6},{8,9},{9,8},{10,11... | collective-permute-start | bytes 4718600 | tf_op jit(solution)/shard_map/ppermute | solution.py:251
  150.4 3.5 %gate_up_first.1 = (f32[192,256]{1,0:T(8,128)S(1)}, f32[192,256]{1,0:T(8,128)S(1)}, f32[192,32]{1,0:T(8,128)S(1)}) custom-call(s32[1]{0:T(128)} %bitcast.2.half_ref, bf16[16,192,256]{2,1,0:T(8,128)(2,1)} %all_to_all.35.y_ref, bf16[7168,256]{1,0:T(8,128)(2,1)S(1)} %bitcast.91, bf16[7168,256]{1,0:T(8,128)(2,1)} %bitcast.94), custom_call_target="tpu_custom_call" | custom-call | flops 704643072 | bytes 5046272 | tf_op jit(solution)/shard_map/gate_up_first/pallas_call | solution.py:106
  154.0 7.2 %gate_up_second.1 = (bf16[192,256]{1,0:T(8,128)(2,1)S(1)}, f32[192,128]{1,0:T(8,128)S(1)}, bf16[16,192,256]{2,1,0:T(8,128)(2,1)S(1)}) custom-call(s32[1]{0:T(128)S(6)} %sub.50.half_ref, bf16[16,192,256]{2,1,0:T(8,128)(2,1)} %collective-permute-done.1.y_ref, bf16[7168,256]{1,0:T(8,128)(2,1)} %bitcast.90, bf16[7168,256]{1,0:T(8,128)(2,1)} %bitcast.95, ...), custom_call_target="tpu_custom_call" | custom-call | flops 1056964608 | bytes 8257536 | tf_op jit(solution)/shard_map/gate_up_second/pallas_call | solution.py:178
  161.3 3.4 %down_own.1 = f32[16,192,256]{2,1,0:T(8,128)S(1)} custom-call(s32[1]{0:T(128)} %bitcast.2.half_ref, bf16[192,256]{1,0:T(8,128)(2,1)S(1)} %get-tuple-element.14.act_ref, f32[192,128]{1,0:T(8,128)S(1)} %get-tuple-element.15.gates_ref, bf16[256,7168]{1,0:T(8,128)(2,1)} %bitcast.97), custom_call_target="tpu_custom_call" | custom-call | flops 352321536 | bytes 4587520 | tf_op jit(solution)/shard_map/down_own/pallas_call | solution.py:223
  166.4 4.4 %all-to-all-start.5 = ((bf16[16,192,256]{2,1,0:T(8,128)(2,1)}), bf16[16,192,256]{2,1,0:T(8,128)(2,1)}, u32[]{:S(2)}, u32[]{:S(2)}) async-start(bf16[16,192,256]{2,1,0:T(8,128)(2,1)} %add_convert_fusion), calls=%async_computation.5 | async-start | bytes 3145728 | tf_op jit(solution)/shard_map/all_to_all | solution.py:354
  173.0 21.0 %all-to-all-done.5 = bf16[16,192,256]{2,1,0:T(8,128)(2,1)} async-done(((bf16[16,192,256]{2,1,0:T(8,128)(2,1)}), bf16[16,192,256]{2,1,0:T(8,128)(2,1)}, u32[]{:S(2)}, u32[]{:S(2)}) %all-to-all-start.5) | async-done | bytes 1572896 | tf_op jit(solution)/shard_map/all_to_all | solution.py:354
  194.0 4.2 %fusion.2 = f32[512,224]{1,0:T(8,128)} fusion(bf16[3072,512]{1,0:T(8,128)(2,1)} %bitcast.99, bf16[3072,256]{1,0:T(8,128)(2,1)} %bitcast.26), kind=kOutput, calls=%fused_computation.8 | convolution fusion | flops 704643072 | bytes 5177344 | tf_op jit(solution)/shard_map/slice | solution.py:356
  201.5 16.5 %all_to_all.36 = bf16[128,4,224]{2,1,0:T(4,128)(2,1)S(1)} all-to-all(bf16[128,4,224]{2,1,0:T(4,128)(2,1)S(1)} %add_convert_fusion.2), channel_id=1, replica_groups=mesh['z'=4,'x'=4,'y'=4,'c'=2] {'z','x','y','c'}, dimensions={0} | all-to-all | bytes 458752 | tf_op jit(solution)/shard_map/all_to_all | solution.py:362
  (85 shorter events, 27.9 us)
Async XLA Ops:
  0.0 1.8 copy-start
  4.1 8.8 %copy-start.7 = (s32[1,3]{1,0:T(1,128)S(1)}, s32[1,3]{1,0:T(1,128)}, u32[]{:S(2)}) copy-start(s32[1,3]{1,0:T(1,128)} %param.18) | copy-start | bytes 40
  4.1 8.9 %copy-start.6 = (bf16[4,576]{1,0:T(4,128)(2,1)S(1)}, bf16[4,576]{1,0:T(4,128)(2,1)}, u32[]{:S(2)}) copy-start(bf16[4,576]{1,0:T(4,128)(2,1)} %param.20) | copy-start | bytes 13828
  4.1 8.9 %copy-start.3 = (bf16[4,128,576]{1,2,0:T(8,128)(2,1)S(1)}, bf16[4,128,576]{1,2,0:T(8,128)(2,1)}, u32[]{:S(2)}) copy-start(bf16[4,128,576]{1,2,0:T(8,128)(2,1)} %param.19) | copy-start | bytes 1769476
  4.1 42.7 %all-to-all-start = ((bf16[32,64,576]{2,1,0:T(8,128)(2,1)}), bf16[32,64,576]{2,1,0:T(8,128)(2,1)}, u32[]{:S(2)}, u32[]{:S(2)}) async-start(bf16[32,64,576]{2,1,0:T(8,128)(2,1)} %gather_fusion), calls=%async_computation | async-start | bytes 5242880 | tf_op jit(solution)/shard_map/all_to_all | solution.py:284
  13.2 2.6 %copy-start.8 = (bf16[3,512,576]{1,2,0:T(8,128)(2,1)S(1)}, bf16[3,512,576]{1,2,0:T(8,128)(2,1)}, u32[]{:S(2)}) copy-start(bf16[3,512,576]{1,2,0:T(8,128)(2,1)} %param.17) | copy-start | bytes 5308420
  53.0 5.8 %copy-start.5 = (bf16[4,7168]{1,0:T(4,128)(2,1)S(1)}, bf16[4,7168]{1,0:T(4,128)(2,1)}, u32[]{:S(2)}) copy-start(bf16[4,7168]{1,0:T(4,128)(2,1)} %param.21) | copy-start | bytes 172036
  54.2 16.3 %all-to-all-start.1 = ((bf16[32,16,512]{2,1,0:T(8,128)(2,1)}), bf16[32,16,512]{2,1,0:T(8,128)(2,1)S(1)}, u32[]{:S(2)}, u32[]{:S(2)}) async-start(bf16[32,16,512]{2,1,0:T(8,128)(2,1)} %copy.77), calls=%async_computation.1 | async-start | bytes 1048576 | tf_op jit(solution)/shard_map/all_to_all | solution.py:319
  76.0 4.0 %collective-permute-start = (bf16[16,128,256]{2,1,0:T(8,128)(2,1)S(1)}, bf16[16,128,256]{2,1,0:T(8,128)(2,1)S(1)}, u32[]{:S(2)}, u32[]{:S(2)}) collective-permute-start(bf16[16,128,256]{2,1,0:T(8,128)(2,1)S(1)} %project.3), channel_id=1, source_target_pairs={{0,1},{1,0},{2,3},{3,2},{4,5},{5,4},{6,7},{7,6},{8,9},{9,8},{10,11... | collective-permute-start | bytes 3145736 | tf_op jit(solution)/shard_map/ppermute | solution.py:251
  80.0 6.5 %copy-start.4 = (s32[512,8]{0,1:T(8,128)S(1)}, s32[512,8]{0,1:T(8,128)}, u32[]{:S(2)}) copy-start(s32[512,8]{0,1:T(8,128)} %param.26) | copy-start | bytes 49156
  81.4 20.3 %all-to-all-start.2 = ((bf16[16,128,256]{2,1,0:T(8,128)(2,1)}), bf16[16,128,256]{2,1,0:T(8,128)(2,1)}, u32[]{:S(2)}, u32[]{:S(2)}) async-start(bf16[16,128,256]{2,1,0:T(8,128)(2,1)} %add_convert_fusion.1), calls=%async_computation.2 | async-start | bytes 2097152 | tf_op jit(solution)/shard_map/all_to_all | solution.py:328
  105.6 10.7 %all-to-all-start.3 = ((bf16[4,128,256]{2,1,0:T(8,128)(2,1)}), bf16[4,128,256]{2,1,0:T(8,128)(2,1)}, u32[]{:S(2)}, u32[]{:S(2)}) async-start(bf16[4,128,256]{2,1,0:T(8,128)(2,1)} %broadcast_in_dim.23), calls=%async_computation.3 | async-start | bytes 524288 | tf_op jit(solution)/shard_map/all_to_all | solution.py:342
  118.1 2.1 copy-start.2
  143.4 10.6 %collective-permute-start.1 = (bf16[16,192,256]{2,1,0:T(8,128)(2,1)}, bf16[16,192,256]{2,1,0:T(8,128)(2,1)}, u32[]{:S(2)}, u32[]{:S(2)}) collective-permute-start(bf16[16,192,256]{2,1,0:T(8,128)(2,1)} %all_to_all.35.y_ref), channel_id=1, source_target_pairs={{0,1},{1,0},{2,3},{3,2},{4,5},{5,4},{6,7},{7,6},{8,9},{9,8},{10,11... | collective-permute-start | bytes 4718600 | tf_op jit(solution)/shard_map/ppermute | solution.py:251
  148.4 2.0 copy-start.1
  161.2 3.5 %collective-permute-start.2 = (bf16[16,192,256]{2,1,0:T(8,128)(2,1)S(1)}, bf16[16,192,256]{2,1,0:T(8,128)(2,1)S(1)}, u32[]{:S(2)}, u32[]{:S(2)}) collective-permute-start(bf16[16,192,256]{2,1,0:T(8,128)(2,1)S(1)} %get-tuple-element.16), channel_id=1, source_target_pairs={{0,1},{1,0},{2,3},{3,2},{4,5},{5,4},{6,7},{7,6},{8,9},{9,8},{10,11... | collective-permute-start | bytes 4718600 | tf_op jit(solution)/shard_map/ppermute | solution.py:251
  166.4 27.7 %all-to-all-start.5 = ((bf16[16,192,256]{2,1,0:T(8,128)(2,1)}), bf16[16,192,256]{2,1,0:T(8,128)(2,1)}, u32[]{:S(2)}, u32[]{:S(2)}) async-start(bf16[16,192,256]{2,1,0:T(8,128)(2,1)} %add_convert_fusion), calls=%async_computation.5 | async-start | bytes 3145728 | tf_op jit(solution)/shard_map/all_to_all | solution.py:354

commit v2 on v1

v2 whole, which is shorter than its diff:
```python
import functools

import jax
import jax.numpy as jnp
from jax import lax
from jax.experimental import pallas as pl
from jax.experimental.pallas import tpu as pltpu
from jax.sharding import Mesh, PartitionSpec as P

LAT = 512
ROPE = 64
NOPE = 128
D = 7168
CAP = 192
NZ, NX, NY, NC = 4, 4, 4, 2
NXY = NX * NY
NDEV = NXY * NC
EXP_G = 8
CHUNK = D // NDEV
LANES = 256
GROUP = 4
BLK = CHUNK * GROUP
STEPS = NXY // GROUP
ROWS = 128
ALL_ROWS = ROWS * NZ
F32 = jnp.float32
BF16 = jnp.bfloat16
SMALL = 16 * 1024 * 1024
LARGE = 20 * 1024 * 1024


def kept(shape, dtype):
    return pltpu.VMEM(shape, dtype)


def in_hbm(array):
    return pltpu.with_memory_space_constraint(array, pltpu.HBM)


def start_all(copies):
    for copy in copies:
        copy.start()
    return copies


WHOLE = pl.BlockSpec(memory_space=pltpu.VMEM)
SCALAR = pl.BlockSpec(memory_space=pltpu.SMEM)
ANYWHERE = pl.BlockSpec(memory_space=pl.ANY)


def attend(query_row, cache_block, valid_mask, own_entry):
    scale_factor = (NOPE + ROPE) ** (-0.5)
    scores = jnp.einsum("hc,kc->hk", query_row, cache_block, preferred_element_type=F32) * scale_factor
    if valid_mask is not None:
        scores = jnp.where(valid_mask[None, :], scores, -jnp.inf)
    own_score = jnp.einsum("hc,c->h", query_row, own_entry, preferred_element_type=F32) * scale_factor
    maximum = jnp.maximum(jnp.max(scores, axis=1), own_score)
    exponent = jnp.exp(scores - maximum[:, None])
    own_exponent = jnp.exp(own_score - maximum)
    totals = jnp.sum(exponent, axis=1) + own_exponent
    weights = (exponent / totals[:, None]).astype(BF16)
    own_weight = (own_exponent / totals).astype(BF16)
    context = jnp.einsum("hk,kl->hl", weights, cache_block[:, :LAT], preferred_element_type=F32)
    context = context + own_weight.astype(F32)[:, None] * own_entry[:LAT].astype(F32)[None, :]
    return context.astype(BF16)


def spread_kernel(owners_ref, cache_ref, out_ref, held_ref, in_sem, out_sem):
    arrive = [pltpu.make_async_copy(cache_ref.at[p], held_ref.at[p], in_sem.at[p]) for p in range(NDEV)]
    leave = [
        pltpu.make_async_copy(held_ref.at[p], out_ref.at[owners_ref[0, p]], out_sem.at[p]) for p in range(NDEV)
    ]
    start_all(arrive)
    for p in range(NDEV):
        arrive[p].wait()
        leave[p].start()
    for p in range(NDEV):
        leave[p].wait()


def spread(owners, cache):
    return pl.pallas_call(
        spread_kernel,
        in_specs=[SCALAR, ANYWHERE],
        out_specs=ANYWHERE,
        scratch_shapes=[
            pltpu.VMEM(cache.shape, cache.dtype),
            pltpu.SemaphoreType.DMA((NDEV,)),
            pltpu.SemaphoreType.DMA((NDEV,)),
        ],
        out_shape=pltpu.HBM(cache.shape, cache.dtype),
        compiler_params=pltpu.CompilerParams(vmem_limit_bytes=SMALL),
        name="spread",
    )(owners, in_hbm(cache))


def prompt_kernel(
    query_hbm, cache_ref, entry_ref, old_hbm, uv_hbm, w_hbm, out_ref, uv_ref, w_ref, all_ref, query_ref, sems
):
    heads_all = query_hbm.shape[1]
    query_copy = pltpu.make_async_copy(query_hbm, query_ref, sems.at[0])
    old_copy = pltpu.make_async_copy(old_hbm, all_ref.at[pl.ds(heads_all, old_hbm.shape[0]), :], sems.at[1])
    uv_copy = pltpu.make_async_copy(uv_hbm, uv_ref, sems.at[2])
    w_copy = pltpu.make_async_copy(w_hbm, w_ref, sems.at[3])
    start_all((query_copy, old_copy, uv_copy, w_copy))
    scale_factor = (NOPE + ROPE) ** (-0.5)
    cache = cache_ref[...].reshape(-1, cache_ref.shape[-1])
    entry = entry_ref[:1, :]
    query_copy.wait()
    query = query_ref[...]
    scores = jnp.dot(cache, query, preferred_element_type=F32) * scale_factor
    own_score = jnp.dot(entry, query, preferred_element_type=F32) * scale_factor
    maximum = jnp.maximum(jnp.max(scores, axis=0, keepdims=True), own_score)
    exponent = jnp.exp(scores - maximum)
    own_exponent = jnp.exp(own_score - maximum)
    totals = jnp.sum(exponent, axis=0, keepdims=True) + own_exponent
    weights = (exponent / totals).astype(BF16)
    own_weight = (own_exponent / totals).astype(BF16)
    over_rows = (((0,), (0,)), ((), ()))
    context = lax.dot_general(weights, cache[:, :LAT], over_rows, preferred_element_type=F32)
    context = context + lax.dot_general(own_weight, entry[:, :LAT], over_rows, preferred_element_type=F32)
    all_ref[:heads_all, :] = context.astype(BF16)
    rows, block = out_ref.shape[0], out_ref.shape[0] // NDEV
    heads = heads_all // NDEV
    to = lax.broadcasted_iota(jnp.int32, (rows, rows), 0)
    source = (to % block) // heads * heads_all + to // block * heads + to % heads
    order = (lax.broadcasted_iota(jnp.int32, (rows, rows), 1) == source).astype(BF16)
    old_copy.wait()
    out_ref[...] = jnp.dot(order, all_ref[...], preferred_element_type=F32).astype(BF16)
    uv_copy.wait()
    w_copy.wait()


def prompt_attention(query, cache, entry, old, w_uv, w_out):
    rows = query.shape[1] + old.shape[0]
    return pl.pallas_call(
        prompt_kernel,
        in_specs=[ANYWHERE, WHOLE, WHOLE, ANYWHERE, ANYWHERE, ANYWHERE],
        out_specs=[WHOLE, ANYWHERE, ANYWHERE],
        out_shape=[
            kept((rows, LAT), BF16), kept(w_uv.shape, BF16), kept(w_out.shape, BF16),
        ],
        scratch_shapes=[
            pltpu.VMEM((rows, LAT), BF16),
            pltpu.VMEM(query.shape, BF16),
            pltpu.SemaphoreType.DMA((4,)),
        ],
        compiler_params=pltpu.CompilerParams(vmem_limit_bytes=LARGE),
        name="prompt_attention",
    )(in_hbm(query), cache, entry, in_hbm(old), in_hbm(w_uv), in_hbm(w_out))


def project_half(half, attn, place_ref, res_ref, w_ref, out_ref):
    for i in range(STEPS):
        at = pl.ds(pl.multiple_of((half * STEPS + i) * BLK, 128), BLK)
        acc = jnp.dot(attn, w_ref[:, at], preferred_element_type=F32)
        acc = acc + jnp.dot(place_ref[...], res_ref[:, at], preferred_element_type=F32)
        for g in range(GROUP):
            part = acc[:, g * CHUNK : (g + 1) * CHUNK]
            out_ref[i * GROUP + g, :, :CHUNK] = part.astype(out_ref.dtype)
            out_ref[i * GROUP + g, :, CHUNK:] = jnp.zeros((ROWS, LANES - CHUNK), out_ref.dtype)


def project_first_kernel(half_ref, context_ref, uv_ref, place_ref, res_ref, w_ref, out_ref, attn_ref):
    heads, rows = uv_ref.shape[0], context_ref.shape[0]
    context = context_ref[...]
    pick = lax.broadcasted_iota(jnp.int32, (ROWS, rows), 1) // heads
    pick = (pick == lax.broadcasted_iota(jnp.int32, (ROWS, rows), 0)).astype(BF16)
    head = lax.broadcasted_iota(jnp.int32, (rows, uv_ref.shape[2]), 0) % heads
    for h in range(heads):
        values = jnp.dot(context, uv_ref[h], preferred_element_type=F32)
        values = jnp.where(head == h, values, 0.0).astype(BF16)
        values = jnp.dot(pick, values, preferred_element_type=F32).astype(BF16)
        attn_ref[:, h * values.shape[1] : (h + 1) * values.shape[1]] = values
    project_half(half_ref[0], attn_ref[...], place_ref, res_ref, w_ref, out_ref)


def project_second_kernel(half_ref, attn_ref, place_ref, res_ref, w_ref, out_ref):
    project_half(half_ref[0], attn_ref[...], place_ref, res_ref, w_ref, out_ref)


def project_call(kernel, name, out_shape, args, depth):
    return pl.pallas_call(
        kernel,
        in_specs=[SCALAR] + [WHOLE] * (len(args) - 1),
        out_specs=[WHOLE] * len(out_shape),
        out_shape=out_shape,
        compiler_params=pltpu.CompilerParams(vmem_limit_bytes=SMALL),
        cost_estimate=pl.CostEstimate(
            flops=2 * ROWS * depth * D // 2, bytes_accessed=depth * D + 2 * ROWS * D, transcendentals=0
        ),
        name=name,
    )(*args)


def project_first(half, context, w_uv, place, res, w_out):
    depth = w_out.shape[0]
    return project_call(
        project_first_kernel,
        "project_first",
        [kept((NXY, ROWS, LANES), BF16), kept((ROWS, depth), BF16)],
        (half, context, w_uv, place, res, w_out),
        depth,
    )


def project_second(half, attn, place, res, w_out):
    return project_call(
        project_second_kernel,
        "project_second",
        [kept((NXY, ROWS, LANES), F32)],
        (half, attn, place, res, w_out),
        w_out.shape[0],
    )[0]


def rows_kernel(rows_dev, part_ref, gain_ref, router_ref, ids_ref, packed_ref, hidden_ref):
    total = part_ref[0].astype(F32)
    for source in range(1, part_ref.shape[0]):
        total = total + part_ref[source].astype(F32)
    total = total.astype(BF16)
    to = lax.broadcasted_iota(jnp.int32, (ROWS, ROWS), 0)
    order = to % (ROWS // rows_dev) * rows_dev + to // (ROWS // rows_dev)
    order = (lax.broadcasted_iota(jnp.int32, (ROWS, ROWS), 1) == order).astype(BF16)
    hidden_ref[...] = jnp.dot(order, total, preferred_element_type=F32)
    hidden = total[:, :CHUNK].astype(F32)
    square = jnp.sum(hidden * hidden, axis=1, keepdims=True)
    scaled = (hidden * gain_ref[...]).astype(BF16)
    logits = jnp.dot(scaled, router_ref[...], preferred_element_type=F32)
    expert = lax.broadcasted_iota(jnp.int32, logits.shape, 1)
    lane = lax.broadcasted_iota(jnp.int32, (ROWS, LANES - CHUNK), 1)
    top = ids_ref.shape[1]
    spare = jnp.zeros((ROWS, LANES - CHUNK), F32)
    for k in range(top + 1):
        value = square
        if k < top:
            value = jnp.sum(jnp.where(expert == ids_ref[:, k : k + 1], logits, 0.0), axis=1, keepdims=True)
        high = value.astype(BF16).astype(F32)
        at_high, at_low = (k, top + k) if k < top else (2 * top, 2 * top + 1)
        spare = jnp.where(lane == at_high, high, jnp.where(lane == at_low, value - high, spare))
    packed_ref[:, :CHUNK] = scaled
    packed_ref[:, CHUNK:] = spare.astype(BF16)


def pack_rows(part, gain, router, ids, rows_dev):
    return pl.pallas_call(
        functools.partial(rows_kernel, rows_dev),
        out_shape=[kept((ROWS, LANES), BF16), kept((ROWS, LANES), F32)],
        compiler_params=pltpu.CompilerParams(vmem_limit_bytes=SMALL),
        name="pack_rows",
    )(part, gain, router, ids)


def slot_kernel(after_ref, ranks_ref, *refs):
    packed_refs, out_ref, rows_ref = refs[:NZ], refs[NZ], refs[NZ + 1]
    for k in range(NZ):
        rows_ref[k * ROWS : (k + 1) * ROWS, :] = packed_refs[k][...]
    slot = lax.broadcasted_iota(jnp.int32, (CAP, ALL_ROWS), 0)
    for e in range(EXP_G):
        table = (ranks_ref[e : e + 1, :] == slot).astype(BF16)
        slotted = jnp.dot(table, rows_ref[...], preferred_element_type=F32).astype(BF16)
        out_ref[2 * e] = slotted
        out_ref[2 * e + 1] = slotted


def slot_rows(after, ranks, packed):
    return pl.pallas_call(
        slot_kernel,
        in_specs=[ANYWHERE] + [WHOLE] * (1 + NZ),
        out_specs=WHOLE,
        out_shape=kept((NXY, CAP, LANES), BF16),
        scratch_shapes=[pltpu.VMEM((ALL_ROWS, LANES), BF16)],
        compiler_params=pltpu.CompilerParams(vmem_limit_bytes=SMALL),
        name="slot_rows",
    )(after, ranks, *packed)


def combine_kernel(plane_ref, out_ref, ranks_ref, hidden_ref, rows_ref, acc_ref):
    slot = lax.broadcasted_iota(jnp.int32, (ALL_ROWS, CAP), 1)
    acc = jnp.zeros((ALL_ROWS, LANES), F32)
    for e in range(EXP_G):
        table = (ranks_ref[:, e : e + 1] == slot).astype(BF16)
        acc = acc + jnp.dot(table, out_ref[2 * e], preferred_element_type=F32)
        acc = acc + jnp.dot(table, out_ref[2 * e + 1], preferred_element_type=F32)
    acc_ref[...] = acc
    span, count = rows_ref.shape[0], rows_ref.shape[1]
    own = ROWS // count
    for r in range(count):
        at = pl.multiple_of(r * span + plane_ref[0] * own, 8)
        acc_ref[pl.ds(at, own), :] += hidden_ref[r * own : (r + 1) * own, :]
    for r in range(count):
        rows_ref[:, r, :] = acc_ref[r * span : (r + 1) * span, :].astype(BF16)


def combine_rows(plane, out, ranks, hidden, count):
    vmem = pl.BlockSpec(memory_space=pltpu.VMEM)
    return pl.pallas_call(
        combine_kernel,
        in_specs=[pl.BlockSpec(memory_space=pltpu.SMEM), vmem, vmem, vmem],
        out_specs=vmem,
        out_shape=kept((ALL_ROWS // count, count, LANES), BF16),
        scratch_shapes=[pltpu.VMEM((ALL_ROWS, LANES), F32)],
        compiler_params=pltpu.CompilerParams(vmem_limit_bytes=SMALL),
        name="combine_rows",
    )(plane, out, ranks, hidden)


def fetch_kernel(after_ref, *refs):
    count = len(refs) // 2
    sems = refs[2 * count]
    copies = [pltpu.make_async_copy(refs[i], refs[count + i], sems.at[i]) for i in range(count)]
    for copy in start_all(copies):
        copy.wait()


def fetch(after, arrays):
    return pl.pallas_call(
        fetch_kernel,
        in_specs=[ANYWHERE] * (1 + len(arrays)),
        out_specs=[ANYWHERE] * len(arrays),
        scratch_shapes=[pltpu.SemaphoreType.DMA((len(arrays),))],
        out_shape=[kept(a.shape, a.dtype) for a in arrays],
        compiler_params=pltpu.CompilerParams(vmem_limit_bytes=SMALL),
        cost_estimate=pl.CostEstimate(
            flops=0, bytes_accessed=4 * sum(a.size for a in arrays), transcendentals=0
        ),
        name="fetch",
    )(after, *[in_hbm(a) for a in arrays])


def gate_up_half(half, y_ref, wg_ref, wu_ref, gate_ref, up_ref, stats_ref):
    gate, up, stats = gate_ref[...], up_ref[...], stats_ref[...]
    for p in range(NXY):
        rows = y_ref[p, :, :CHUNK]
        at = pl.ds(pl.multiple_of((half * NXY + p) * CHUNK, 16), CHUNK)
        gate = gate + jnp.dot(rows, wg_ref[0, at, :], preferred_element_type=F32)
        up = up + jnp.dot(rows, wu_ref[0, at, :], preferred_element_type=F32)
        stats = stats + y_ref[p, :, CHUNK:].astype(F32)
    gate_ref[...] = gate
    up_ref[...] = up
    stats_ref[...] = stats


def first_kernel(half_ref, y_ref, wg_ref, wu_ref, gate_ref, up_ref, stats_ref):
    gate_ref[...] = jnp.zeros_like(gate_ref)
    up_ref[...] = jnp.zeros_like(up_ref)
    stats_ref[...] = jnp.zeros_like(stats_ref)
    gate_up_half(half_ref[0], y_ref, wg_ref, wu_ref, gate_ref, up_ref, stats_ref)


def first_half(half, y, w_gate, w_up):
    hidden = w_gate.shape[2]
    return pl.pallas_call(
        first_kernel,
        in_specs=[SCALAR, WHOLE, WHOLE, WHOLE],
        out_specs=[WHOLE] * 3,
        out_shape=[
            kept((CAP, hidden), F32),
            kept((CAP, hidden), F32),
            kept((CAP, LANES - CHUNK), F32),
        ],
        compiler_params=pltpu.CompilerParams(vmem_limit_bytes=SMALL),
        cost_estimate=pl.CostEstimate(
            flops=2 * CAP * D * hidden, bytes_accessed=2 * D * hidden + CAP * D, transcendentals=0
        ),
        name="gate_up_first",
    )(half, y, w_gate, w_up)


def down_step(half, act, gates, wd_ref, out_ref):
    for i in range(STEPS):
        at = pl.ds(pl.multiple_of((half * STEPS + i) * BLK, 128), BLK)
        acc = jnp.dot(act, wd_ref[0, :, at], preferred_element_type=F32) * gates
        for g in range(GROUP):
            out_ref[i * GROUP + g, :, :CHUNK] = acc[:, g * CHUNK : (g + 1) * CHUNK].astype(out_ref.dtype)
            out_ref[i * GROUP + g, :, CHUNK:] = jnp.zeros((CAP, LANES - CHUNK), out_ref.dtype)


def second_kernel(
    half_ref, y_ref, wg_ref, wu_ref, wd_ref, gate0_ref, up0_ref, stats0_ref, mine_ref,
    act_ref, gates_ref, out_ref, gate_acc, up_acc, stats_acc,
):
    gate_acc[...] = gate0_ref[...]
    up_acc[...] = up0_ref[...]
    stats_acc[...] = stats0_ref[...]
    gate_up_half(half_ref[0], y_ref, wg_ref, wu_ref, gate_acc, up_acc, stats_acc)
    stats = stats_acc[...]
    square = stats[:, 16:17] + stats[:, 17:18]
    scale = lax.rsqrt(square * (1.0 / D) + 1e-6)
    affinity = jax.nn.sigmoid((stats[:, 0:8] + stats[:, 8:16]) * scale)
    own = jnp.sum(affinity * mine_ref[...], axis=1, keepdims=True)
    gates = 2.5 * own / jnp.sum(affinity, axis=1, keepdims=True)
    gates_ref[...] = jnp.broadcast_to(gates.astype(BF16).astype(F32), gates_ref.shape)
    gate = gate_acc[...] * scale
    up = up_acc[...] * scale
    act_ref[...] = (gate * jax.nn.sigmoid(gate) * up).astype(BF16)
    down_step(half_ref[0], act_ref[...], gates_ref[:, :1], wd_ref, out_ref)


def second_half(half, y, w_gate, w_up, w_down, gate, up, stats, mine):
    hidden = w_gate.shape[2]
    return pl.pallas_call(
        second_kernel,
        in_specs=[SCALAR] + [WHOLE] * 8,
        out_specs=[WHOLE] * 3,
        out_shape=[kept((CAP, hidden), BF16), kept((CAP, 128), F32), kept((NXY, CAP, LANES), BF16)],
        scratch_shapes=[
            pltpu.VMEM((CAP, hidden), F32),
            pltpu.VMEM((CAP, hidden), F32),
            pltpu.VMEM((CAP, LANES - CHUNK), F32),
        ],
        compiler_params=pltpu.CompilerParams(vmem_limit_bytes=SMALL),
        cost_estimate=pl.CostEstimate(
            flops=3 * CAP * D * hidden, bytes_accessed=3 * D * hidden + 2 * CAP * D, transcendentals=0
        ),
        name="gate_up_second",
    )(half, y, w_gate, w_up, w_down, gate, up, stats, mine)


def down_kernel(half_ref, act_ref, gates_ref, wd_ref, out_ref):
    down_step(half_ref[0], act_ref[...], gates_ref[:, :1], wd_ref, out_ref)


def down_own(half, act, gates, w_down):
    hidden = act.shape[1]
    return pl.pallas_call(
        down_kernel,
        in_specs=[SCALAR] + [WHOLE] * 3,
        out_specs=WHOLE,
        out_shape=kept((NXY, CAP, LANES), F32),
        compiler_params=pltpu.CompilerParams(vmem_limit_bytes=SMALL),
        cost_estimate=pl.CostEstimate(
            flops=CAP * D * hidden, bytes_accessed=D * hidden + 2 * CAP * D, transcendentals=0
        ),
        name="down_own",
    )(half, act, gates, w_down)


def swap_cores(values):
    return lax.ppermute(values, "c", [(0, 1), (1, 0)])


def per_device(
    prompt_cache,
    assignment,
    resident_cache,
    resident_len,
    queries,
    new_latent,
    residual,
    w_uv,
    w_out,
    norm_gain,
    w_router,
    expert_ids,
    w_gate,
    w_up,
    w_down,
):
    plane = lax.axis_index("z")
    core = lax.axis_index("c")
    place_xy = lax.axis_index("x") * NY + lax.axis_index("y")
    dev_index = place_xy * NC + core
    rows_dev = queries.shape[0]
    own_half = jnp.reshape(core, (1,)).astype(jnp.int32)
    other_half = 1 - own_half
    plane_index = jnp.reshape(plane, (1,)).astype(jnp.int32)
    chunk = core * NXY + place_xy

    received = lax.all_to_all(spread(assignment, prompt_cache), ("x", "y", "c"), 0, 0, tiled=True)

    ids_plane = expert_ids - plane * EXP_G
    named = jnp.any(expert_ids[:, :, None] == jnp.arange(NZ * EXP_G, dtype=jnp.int32)[None, None, :], axis=1)
    lower = (jnp.arange(ALL_ROWS)[:, None] > jnp.arange(ALL_ROWS)[None, :]).astype(BF16)
    ranks = jnp.dot(lower, named.astype(BF16), preferred_element_type=F32).astype(jnp.int32)
    ranks = jnp.where(named, ranks, -1)
    plane_ranks = lax.dynamic_slice_in_dim(ranks, plane * EXP_G, EXP_G, 1)
    own_expert = place_xy // 2
    slot_iota = jnp.arange(CAP, dtype=jnp.int32)
    own_ranks = lax.dynamic_index_in_dim(plane_ranks, own_expert, 1, keepdims=False)
    own_slots = (own_ranks[None, :] == slot_iota[:, None]).astype(BF16)
    slot_ids = jnp.dot(own_slots, ids_plane.astype(BF16), preferred_element_type=F32)
    mine = (slot_ids == own_expert.astype(F32)).astype(F32)
    group_ids = lax.dynamic_slice_in_dim(expert_ids, plane * ROWS, ROWS, 0)
    by_group = plane_ranks.reshape(NZ, ROWS, EXP_G)
    step_order = (plane - jnp.arange(NZ, dtype=jnp.int32)) % NZ
    step_ranks = by_group.at[step_order].get(mode="promise_in_bounds").reshape(ALL_ROWS, EXP_G).T
    owner_ranks = plane_ranks.reshape(NZ * NDEV, rows_dev, EXP_G).transpose(1, 0, 2).reshape(ALL_ROWS, EXP_G)
    gain_chunk = lax.dynamic_slice_in_dim(norm_gain, chunk * CHUNK, CHUNK, 0).astype(F32)[None, :]
    router_chunk = lax.dynamic_slice_in_dim(w_router, chunk * CHUNK, CHUNK, 0)
    row_iota = jnp.arange(ROWS, dtype=jnp.int32)
    place = (row_iota[:, None] == dev_index * rows_dev + jnp.arange(16, dtype=jnp.int32)[None, :]) & (
        jnp.arange(16) < rows_dev
    )[None, :]
    place = place.astype(BF16)
    res = jnp.pad(residual, ((0, 16 - rows_dev), (0, 0)))

    cache_iota = jnp.arange(resident_cache.shape[1], dtype=jnp.int32)
    old_masks = cache_iota[None, :] < resident_len[0][:, None]
    context_old = jax.vmap(attend)(queries[1:], resident_cache, old_masks, new_latent[1:])
    context_old = context_old.reshape(-1, LAT)
    held = (
        received, context_old, queries[0].T, step_ranks, owner_ranks, mine, group_ids, gain_chunk,
        router_chunk, place, res, own_half, other_half, plane_index,
    )
    (
        received, context_old, first_query, step_ranks, owner_ranks, mine, group_ids, gain_chunk,
        router_chunk, place, res, own_half, other_half, plane_index,
    ) = lax.optimization_barrier(held)
    context, w_uv, w_out = prompt_attention(first_query, received, new_latent, context_old, w_uv, w_out)

    context = lax.all_to_all(context.reshape(NDEV, -1, LAT), ("x", "y", "c"), 0, 0, tiled=True)
    context = context.reshape(-1, LAT)

    partial_other, attn = project_first(other_half, context, w_uv, place, res, w_out)
    partial_got = swap_cores(partial_other)
    partial_own = project_second(own_half, attn, place, res, w_out)
    partial = (partial_own + partial_got.astype(F32)).astype(BF16)
    partial = lax.all_to_all(partial, ("x", "y"), 0, 0, tiled=True)

    packed, hidden = pack_rows(partial, gain_chunk, router_chunk, group_ids, rows_dev)

    groups = [packed]
    for k in range(1, NZ):
        groups.append(lax.ppermute(packed, "z", [(i, (i + k) % NZ) for i in range(NZ)]))
    w_gate, w_up, w_down = fetch(packed, (w_gate, w_up, w_down))
    slotted = slot_rows(w_down, step_ranks, groups)
    slotted = lax.all_to_all(slotted, ("x", "y"), 0, 0, tiled=True)

    slotted_other = swap_cores(slotted)
    gate, up, stats = first_half(own_half, slotted, w_gate, w_up)
    act, gates, out_other = second_half(
        other_half, slotted_other, w_gate, w_up, w_down, gate, up, stats, mine
    )
    out_got = swap_cores(out_other)
    out_own = down_own(own_half, act, gates, w_down)
    out = (out_own + out_got.astype(F32)).astype(BF16)
    out = lax.all_to_all(out, ("x", "y"), 0, 0, tiled=True)

    total = combine_rows(plane_index, out, owner_ranks, hidden, rows_dev)
    total = lax.all_to_all(total, ("z", "x", "y", "c"), 0, 0, tiled=True)
    total = jnp.sum(total.reshape(NZ, NXY, NC, rows_dev, LANES)[..., :CHUNK].astype(F32), axis=0)
    return total.transpose(2, 1, 0, 3).reshape(rows_dev, D).astype(BF16)


def solution(mesh):
    grid = Mesh(mesh.devices.reshape(NZ, NX, NY, NC), ("z", "x", "y", "c"))
    dev = ("x", "y", "c")
    every = ("z", "x", "y", "c")
    return jax.shard_map(
        per_device,
        mesh=grid,
        in_specs=(
            P("z", dev, None),
            P("z", None),
            P(every, None, None),
            P(every, None),
            P(every, None, None),
            P(every, None),
            P(every, None),
            P(dev, None, None),
            P(dev, None),
            P(),
            P(),
            P(),
            P(every, None, None),
            P(every, None, None),
            P(every, None, None),
        ),
        out_specs=P(every, None),
        check_vma=False,
    )
```

time: 220 us -> 184 us (0.84)
  blocking collectives: 39.7 us -> 99.5 us
  waiting for transfers between devices: 81.4 us -> 28.7 us
  starting transfers between devices: 32.1 us -> 18.9 us
  matrix products: 17.9 us -> 5.46 us
  local copies, waits for them, and re-layouts: 15.1 us -> 5.36 us
  other arithmetic: 10.4 us -> 2.23 us
    all_to_all x0 -> x3, blocking collectives: none -> 59.2 us  [the longest x1 24.7 us: per_device(): out = lax.all_to_all(out, ('x', 'y'), 0, 0, tiled=True)]
    all_to_all x5 -> x1, waiting for transfers between devices: 81.4 us -> 23.1 us  [per_device(): lax.all_to_all(spread(assignment, prompt_cache), ('x', 'y', 'c'), 0, 0, t...]
    all_to_all x5 -> x1, starting transfers between devices: 27.1 us -> 8.73 us  [per_device(): lax.all_to_all(spread(assignment, prompt_cache), ('x', 'y', 'c'), 0, 0, t...]
    ppermute x3, waiting for transfers between devices: 0.01 us -> 5.53 us  [swap_cores(): return lax.ppermute(values, 'c', [(0, 1), (1, 0)])]
    ppermute x0 -> x3, starting transfers between devices: none -> 4.56 us  [per_device(): lax.ppermute(packed, 'z', [(i, (i + k) % NZ) for i in range(NZ)])]
    dot_general x3 -> x0, matrix products: 4.37 us -> none  [the longest x1 2.12 us: per_device(): jnp.dot(table, packed, preferred_element_type=F32).astype(BF16)]
    slice x1 -> x0, matrix products: 4.19 us -> none  [per_device(): lax.dot_general(table, out.reshape(NXY * CAP, LANES), (((0,), (0,)), ((),...]
    reshape x2 -> x1, local copies, waits for them, and re-layouts: 3.06 us -> 0.01 us  [per_device(): by_group = plane_ranks.reshape(NZ, ROWS, EXP_G)]
  transfers between devices with their start and end apart: 8 -> 7, of which waited for: 5 -> 5; matrix products, arithmetic and copies ran while one was open for 4% -> 5% of each run, Pallas kernels for 5% -> 4%
where the time goes in v2:
time: 184 us; the launch traced here: 183 us
  blocking collectives  99.5 us (54%)
  waiting for transfers between devices  28.7 us (16%)
  Pallas kernels  22.9 us (12%)
  starting transfers between devices  18.9 us (10%)
  matrix products  5.46 us (3%)
  local copies, waits for them, and re-layouts  5.36 us (3%)
  other arithmetic  2.23 us (1%)
    all_to_all x1, blocking collectives, per_device(): out = lax.all_to_all(out, ('x', 'y'), 0, 0, tiled=True)  24.7 us
    all_to_all x1, waiting for transfers between devices, per_device(): lax.all_to_all(spread(assignment, prompt_cache), ('x', 'y', 'c'), 0, 0, t...  23.1 us
    all_to_all x1, blocking collectives, per_device(): slotted = lax.all_to_all(slotted, ('x', 'y'), 0, 0, tiled=True)  22.3 us
    all_to_all x1, blocking collectives, per_device(): partial = lax.all_to_all(partial, ('x', 'y'), 0, 0, tiled=True)  18.8 us
    all_to_all x1, blocking collectives, per_device(): total = lax.all_to_all(total, ('z', 'x', 'y', 'c'), 0, 0, tiled=True)  18 us
    all_to_all x1, blocking collectives, per_device(): lax.all_to_all(context.reshape(NDEV, -1, LAT), ('x', 'y', 'c'), 0, 0, til...  15.7 us
    all_to_all x1, starting transfers between devices, per_device(): lax.all_to_all(spread(assignment, prompt_cache), ('x', 'y', 'c'), 0, 0, t...  8.73 us
    ppermute x3, starting transfers between devices, swap_cores(): return lax.ppermute(values, 'c', [(0, 1), (1, 0)])  5.63 us
  transfers between devices with their start and end apart: 7, of which 5 were waited for; matrix products, arithmetic and copies ran while one was open for 5% of the time, Pallas kernels for 4%

profile of v2, /device:TPU:1, one launch (start us, length us, event | category | flops | bytes accessed | tf_op | source)
XLA Modules:
  0.0 183.5 jit_solution(7349676777599326396)
XLA Ops:
  0.7 3.6 %spread.1 = bf16[32,64,576]{2,1,0:T(8,128)(2,1)} custom-call(s32[1,32]{1,0:T(1,128)S(1)} %copy-done.3, bf16[32,64,576]{2,1,0:T(8,128)(2,1)} %cache_ref.1), custom_call_target="tpu_custom_call" | custom-call | tf_op jit(solution)/shard_map/spread/pallas_call | solution.py:82
  4.4 8.7 %all-to-all-start = ((bf16[32,64,576]{2,1,0:T(8,128)(2,1)}), bf16[32,64,576]{2,1,0:T(8,128)(2,1)S(1)}, u32[]{:S(2)}, u32[]{:S(2)}) async-start(bf16[32,64,576]{2,1,0:T(8,128)(2,1)} %spread.1), calls=%async_computation | async-start | bytes 5242880 | tf_op jit(solution)/shard_map/all_to_all | solution.py:470
  15.0 1.2 fusion.19
  17.9 2.4 %fusion.26 = (f32[3,128]{1,0:T(4,128)S(1)}, f32[3,128,512]{2,1,0:T(8,128)S(1)}) fusion(bf16[4,128,576]{1,2,0:T(8,128)(2,1)} %param.19, bf16[3,512,576]{1,2,0:T(8,128)(2,1)} %param.17, pred[3,512]{1,0:T(4,128)(4,1)S(1)} %iota_compare_fusion.6), kind=kOutput, calls=%fused_computation.55 | convolution fusion | flops 227081856 | bytes 3148800 | tf_op jit(solution)/shard_map/vmap(hc,kc->hk)/dot_general | solution.py:53
  20.9 1.6 slice_bitcast_fusion.query_hbm
  22.4 1.5 fusion.6
  23.9 23.1 %all-to-all-done.cache_ref = bf16[32,64,576]{2,1,0:T(8,128)(2,1)S(1)} async-done(((bf16[32,64,576]{2,1,0:T(8,128)(2,1)}), bf16[32,64,576]{2,1,0:T(8,128)(2,1)S(1)}, u32[]{:S(2)}, u32[]{:S(2)}) %all-to-all-start) | async-done | bytes 2359328 | tf_op jit(solution)/shard_map/all_to_all | solution.py:470
  47.0 4.1 %prompt_attention.1 = (bf16[512,512]{1,0:T(8,128)(2,1)S(1)}, bf16[4,512,128]{2,1,0:T(8,128)(2,1)S(1)}, bf16[512,7168]{1,0:T(8,128)(2,1)S(1)}) custom-call(bf16[576,128]{1,0:T(8,128)(2,1)} %slice_bitcast_fusion.query_hbm, bf16[32,64,576]{2,1,0:T(8,128)(2,1)S(1)} %all-to-all-done.cache_ref, bf16[4,576]{1,0:T(4,128)(2,1)S(1)} %copy-done.2, ...), custom_call_target="tpu_custom_call" | custom-call | tf_op jit(solution)/shard_map/prompt_attention/pallas_call | solution.py:136
  51.1 15.7 %all_to_all.30 = bf16[32,16,512]{2,1,0:T(8,128)(2,1)S(1)} all-to-all(bf16[32,16,512]{2,1,0:T(8,128)(2,1)S(1)} %bitcast.52), channel_id=1, replica_groups=mesh['z'=4,'x'=4,'y'=4,'c'=2] {'x','y','c'}, dimensions={0} | all-to-all | bytes 1048576 | tf_op jit(solution)/shard_map/all_to_all | solution.py:512
  66.8 2.7 %project_first.1 = (bf16[16,128,256]{2,1,0:T(8,128)(2,1)S(1)}, bf16[128,512]{1,0:T(8,128)(2,1)S(1)}) custom-call(s32[1]{0:T(128)S(6)} %sub.45.half_ref, bf16[512,512]{1,0:T(8,128)(2,1)S(1)} %bitcast.50, bf16[4,512,128]{2,1,0:T(8,128)(2,1)S(1)} %get-tuple-element.42.uv_ref, bf16[128,16]{1,0:T(8,128)(2,1)S(1)} %fusion.17.place_ref, ...), custom_call_target="tpu_custom_call" | custom-call | flops 469762048 | bytes 5505024 | tf_op jit(solution)/shard_map/project_first/pallas_call | solution.py:183
  69.5 1.1 project_second.1
  70.6 1.5 collective-permute-done
  72.5 18.8 %all_to_all.31.part_ref = bf16[16,128,256]{2,1,0:T(8,128)(2,1)S(1)} all-to-all(bf16[16,128,256]{2,1,0:T(8,128)(2,1)S(1)} %add_convert_fusion.1), channel_id=1, replica_groups=mesh['z'=4,'x'=4,'y'=4,'c'=2] {'x','y'}, dimensions={0} | all-to-all | bytes 2097152 | tf_op jit(solution)/shard_map/all_to_all | solution.py:519
  92.2 3.9 %collective-permute-start.3 = (bf16[128,256]{1,0:T(8,128)(2,1)S(1)}, bf16[128,256]{1,0:T(8,128)(2,1)S(1)}, u32[]{:S(2)}, u32[]{:S(2)}) collective-permute-start(bf16[128,256]{1,0:T(8,128)(2,1)S(1)} %get-tuple-element.51.after_ref.refs_0_), channel_id=1, source_target_pairs={{0,96},{32,0},{64,32},{96,64},{1,97},{33,1},{65,33},{97,65},{2,98}... | collective-permute-start | bytes 196616 | tf_op jit(solution)/shard_map/ppermute | solution.py:525
  96.8 4.2 %fetch.1 = (bf16[1,7168,256]{2,1,0:T(8,128)(2,1)S(1)}, bf16[1,7168,256]{2,1,0:T(8,128)(2,1)S(1)}, bf16[1,256,7168]{2,1,0:T(8,128)(2,1)S(1)}) custom-call(bf16[128,256]{1,0:T(8,128)(2,1)S(1)} %get-tuple-element.51.after_ref.refs_0_, bf16[1,7168,256]{2,1,0:T(8,128)(2,1)} %refs_0_.1, bf16[1,7168,256]{2,1,0:T(8,128)(2,1)} %refs_1_.1, bf16[1,256,7168]{2,1,0:T(8,128)(2,1)} %refs_2_.1), custom_call_target="tpu_custom_call" | custom-call | bytes 22020096 | tf_op jit(solution)/shard_map/fetch/pallas_call | solution.py:317
  101.7 22.3 %all_to_all.32.y_ref = bf16[16,192,256]{2,1,0:T(8,128)(2,1)S(1)} all-to-all(bf16[16,192,256]{2,1,0:T(8,128)(2,1)S(1)} %slot_rows.1), channel_id=1, replica_groups=mesh['z'=4,'x'=4,'y'=4,'c'=2] {'x','y'}, dimensions={0} | all-to-all | bytes 3145728 | tf_op jit(solution)/shard_map/all_to_all | solution.py:528
  124.0 5.1 %collective-permute-start.4 = (bf16[16,192,256]{2,1,0:T(8,128)(2,1)S(1)}, bf16[16,192,256]{2,1,0:T(8,128)(2,1)S(1)}, u32[]{:S(2)}, u32[]{:S(2)}) collective-permute-start(bf16[16,192,256]{2,1,0:T(8,128)(2,1)S(1)} %all_to_all.32.y_ref), channel_id=1, source_target_pairs={{0,1},{1,0},{2,3},{3,2},{4,5},{5,4},{6,7},{7,6},{8,9},{9,8},{10,11... | collective-permute-start | bytes 4718600 | tf_op jit(solution)/shard_map/ppermute | solution.py:440
  130.0 2.1 %collective-permute-done.4.y_ref = bf16[16,192,256]{2,1,0:T(8,128)(2,1)S(1)} collective-permute-done((bf16[16,192,256]{2,1,0:T(8,128)(2,1)S(1)}, bf16[16,192,256]{2,1,0:T(8,128)(2,1)S(1)}, u32[]{:S(2)}, u32[]{:S(2)}) %collective-permute-start.4) | collective-permute-done | bytes 1572896 | tf_op jit(solution)/shard_map/ppermute | solution.py:440
  132.1 1.8 gate_up_second.1
  134.4 1.1 down_own.1
  135.5 1.9 %collective-permute-done.5 = bf16[16,192,256]{2,1,0:T(8,128)(2,1)S(1)} collective-permute-done((bf16[16,192,256]{2,1,0:T(8,128)(2,1)S(1)}, bf16[16,192,256]{2,1,0:T(8,128)(2,1)S(1)}, u32[]{:S(2)}, u32[]{:S(2)}) %collective-permute-start.5) | collective-permute-done | bytes 1572896 | tf_op jit(solution)/shard_map/ppermute | solution.py:440
  137.9 24.7 %all_to_all.33.out_ref = bf16[16,192,256]{2,1,0:T(8,128)(2,1)S(1)} all-to-all(bf16[16,192,256]{2,1,0:T(8,128)(2,1)S(1)} %add_convert_fusion), channel_id=1, replica_groups=mesh['z'=4,'x'=4,'y'=4,'c'=2] {'x','y'}, dimensions={0} | all-to-all | bytes 3145728 | tf_op jit(solution)/shard_map/all_to_all | solution.py:538
  162.6 1.9 %combine_rows.1 = bf16[128,4,256]{2,1,0:T(4,128)(2,1)S(1)} custom-call(s32[1]{0:T(128)} %bitcast.16.plane_ref, bf16[16,192,256]{2,1,0:T(8,128)(2,1)S(1)} %all_to_all.33.out_ref, s32[512,8]{1,0:T(8,128)S(1)} %bitcast.51, f32[128,256]{1,0:T(8,128)S(1)} %get-tuple-element.64.hidden_ref), custom_call_target="tpu_custom_call" | custom-call | tf_op jit(solution)/shard_map/combine_rows/pallas_call | solution.py:297
  164.5 18.0 %all_to_all.34 = bf16[128,4,256]{2,1,0:T(4,128)(2,1)S(1)} all-to-all(bf16[128,4,256]{2,1,0:T(4,128)(2,1)S(1)} %combine_rows.1), channel_id=1, replica_groups=mesh['z'=4,'x'=4,'y'=4,'c'=2] {'z','x','y','c'}, dimensions={0} | all-to-all | bytes 524288 | tf_op jit(solution)/shard_map/all_to_all | solution.py:541
  (59 shorter events, 10.3 us)
Async XLA Ops:
  0.0 14.9 %copy-start = (bf16[7168,32]{0,1:T(8,128)(2,1)S(1)}, bf16[7168,32]{0,1:T(8,128)(2,1)}, u32[]{:S(2)}) copy-start(bf16[7168,32]{0,1:T(8,128)(2,1)} %param.25) | copy-start | bytes 1376260
  0.0 0.7 copy-start.3
  4.3 8.8 %copy-start.5 = (s32[512,8]{0,1:T(8,128)S(1)}, s32[512,8]{0,1:T(8,128)}, u32[]{:S(2)}) copy-start(s32[512,8]{0,1:T(8,128)} %param.26) | copy-start | bytes 49156
  4.3 9.2 %copy-start.7 = (s32[1,3]{1,0:T(1,128)S(1)}, s32[1,3]{1,0:T(1,128)}, u32[]{:S(2)}) copy-start(s32[1,3]{1,0:T(1,128)} %param.18) | copy-start | bytes 40
  4.3 9.8 %copy-start.2 = (bf16[4,576]{1,0:T(4,128)(2,1)S(1)}, bf16[4,576]{1,0:T(4,128)(2,1)}, u32[]{:S(2)}) copy-start(bf16[4,576]{1,0:T(4,128)(2,1)} %entry_ref.1) | copy-start | bytes 13828
  4.4 42.6 %all-to-all-start = ((bf16[32,64,576]{2,1,0:T(8,128)(2,1)}), bf16[32,64,576]{2,1,0:T(8,128)(2,1)S(1)}, u32[]{:S(2)}, u32[]{:S(2)}) async-start(bf16[32,64,576]{2,1,0:T(8,128)(2,1)} %spread.1), calls=%async_computation | async-start | bytes 5242880 | tf_op jit(solution)/shard_map/all_to_all | solution.py:470
  13.1 4.1 %copy-start.4 = (bf16[4,7168]{1,0:T(4,128)(2,1)S(1)}, bf16[4,7168]{1,0:T(4,128)(2,1)}, u32[]{:S(2)}) copy-start(bf16[4,7168]{1,0:T(4,128)(2,1)} %param.21) | copy-start | bytes 172036
  13.5 0.6 copy-start.6
  17.9 4.5 %copy-start.8 = (bf16[3,512,576]{1,2,0:T(8,128)(2,1)S(1)}, bf16[3,512,576]{1,2,0:T(8,128)(2,1)}, u32[]{:S(2)}) copy-start(bf16[3,512,576]{1,2,0:T(8,128)(2,1)} %param.17) | copy-start | bytes 5308420
  69.4 2.7 %collective-permute-start = (bf16[16,128,256]{2,1,0:T(8,128)(2,1)S(1)}, bf16[16,128,256]{2,1,0:T(8,128)(2,1)S(1)}, u32[]{:S(2)}, u32[]{:S(2)}) collective-permute-start(bf16[16,128,256]{2,1,0:T(8,128)(2,1)S(1)} %get-tuple-element.47), channel_id=1, source_target_pairs={{0,1},{1,0},{2,3},{3,2},{4,5},{5,4},{6,7},{7,6},{8,9},{9,8},{10,11... | collective-permute-start | bytes 3145736 | tf_op jit(solution)/shard_map/ppermute | solution.py:440
  92.2 8.8 %collective-permute-start.3 = (bf16[128,256]{1,0:T(8,128)(2,1)S(1)}, bf16[128,256]{1,0:T(8,128)(2,1)S(1)}, u32[]{:S(2)}, u32[]{:S(2)}) collective-permute-start(bf16[128,256]{1,0:T(8,128)(2,1)S(1)} %get-tuple-element.51.after_ref.refs_0_), channel_id=1, source_target_pairs={{0,96},{32,0},{64,32},{96,64},{1,97},{33,1},{65,33},{97,65},{2,98}... | collective-permute-start | bytes 196616 | tf_op jit(solution)/shard_map/ppermute | solution.py:525
  96.1 5.0 %collective-permute-start.2 = (bf16[128,256]{1,0:T(8,128)(2,1)S(1)}, bf16[128,256]{1,0:T(8,128)(2,1)S(1)}, u32[]{:S(2)}, u32[]{:S(2)}) collective-permute-start(bf16[128,256]{1,0:T(8,128)(2,1)S(1)} %get-tuple-element.51.after_ref.refs_0_), channel_id=1, source_target_pairs={{0,64},{32,96},{64,0},{96,32},{1,65},{33,97},{65,1},{97,33},{2,66}... | collective-permute-start | bytes 196616 | tf_op jit(solution)/shard_map/ppermute | solution.py:525
  96.1 5.0 %collective-permute-start.1 = (bf16[128,256]{1,0:T(8,128)(2,1)S(1)}, bf16[128,256]{1,0:T(8,128)(2,1)S(1)}, u32[]{:S(2)}, u32[]{:S(2)}) collective-permute-start(bf16[128,256]{1,0:T(8,128)(2,1)S(1)} %get-tuple-element.51.after_ref.refs_0_), channel_id=1, source_target_pairs={{0,32},{32,64},{64,96},{96,0},{1,33},{33,65},{65,97},{97,1},{2,34}... | collective-permute-start | bytes 196616 | tf_op jit(solution)/shard_map/ppermute | solution.py:525
  124.0 8.1 %collective-permute-start.4 = (bf16[16,192,256]{2,1,0:T(8,128)(2,1)S(1)}, bf16[16,192,256]{2,1,0:T(8,128)(2,1)S(1)}, u32[]{:S(2)}, u32[]{:S(2)}) collective-permute-start(bf16[16,192,256]{2,1,0:T(8,128)(2,1)S(1)} %all_to_all.32.y_ref), channel_id=1, source_target_pairs={{0,1},{1,0},{2,3},{3,2},{4,5},{5,4},{6,7},{7,6},{8,9},{9,8},{10,11... | collective-permute-start | bytes 4718600 | tf_op jit(solution)/shard_map/ppermute | solution.py:440
  133.9 3.5 %collective-permute-start.5 = (bf16[16,192,256]{2,1,0:T(8,128)(2,1)S(1)}, bf16[16,192,256]{2,1,0:T(8,128)(2,1)S(1)}, u32[]{:S(2)}, u32[]{:S(2)}) collective-permute-start(bf16[16,192,256]{2,1,0:T(8,128)(2,1)S(1)} %get-tuple-element.62), channel_id=1, source_target_pairs={{0,1},{1,0},{2,3},{3,2},{4,5},{5,4},{6,7},{7,6},{8,9},{9,8},{10,11... | collective-permute-start | bytes 4718600 | tf_op jit(solution)/shard_map/ppermute | solution.py:440
  137.9 45.6 %copy-start.1 = (bf16[7168,32]{0,1:T(8,128)(2,1)S(1)}, bf16[7168,32]{0,1:T(8,128)(2,1)}, u32[]{:S(2)}) copy-start(bf16[7168,32]{0,1:T(8,128)(2,1)} %param.25) | copy-start | bytes 1376260

commit v3 on v2

--- a/solution.py
+++ b/solution.py
@@ -17,6 +17,7 @@
 NDEV = NXY * NC
 EXP_G = 8
 CHUNK = D // NDEV
+HALF = D // 2
 LANES = 256
 GROUP = 4
 BLK = CHUNK * GROUP
@@ -95,14 +96,21 @@
 
 
 def prompt_kernel(
-    query_hbm, cache_ref, entry_ref, old_hbm, uv_hbm, w_hbm, out_ref, uv_ref, w_ref, all_ref, query_ref, sems
+    half_ref, query_hbm, cache_ref, entry_ref, old_hbm, uv_hbm, w_hbm, res_hbm, got_hbm,
+    out_ref, uv_ref, w_ref, all_ref, query_ref, sems,
 ):
     heads_all = query_hbm.shape[1]
     query_copy = pltpu.make_async_copy(query_hbm, query_ref, sems.at[0])
     old_copy = pltpu.make_async_copy(old_hbm, all_ref.at[pl.ds(heads_all, old_hbm.shape[0]), :], sems.at[1])
     uv_copy = pltpu.make_async_copy(uv_hbm, uv_ref, sems.at[2])
-    w_copy = pltpu.make_async_copy(w_hbm, w_ref, sems.at[3])
-    start_all((query_copy, old_copy, uv_copy, w_copy))
+    depth = w_hbm.shape[0]
+    at = pl.ds(pl.multiple_of(half_ref[0] * HALF, 128), HALF)
+    w_copies = (
+        pltpu.make_async_copy(w_hbm.at[:, at], w_ref.at[pl.ds(0, depth), :], sems.at[3]),
+        pltpu.make_async_copy(res_hbm.at[:, at], w_ref.at[pl.ds(depth, 16), :], sems.at[4]),
+        pltpu.make_async_copy(got_hbm, w_ref.at[pl.ds(depth + 16, depth + 16), :], sems.at[5]),
+    )
+    start_all((query_copy, old_copy, uv_copy) + w_copies)
     scale_factor = (NOPE + ROPE) ** (-0.5)
     cache = cache_ref[...].reshape(-1, cache_ref.shape[-1])
     entry = entry_ref[:1, :]
@@ -128,40 +136,30 @@
     old_copy.wait()
     out_ref[...] = jnp.dot(order, all_ref[...], preferred_element_type=F32).astype(BF16)
     uv_copy.wait()
-    w_copy.wait()
-
-
-def prompt_attention(query, cache, entry, old, w_uv, w_out):
+    for copy in w_copies:
+        copy.wait()
+
+
+def prompt_attention(half, query, cache, entry, old, w_uv, w_out, res, got):
     rows = query.shape[1] + old.shape[0]
     return pl.pallas_call(
         prompt_kernel,
-        in_specs=[ANYWHERE, WHOLE, WHOLE, ANYWHERE, ANYWHERE, ANYWHERE],
+        in_specs=[SCALAR, ANYWHERE, WHOLE, WHOLE] + [ANYWHERE] * 5,
         out_specs=[WHOLE, ANYWHERE, ANYWHERE],
         out_shape=[
-            kept((rows, LAT), BF16), kept(w_uv.shape, BF16), kept(w_out.shape, BF16),
+            kept((rows, LAT), BF16), kept(w_uv.shape, BF16), kept((2 * got.shape[0], HALF), BF16),
         ],
         scratch_shapes=[
             pltpu.VMEM((rows, LAT), BF16),
             pltpu.VMEM(query.shape, BF16),
-            pltpu.SemaphoreType.DMA((4,)),
+            pltpu.SemaphoreType.DMA((6,)),
         ],
         compiler_params=pltpu.CompilerParams(vmem_limit_bytes=LARGE),
         name="prompt_attention",
-    )(in_hbm(query), cache, entry, in_hbm(old), in_hbm(w_uv), in_hbm(w_out))
-
-
-def project_half(half, attn, place_ref, res_ref, w_ref, out_ref):
-    for i in range(STEPS):
-        at = pl.ds(pl.multiple_of((half * STEPS + i) * BLK, 128), BLK)
-        acc = jnp.dot(attn, w_ref[:, at], preferred_element_type=F32)
-        acc = acc + jnp.dot(place_ref[...], res_ref[:, at], preferred_element_type=F32)
-        for g in range(GROUP):
-            part = acc[:, g * CHUNK : (g + 1) * CHUNK]
-            out_ref[i * GROUP + g, :, :CHUNK] = part.astype(out_ref.dtype)
-            out_ref[i * GROUP + g, :, CHUNK:] = jnp.zeros((ROWS, LANES - CHUNK), out_ref.dtype)
-
-
-def project_first_kernel(half_ref, context_ref, uv_ref, place_ref, res_ref, w_ref, out_ref, attn_ref):
+    )(half, in_hbm(query), cache, entry, *[in_hbm(a) for a in (old, w_uv, w_out, res, got)])
+
+
+def values_kernel(context_ref, uv_ref, attn_ref):
     heads, rows = uv_ref.shape[0], context_ref.shape[0]
     context = context_ref[...]
     pick = lax.broadcasted_iota(jnp.int32, (ROWS, rows), 1) // heads
@@ -172,46 +170,43 @@
         values = jnp.where(head == h, values, 0.0).astype(BF16)
         values = jnp.dot(pick, values, preferred_element_type=F32).astype(BF16)
         attn_ref[:, h * values.shape[1] : (h + 1) * values.shape[1]] = values
-    project_half(half_ref[0], attn_ref[...], place_ref, res_ref, w_ref, out_ref)
-
-
-def project_second_kernel(half_ref, attn_ref, place_ref, res_ref, w_ref, out_ref):
-    project_half(half_ref[0], attn_ref[...], place_ref, res_ref, w_ref, out_ref)
-
-
-def project_call(kernel, name, out_shape, args, depth):
-    return pl.pallas_call(
-        kernel,
-        in_specs=[SCALAR] + [WHOLE] * (len(args) - 1),
-        out_specs=[WHOLE] * len(out_shape),
-        out_shape=out_shape,
-        compiler_params=pltpu.CompilerParams(vmem_limit_bytes=SMALL),
-        cost_estimate=pl.CostEstimate(
-            flops=2 * ROWS * depth * D // 2, bytes_accessed=depth * D + 2 * ROWS * D, transcendentals=0
-        ),
-        name=name,
-    )(*args)
-
-
-def project_first(half, context, w_uv, place, res, w_out):
-    depth = w_out.shape[0]
-    return project_call(
-        project_first_kernel,
-        "project_first",
-        [kept((NXY, ROWS, LANES), BF16), kept((ROWS, depth), BF16)],
-        (half, context, w_uv, place, res, w_out),
-        depth,
-    )
-
-
-def project_second(half, attn, place, res, w_out):
-    return project_call(
-        project_second_kernel,
-        "project_second",
-        [kept((NXY, ROWS, LANES), F32)],
-        (half, attn, place, res, w_out),
-        w_out.shape[0],
-    )[0]
+
+
+def head_values(context, w_uv):
+    return pl.pallas_call(
+        values_kernel,
+        in_specs=[WHOLE, WHOLE],
+        out_specs=WHOLE,
+        out_shape=kept((ROWS, w_uv.shape[0] * w_uv.shape[2]), BF16),
+        compiler_params=pltpu.CompilerParams(vmem_limit_bytes=SMALL),
+        name="head_values",
+    )(context, w_uv)
+
+
+def project_kernel(own_ref, got_ref, place_ref, w_ref, out_ref):
+    depth = own_ref.shape[1]
+    lhs = (own_ref[...], place_ref[0], got_ref[...], place_ref[1])
+    for i in range(STEPS):
+        at, acc = 0, jnp.zeros((ROWS, BLK), F32)
+        for left in lhs:
+            acc = acc + jnp.dot(
+                left, w_ref[at : at + left.shape[1], i * BLK : (i + 1) * BLK], preferred_element_type=F32
+            )
+            at += left.shape[1]
+        for g in range(GROUP):
+            out_ref[i * GROUP + g, :, :CHUNK] = acc[:, g * CHUNK : (g + 1) * CHUNK].astype(BF16)
+            out_ref[i * GROUP + g, :, CHUNK:] = jnp.zeros((ROWS, LANES - CHUNK), BF16)
+
+
+def project(own, got, place, w_out):
+    return pl.pallas_call(
+        project_kernel,
+        in_specs=[WHOLE] * 4,
+        out_specs=WHOLE,
+        out_shape=kept((NXY, ROWS, LANES), BF16),
+        compiler_params=pltpu.CompilerParams(vmem_limit_bytes=SMALL),
+        name="project",
+    )(own, got, place, w_out)
 
 
 def rows_kernel(rows_dev, part_ref, gain_ref, router_ref, ids_ref, packed_ref, hidden_ref):
@@ -305,135 +300,153 @@
     )(plane, out, ranks, hidden)
 
 
-def fetch_kernel(after_ref, *refs):
-    count = len(refs) // 2
-    sems = refs[2 * count]
-    copies = [pltpu.make_async_copy(refs[i], refs[count + i], sems.at[i]) for i in range(count)]
+def give_kernel(
+    half_ref, out_hbm, res_hbm, gate_hbm, up_hbm, down_hbm, to_out, to_in, to_down,
+    out_ref, in_ref, down_ref, in_sems, out_sems,
+):
+    depth = out_hbm.shape[0]
+    columns = pl.ds(pl.multiple_of(half_ref[0] * HALF, 128), HALF)
+    rows = pl.ds(pl.multiple_of(half_ref[0] * HALF, 16), HALF)
+    sources = (
+        (out_hbm.at[:, columns], out_ref.at[pl.ds(0, depth), :], to_out.at[pl.ds(0, depth), :]),
+        (res_hbm.at[:, columns], out_ref.at[pl.ds(depth, 16), :], to_out.at[pl.ds(depth, 16), :]),
+        (gate_hbm.at[0, rows, :], in_ref.at[0], to_in.at[0]),
+        (up_hbm.at[0, rows, :], in_ref.at[1], to_in.at[1]),
+        (down_hbm.at[0, :, columns], down_ref, to_down),
+    )
+    arrive = [pltpu.make_async_copy(a, b, in_sems.at[n]) for n, (a, b, _) in enumerate(sources)]
+    leave = [pltpu.make_async_copy(b, c, out_sems.at[n]) for n, (_, b, c) in enumerate(sources)]
+    start_all(arrive)
+    for first, second in zip(arrive, leave):
+        first.wait()
+        second.start()
+    for copy in leave:
+        copy.wait()
+
+
+def give_weights(half, w_out, res, w_gate, w_up, w_down):
+    hidden = w_gate.shape[2]
+    arrays = (w_out, res, w_gate, w_up, w_down)
+    return pl.pallas_call(
+        give_kernel,
+        in_specs=[SCALAR] + [ANYWHERE] * 5,
+        out_specs=[ANYWHERE] * 3,
+        out_shape=[
+            pltpu.HBM((w_out.shape[0] + 16, HALF), BF16),
+            pltpu.HBM((2, HALF, hidden), BF16),
+            pltpu.HBM((hidden, HALF), BF16),
+        ],
+        scratch_shapes=[
+            pltpu.VMEM((w_out.shape[0] + 16, HALF), BF16),
+            pltpu.VMEM((2, HALF, hidden), BF16),
+            pltpu.VMEM((hidden, HALF), BF16),
+            pltpu.SemaphoreType.DMA((5,)),
+            pltpu.SemaphoreType.DMA((5,)),
+        ],
+        compiler_params=pltpu.CompilerParams(vmem_limit_bytes=SMALL),
+        name="give_weights",
+    )(half, *[in_hbm(a) for a in arrays])
+
+
+def fetch_kernel(
+    after_ref, half_ref, gate_hbm, up_hbm, down_hbm, got_in_hbm, got_down_hbm, in_ref, down_ref, sems
+):
+    hidden = gate_hbm.shape[2]
+    columns = pl.ds(pl.multiple_of(half_ref[0] * HALF, 128), HALF)
+    rows = pl.ds(pl.multiple_of(half_ref[0] * HALF, 16), HALF)
+    sources = (gate_hbm.at[0, rows, :], up_hbm.at[0, rows, :], got_in_hbm.at[0], got_in_hbm.at[1])
+    copies = [
+        pltpu.make_async_copy(source, in_ref.at[:, pl.ds(j * hidden, hidden)], sems.at[j])
+        for j, source in enumerate(sources)
+    ]
+    copies.append(
+        pltpu.make_async_copy(down_hbm.at[0, :, columns], down_ref.at[pl.ds(0, hidden), :], sems.at[4])
+    )
+    copies.append(pltpu.make_async_copy(got_down_hbm, down_ref.at[pl.ds(hidden, hidden), :], sems.at[5]))
     for copy in start_all(copies):
         copy.wait()
 
 
-def fetch(after, arrays):
+def fetch_experts(after, half, w_gate, w_up, w_down, got_in, got_down):
+    hidden = w_gate.shape[2]
     return pl.pallas_call(
         fetch_kernel,
-        in_specs=[ANYWHERE] * (1 + len(arrays)),
-        out_specs=[ANYWHERE] * len(arrays),
-        scratch_shapes=[pltpu.SemaphoreType.DMA((len(arrays),))],
-        out_shape=[kept(a.shape, a.dtype) for a in arrays],
-        compiler_params=pltpu.CompilerParams(vmem_limit_bytes=SMALL),
-        cost_estimate=pl.CostEstimate(
-            flops=0, bytes_accessed=4 * sum(a.size for a in arrays), transcendentals=0
-        ),
-        name="fetch",
-    )(after, *[in_hbm(a) for a in arrays])
-
-
-def gate_up_half(half, y_ref, wg_ref, wu_ref, gate_ref, up_ref, stats_ref):
-    gate, up, stats = gate_ref[...], up_ref[...], stats_ref[...]
+        in_specs=[ANYWHERE, SCALAR] + [ANYWHERE] * 5,
+        out_specs=[ANYWHERE] * 2,
+        out_shape=[kept((HALF, 4 * hidden), BF16), kept((2 * hidden, HALF), BF16)],
+        scratch_shapes=[pltpu.SemaphoreType.DMA((6,))],
+        compiler_params=pltpu.CompilerParams(vmem_limit_bytes=SMALL),
+        cost_estimate=pl.CostEstimate(flops=0, bytes_accessed=12 * D * hidden, transcendentals=0),
+        name="fetch_experts",
+    )(after, half, *[in_hbm(a) for a in (w_gate, w_up, w_down, got_in, got_down)])
+
+
+def gate_up_kernel(y_ref, w_ref, own_ref, send_ref):
+    width = w_ref.shape[1]
+    acc = jnp.zeros((CAP, width), F32)
+    stats = jnp.zeros((CAP, LANES - CHUNK), F32)
     for p in range(NXY):
-        rows = y_ref[p, :, :CHUNK]
-        at = pl.ds(pl.multiple_of((half * NXY + p) * CHUNK, 16), CHUNK)
-        gate = gate + jnp.dot(rows, wg_ref[0, at, :], preferred_element_type=F32)
-        up = up + jnp.dot(rows, wu_ref[0, at, :], preferred_element_type=F32)
+        acc = acc + jnp.dot(
+            y_ref[p, :, :CHUNK], w_ref[p * CHUNK : (p + 1) * CHUNK, :], preferred_element_type=F32
+        )
         stats = stats + y_ref[p, :, CHUNK:].astype(F32)
-    gate_ref[...] = gate
-    up_ref[...] = up
-    stats_ref[...] = stats
-
-
-def first_kernel(half_ref, y_ref, wg_ref, wu_ref, gate_ref, up_ref, stats_ref):
-    gate_ref[...] = jnp.zeros_like(gate_ref)
-    up_ref[...] = jnp.zeros_like(up_ref)
-    stats_ref[...] = jnp.zeros_like(stats_ref)
-    gate_up_half(half_ref[0], y_ref, wg_ref, wu_ref, gate_ref, up_ref, stats_ref)
-
-
-def first_half(half, y, w_gate, w_up):
-    hidden = w_gate.shape[2]
-    return pl.pallas_call(
-        first_kernel,
-        in_specs=[SCALAR, WHOLE, WHOLE, WHOLE],
-        out_specs=[WHOLE] * 3,
-        out_shape=[
-            kept((CAP, hidden), F32),
-            kept((CAP, hidden), F32),
-            kept((CAP, LANES - CHUNK), F32),
-        ],
-        compiler_params=pltpu.CompilerParams(vmem_limit_bytes=SMALL),
-        cost_estimate=pl.CostEstimate(
-            flops=2 * CAP * D * hidden, bytes_accessed=2 * D * hidden + CAP * D, transcendentals=0
-        ),
-        name="gate_up_first",
-    )(half, y, w_gate, w_up)
-
-
-def down_step(half, act, gates, wd_ref, out_ref):
-    for i in range(STEPS):
-        at = pl.ds(pl.multiple_of((half * STEPS + i) * BLK, 128), BLK)
-        acc = jnp.dot(act, wd_ref[0, :, at], preferred_element_type=F32) * gates
-        for g in range(GROUP):
-            out_ref[i * GROUP + g, :, :CHUNK] = acc[:, g * CHUNK : (g + 1) * CHUNK].astype(out_ref.dtype)
-            out_ref[i * GROUP + g, :, CHUNK:] = jnp.zeros((CAP, LANES - CHUNK), out_ref.dtype)
-
-
-def second_kernel(
-    half_ref, y_ref, wg_ref, wu_ref, wd_ref, gate0_ref, up0_ref, stats0_ref, mine_ref,
-    act_ref, gates_ref, out_ref, gate_acc, up_acc, stats_acc,
-):
-    gate_acc[...] = gate0_ref[...]
-    up_acc[...] = up0_ref[...]
-    stats_acc[...] = stats0_ref[...]
-    gate_up_half(half_ref[0], y_ref, wg_ref, wu_ref, gate_acc, up_acc, stats_acc)
-    stats = stats_acc[...]
+    own_ref[:, :width] = acc
+    send_ref[:, :width] = acc.astype(BF16)
+    high = stats.astype(BF16).astype(F32)
+    spare = jnp.zeros((CAP, 128 - 2 * stats.shape[1]), F32)
+    own_ref[:, width:] = jnp.concatenate([stats, jnp.zeros_like(stats), spare], axis=1)
+    send_ref[:, width:] = jnp.concatenate([high, stats - high, spare], axis=1).astype(BF16)
+
+
+def gate_up(y, w):
+    width = w.shape[1] + 128
+    return pl.pallas_call(
+        gate_up_kernel,
+        in_specs=[WHOLE] * 2,
+        out_specs=[WHOLE] * 2,
+        out_shape=[kept((CAP, width), F32), kept((CAP, width), BF16)],
+        compiler_params=pltpu.CompilerParams(vmem_limit_bytes=SMALL),
+        name="gate_up",
+    )(y, w)
+
+
+def down_kernel(own_ref, got_ref, mine_ref, w_ref, out_ref):
+    slices = w_ref.shape[0]
+    hidden = slices // 2
+    width = 2 * slices
+    lanes = LANES - CHUNK
+    stats = own_ref[:, width : width + lanes]
+    stats = stats + got_ref[:, width : width + lanes].astype(F32)
+    stats = stats + got_ref[:, width + lanes : width + 2 * lanes].astype(F32)
     square = stats[:, 16:17] + stats[:, 17:18]
     scale = lax.rsqrt(square * (1.0 / D) + 1e-6)
     affinity = jax.nn.sigmoid((stats[:, 0:8] + stats[:, 8:16]) * scale)
     own = jnp.sum(affinity * mine_ref[...], axis=1, keepdims=True)
     gates = 2.5 * own / jnp.sum(affinity, axis=1, keepdims=True)
-    gates_ref[...] = jnp.broadcast_to(gates.astype(BF16).astype(F32), gates_ref.shape)
-    gate = gate_acc[...] * scale
-    up = up_acc[...] * scale
-    act_ref[...] = (gate * jax.nn.sigmoid(gate) * up).astype(BF16)
-    down_step(half_ref[0], act_ref[...], gates_ref[:, :1], wd_ref, out_ref)
-
-
-def second_half(half, y, w_gate, w_up, w_down, gate, up, stats, mine):
-    hidden = w_gate.shape[2]
-    return pl.pallas_call(
-        second_kernel,
-        in_specs=[SCALAR] + [WHOLE] * 8,
-        out_specs=[WHOLE] * 3,
-        out_shape=[kept((CAP, hidden), BF16), kept((CAP, 128), F32), kept((NXY, CAP, LANES), BF16)],
-        scratch_shapes=[
-            pltpu.VMEM((CAP, hidden), F32),
-            pltpu.VMEM((CAP, hidden), F32),
-            pltpu.VMEM((CAP, LANES - CHUNK), F32),
-        ],
-        compiler_params=pltpu.CompilerParams(vmem_limit_bytes=SMALL),
-        cost_estimate=pl.CostEstimate(
-            flops=3 * CAP * D * hidden, bytes_accessed=3 * D * hidden + 2 * CAP * D, transcendentals=0
-        ),
-        name="gate_up_second",
-    )(half, y, w_gate, w_up, w_down, gate, up, stats, mine)
-
-
-def down_kernel(half_ref, act_ref, gates_ref, wd_ref, out_ref):
-    down_step(half_ref[0], act_ref[...], gates_ref[:, :1], wd_ref, out_ref)
-
-
-def down_own(half, act, gates, w_down):
-    hidden = act.shape[1]
+    gates = gates.astype(BF16).astype(F32)
+    acts = []
+    for j in range(2):
+        here, there = j * slices, (1 - j) * slices
+        both = own_ref[:, here : here + slices] + got_ref[:, there : there + slices].astype(F32)
+        gate = both[:, :hidden] * scale
+        acts.append((gate * jax.nn.sigmoid(gate) * (both[:, hidden:] * scale)).astype(BF16))
+    act = jnp.concatenate(acts, axis=1)
+    for i in range(STEPS):
+        acc = jnp.dot(act, w_ref[:, i * BLK : (i + 1) * BLK], preferred_element_type=F32) * gates
+        for g in range(GROUP):
+            out_ref[i * GROUP + g, :, :CHUNK] = acc[:, g * CHUNK : (g + 1) * CHUNK].astype(BF16)
+            out_ref[i * GROUP + g, :, CHUNK:] = jnp.zeros((CAP, LANES - CHUNK), BF16)
+
+
+def down(own, got, mine, w):
     return pl.pallas_call(
         down_kernel,
-        in_specs=[SCALAR] + [WHOLE] * 3,
+        in_specs=[WHOLE] * 4,
         out_specs=WHOLE,
-        out_shape=kept((NXY, CAP, LANES), F32),
-        compiler_params=pltpu.CompilerParams(vmem_limit_bytes=SMALL),
-        cost_estimate=pl.CostEstimate(
-            flops=CAP * D * hidden, bytes_accessed=D * hidden + 2 * CAP * D, transcendentals=0
-        ),
-        name="down_own",
-    )(half, act, gates, w_down)
+        out_shape=kept((NXY, CAP, LANES), BF16),
+        compiler_params=pltpu.CompilerParams(vmem_limit_bytes=SMALL),
+        name="down",
+    )(own, got, mine, w)
 
 
 def swap_cores(values):
@@ -460,7 +473,6 @@
     plane = lax.axis_index("z")
     core = lax.axis_index("c")
     place_xy = lax.axis_index("x") * NY + lax.axis_index("y")
-    dev_index = place_xy * NC + core
     rows_dev = queries.shape[0]
     own_half = jnp.reshape(core, (1,)).astype(jnp.int32)
     other_half = 1 - own_half
@@ -489,11 +501,14 @@
     gain_chunk = lax.dynamic_slice_in_dim(norm_gain, chunk * CHUNK, CHUNK, 0).astype(F32)[None, :]
     router_chunk = lax.dynamic_slice_in_dim(w_router, chunk * CHUNK, CHUNK, 0)
     row_iota = jnp.arange(ROWS, dtype=jnp.int32)
-    place = (row_iota[:, None] == dev_index * rows_dev + jnp.arange(16, dtype=jnp.int32)[None, :]) & (
-        jnp.arange(16) < rows_dev
-    )[None, :]
-    place = place.astype(BF16)
+    pair = jnp.arange(2, dtype=jnp.int32)
+    first_rows = (place_xy * NC + core + pair * (1 - 2 * core)) * rows_dev
+    place = row_iota[None, :, None] == (first_rows[:, None] + jnp.arange(16, dtype=jnp.int32)[None, :])[:, None, :]
+    place = (place & (jnp.arange(16) < rows_dev)[None, None, :]).astype(BF16)
     res = jnp.pad(residual, ((0, 16 - rows_dev), (0, 0)))
+
+    given = give_weights(other_half, w_out, res, w_gate, w_up, w_down)
+    got_out, got_in, got_down = [swap_cores(a) for a in given]
 
     cache_iota = jnp.arange(resident_cache.shape[1], dtype=jnp.int32)
     old_masks = cache_iota[None, :] < resident_len[0][:, None]
@@ -501,21 +516,21 @@
     context_old = context_old.reshape(-1, LAT)
     held = (
         received, context_old, queries[0].T, step_ranks, owner_ranks, mine, group_ids, gain_chunk,
-        router_chunk, place, res, own_half, other_half, plane_index,
+        router_chunk, place, res, own_half, plane_index, got_out, got_in, got_down,
     )
     (
         received, context_old, first_query, step_ranks, owner_ranks, mine, group_ids, gain_chunk,
-        router_chunk, place, res, own_half, other_half, plane_index,
+        router_chunk, place, res, own_half, plane_index, got_out, got_in, got_down,
     ) = lax.optimization_barrier(held)
-    context, w_uv, w_out = prompt_attention(first_query, received, new_latent, context_old, w_uv, w_out)
+    context, w_uv, w_out = prompt_attention(
+        own_half, first_query, received, new_latent, context_old, w_uv, w_out, res, got_out
+    )
 
     context = lax.all_to_all(context.reshape(NDEV, -1, LAT), ("x", "y", "c"), 0, 0, tiled=True)
     context = context.reshape(-1, LAT)
 
-    partial_other, attn = project_first(other_half, context, w_uv, place, res, w_out)
-    partial_got = swap_cores(partial_other)
-    partial_own = project_second(own_half, attn, place, res, w_out)
-    partial = (partial_own + partial_got.astype(F32)).astype(BF16)
+    attn = head_values(context, w_uv)
+    partial = project(attn, swap_cores(attn), place, w_out)
     partial = lax.all_to_all(partial, ("x", "y"), 0, 0, tiled=True)
 
     packed, hidden = pack_rows(partial, gain_chunk, router_chunk, group_ids, rows_dev)
@@ -523,18 +538,12 @@
     groups = [packed]
     for k in range(1, NZ):
         groups.append(lax.ppermute(packed, "z", [(i, (i + k) % NZ) for i in range(NZ)]))
-    w_gate, w_up, w_down = fetch(packed, (w_gate, w_up, w_down))
+    w_in, w_down = fetch_experts(packed, own_half, w_gate, w_up, w_down, got_in, got_down)
     slotted = slot_rows(w_down, step_ranks, groups)
     slotted = lax.all_to_all(slotted, ("x", "y"), 0, 0, tiled=True)
 
-    slotted_other = swap_cores(slotted)
-    gate, up, stats = first_half(own_half, slotted, w_gate, w_up)
-    act, gates, out_other = second_half(
-        other_half, slotted_other, w_gate, w_up, w_down, gate, up, stats, mine
-    )
-    out_got = swap_cores(out_other)
-    out_own = down_own(own_half, act, gates, w_down)
-    out = (out_own + out_got.astype(F32)).astype(BF16)
+    sums, to_send = gate_up(slotted, w_in)
+    out = down(sums, swap_cores(to_send), mine, w_down)
     out = lax.all_to_all(out, ("x", "y"), 0, 0, tiled=True)
 
     total = combine_rows(plane_index, out, owner_ranks, hidden, rows_dev)

time: 184 us -> 179 us (0.973)
  waiting for transfers between devices: 28.7 us -> 15.3 us
  Pallas kernels: 22.9 us -> 28.7 us
  matrix products: 5.46 us -> 7.83 us
    all_to_all x1, waiting for transfers between devices: 23.1 us -> 12.5 us  [per_device(): lax.all_to_all(spread(assignment, prompt_cache), ('x', 'y', 'c'), 0, 0, t...]
    pallas_call x7, Pallas kernels: 16 us -> 21.8 us  [the longest x1 6.71 us: give_weights(): pl.pallas_call(give_kernel, in_specs=[SCALAR] + [ANYWHERE] * 5, out_specs...]
    ppermute x3 -> x5, waiting for transfers between devices: 5.53 us -> 2.76 us  [swap_cores(): return lax.ppermute(values, 'c', [(0, 1), (1, 0)])]
    ppermute x3 -> x5, starting transfers between devices: 5.63 us -> 6.09 us  [swap_cores(): return lax.ppermute(values, 'c', [(0, 1), (1, 0)])]
  transfers between devices with their start and end apart: 7 -> 9, of which waited for: 5 -> 3; matrix products, arithmetic and copies ran while one was open for 5% -> 8% of each run, Pallas kernels for 4% -> 6%
where the time goes in v3:
time: 179 us; the launch traced here: 178 us
  blocking collectives  99.3 us (55%)
  Pallas kernels  28.7 us (16%)
  starting transfers between devices  19.3 us (11%)
  waiting for transfers between devices  15.3 us (9%)
  matrix products  7.83 us (4%)
  local copies, waits for them, and re-layouts  4.88 us (3%)
  other arithmetic  2.6 us (1%)
    all_to_all x1, blocking collectives, per_device(): out = lax.all_to_all(out, ('x', 'y'), 0, 0, tiled=True)  24.6 us
    all_to_all x1, blocking collectives, per_device(): slotted = lax.all_to_all(slotted, ('x', 'y'), 0, 0, tiled=True)  22.3 us
    all_to_all x1, blocking collectives, per_device(): partial = lax.all_to_all(partial, ('x', 'y'), 0, 0, tiled=True)  18.8 us
    all_to_all x1, blocking collectives, per_device(): total = lax.all_to_all(total, ('z', 'x', 'y', 'c'), 0, 0, tiled=True)  18 us
    all_to_all x1, blocking collectives, per_device(): lax.all_to_all(context.reshape(NDEV, -1, LAT), ('x', 'y', 'c'), 0, 0, til...  15.7 us
    all_to_all x1, waiting for transfers between devices, per_device(): lax.all_to_all(spread(assignment, prompt_cache), ('x', 'y', 'c'), 0, 0, t...  12.5 us
    all_to_all x1, starting transfers between devices, per_device(): lax.all_to_all(spread(assignment, prompt_cache), ('x', 'y', 'c'), 0, 0, t...  8.73 us
    pallas_call x1, Pallas kernels, give_weights(): pl.pallas_call(give_kernel, in_specs=[SCALAR] + [ANYWHERE] * 5, out_specs...  6.71 us
  transfers between devices with their start and end apart: 9, of which 3 were waited for; matrix products, arithmetic and copies ran while one was open for 8% of the time, Pallas kernels for 6%

profile of v3, /device:TPU:1, one launch (start us, length us, event | category | flops | bytes accessed | tf_op | source)
XLA Modules:
  0.0 178.4 jit_solution(2962550660475096043)
XLA Ops:
  0.7 3.6 %spread.1 = bf16[32,64,576]{2,1,0:T(8,128)(2,1)} custom-call(s32[1,32]{1,0:T(1,128)S(1)} %copy-done.3, bf16[32,64,576]{2,1,0:T(8,128)(2,1)} %cache_ref.1), custom_call_target="tpu_custom_call" | custom-call | tf_op jit(solution)/shard_map/spread/pallas_call | solution.py:83
  4.3 8.7 %all-to-all-start = ((bf16[32,64,576]{2,1,0:T(8,128)(2,1)}), bf16[32,64,576]{2,1,0:T(8,128)(2,1)S(1)}, u32[]{:S(2)}, u32[]{:S(2)}) async-start(bf16[32,64,576]{2,1,0:T(8,128)(2,1)} %spread.1), calls=%async_computation | async-start | bytes 5242880 | tf_op jit(solution)/shard_map/all_to_all | solution.py:482
  13.8 6.7 %give_weights.1 = (bf16[528,3584]{1,0:T(8,128)(2,1)}, bf16[2,3584,256]{2,1,0:T(8,128)(2,1)}, bf16[256,3584]{1,0:T(8,128)(2,1)}) custom-call(s32[1]{0:T(128)S(6)} %sub.49.half_ref, bf16[512,7168]{1,0:T(8,128)(2,1)} %w_hbm.1, bf16[16,7168]{1,0:T(8,128)(2,1)} %pad.4.res_hbm, bf16[1,7168,256]{2,1,0:T(8,128)(2,1)} %gate_hbm.3, bf16[1,7168,256]{2,1,0:T(8,128)(2,1)} %up_hbm.3, ...), custom_call_target="tpu_custom_call" | custom-call | tf_op jit(solution)/shard_map/give_weights/pallas_call | solution.py:330
  23.9 3.1 %fusion.26 = (f32[3,128]{1,0:T(4,128)S(1)}, f32[3,128,512]{2,1,0:T(8,128)}) fusion(bf16[4,128,576]{1,2,0:T(8,128)(2,1)} %param.19, bf16[3,512,576]{1,2,0:T(8,128)(2,1)} %param.17, pred[3,512]{1,0:T(4,128)(4,1)S(1)} %iota_compare_fusion.6), kind=kOutput, calls=%fused_computation.54 | convolution fusion | flops 227081856 | bytes 3148800 | tf_op jit(solution)/shard_map/vmap(hc,kc->hk)/dot_general | solution.py:54
  28.0 1.4 fusion.11
  29.7 1.6 slice_bitcast_fusion.query_hbm
  31.3 3.1 %fusion.6 = bf16[3,128,512]{2,1,0:T(8,128)(2,1)} fusion(bf16[3,512,576]{1,2,0:T(8,128)(2,1)} %param.17, f32[3,128,512]{2,1,0:T(8,128)} %get-tuple-element.64, f32[3,512]{1,0:T(4,128)S(1)} %slice_convert_fusion, f32[3,128]{1,0:T(4,128)S(1)} %get-tuple-element.62, f32[3,128]{1,0:T(4,128)S(1)} %get-tuple-element.61, f32[3,128]{1,0:T(4,128)S(1)} %fusion.21), kind=kOutput, calls=%fused_computation.6 | convolution fusion | flops 202506240 | bytes 2763264 | tf_op jit(solution)/shard_map/vmap(hk,kl->hl)/dot_general | solution.py:64
  34.4 12.5 %all-to-all-done.cache_ref = bf16[32,64,576]{2,1,0:T(8,128)(2,1)S(1)} async-done(((bf16[32,64,576]{2,1,0:T(8,128)(2,1)}), bf16[32,64,576]{2,1,0:T(8,128)(2,1)S(1)}, u32[]{:S(2)}, u32[]{:S(2)}) %all-to-all-start) | async-done | bytes 2359328 | tf_op jit(solution)/shard_map/all_to_all | solution.py:482
  47.0 4.1 %prompt_attention.1 = (bf16[512,512]{1,0:T(8,128)(2,1)S(1)}, bf16[4,512,128]{2,1,0:T(8,128)(2,1)S(1)}, bf16[1056,3584]{1,0:T(8,128)(2,1)S(1)}) custom-call(s32[1]{0:T(128)} %bitcast.15.half_ref, bf16[576,128]{1,0:T(8,128)(2,1)} %slice_bitcast_fusion.query_hbm, bf16[32,64,576]{2,1,0:T(8,128)(2,1)S(1)} %all-to-all-done.cache_ref, ...), custom_call_target="tpu_custom_call" | custom-call | tf_op jit(solution)/shard_map/prompt_attention/pallas_call | solution.py:145
  51.1 15.7 %all_to_all.30 = bf16[32,16,512]{2,1,0:T(8,128)(2,1)S(1)} all-to-all(bf16[32,16,512]{2,1,0:T(8,128)(2,1)S(1)} %bitcast.52), channel_id=1, replica_groups=mesh['z'=4,'x'=4,'y'=4,'c'=2] {'x','y','c'}, dimensions={0} | all-to-all | bytes 1048576 | tf_op jit(solution)/shard_map/all_to_all | solution.py:529
  66.8 1.7 head_values.1.own_ref
  68.6 1.3 collective-permute-done.3.got_ref
  69.9 1.8 %project.1 = bf16[16,128,256]{2,1,0:T(8,128)(2,1)S(1)} custom-call(bf16[128,512]{1,0:T(8,128)(2,1)S(1)} %head_values.1.own_ref, bf16[128,512]{1,0:T(8,128)(2,1)S(1)} %collective-permute-done.3.got_ref, bf16[2,128,16]{2,1,0:T(8,128)(2,1)S(1)} %fusion.17.place_ref, bf16[1056,3584]{1,0:T(8,128)(2,1)S(1)} %get-tuple-element.46.w_ref), custom_call_target="tpu_custom_call" | custom-call | tf_op jit(solution)/shard_map/project/pallas_call | solution.py:202
  71.7 18.8 %all_to_all.31.part_ref = bf16[16,128,256]{2,1,0:T(8,128)(2,1)S(1)} all-to-all(bf16[16,128,256]{2,1,0:T(8,128)(2,1)S(1)} %project.1), channel_id=1, replica_groups=mesh['z'=4,'x'=4,'y'=4,'c'=2] {'x','y'}, dimensions={0} | all-to-all | bytes 2097152 | tf_op jit(solution)/shard_map/all_to_all | solution.py:534
  91.4 3.8 %collective-permute-start.6 = (bf16[128,256]{1,0:T(8,128)(2,1)S(1)}, bf16[128,256]{1,0:T(8,128)(2,1)S(1)}, u32[]{:S(2)}, u32[]{:S(2)}) collective-permute-start(bf16[128,256]{1,0:T(8,128)(2,1)S(1)} %get-tuple-element.50.after_ref.refs_0_), channel_id=1, source_target_pairs={{0,96},{32,0},{64,32},{96,64},{1,97},{33,1},{65,33},{97,65},{2,98}... | collective-permute-start | bytes 196616 | tf_op jit(solution)/shard_map/ppermute | solution.py:540
  95.9 4.2 %fetch_experts.1 = (bf16[3584,1024]{1,0:T(8,128)(2,1)S(1)}, bf16[512,3584]{1,0:T(8,128)(2,1)S(1)}) custom-call(bf16[128,256]{1,0:T(8,128)(2,1)S(1)} %get-tuple-element.50.after_ref.refs_0_, s32[1]{0:T(128)} %bitcast.15.half_ref, bf16[1,7168,256]{2,1,0:T(8,128)(2,1)} %gate_hbm.3, bf16[1,7168,256]{2,1,0:T(8,128)(2,1)} %up_hbm.3, ...), custom_call_target="tpu_custom_call" | custom-call | bytes 22020096 | tf_op jit(solution)/shard_map/fetch_experts/pallas_call | solution.py:372
  100.8 22.3 %all_to_all.32.y_ref = bf16[16,192,256]{2,1,0:T(8,128)(2,1)S(1)} all-to-all(bf16[16,192,256]{2,1,0:T(8,128)(2,1)S(1)} %slot_rows.1), channel_id=1, replica_groups=mesh['z'=4,'x'=4,'y'=4,'c'=2] {'x','y'}, dimensions={0} | all-to-all | bytes 3145728 | tf_op jit(solution)/shard_map/all_to_all | solution.py:543
  123.1 1.8 %gate_up.1 = (f32[192,1152]{1,0:T(8,128)S(1)}, bf16[192,1152]{1,0:T(8,128)(2,1)S(1)}) custom-call(bf16[16,192,256]{2,1,0:T(8,128)(2,1)S(1)} %all_to_all.32.y_ref, bf16[3584,1024]{1,0:T(8,128)(2,1)S(1)} %get-tuple-element.55.w_ref), custom_call_target="tpu_custom_call" | custom-call | tf_op jit(solution)/shard_map/gate_up/pallas_call | solution.py:403
  125.0 5.2 %collective-permute-start.7 = (bf16[192,1152]{1,0:T(8,128)(2,1)S(1)}, bf16[192,1152]{1,0:T(8,128)(2,1)S(1)}, u32[]{:S(2)}, u32[]{:S(2)}) collective-permute-start(bf16[192,1152]{1,0:T(8,128)(2,1)S(1)} %get-tuple-element.57), channel_id=1, source_target_pairs={{0,1},{1,0},{2,3},{3,2},{4,5},{5,4},{6,7},{7,6},{8,9},{9,8},{10,11... | collective-permute-start | bytes 1327112 | tf_op jit(solution)/shard_map/ppermute | solution.py:453
  130.1 1.4 collective-permute-done.7.got_ref
  131.6 1.3 down.1
  132.9 24.6 %all_to_all.33.out_ref = bf16[16,192,256]{2,1,0:T(8,128)(2,1)S(1)} all-to-all(bf16[16,192,256]{2,1,0:T(8,128)(2,1)S(1)} %down.1), channel_id=1, replica_groups=mesh['z'=4,'x'=4,'y'=4,'c'=2] {'x','y'}, dimensions={0} | all-to-all | bytes 3145728 | tf_op jit(solution)/shard_map/all_to_all | solution.py:547
  157.5 1.9 %combine_rows.1 = bf16[128,4,256]{2,1,0:T(4,128)(2,1)S(1)} custom-call(s32[1]{0:T(128)} %bitcast.16.plane_ref, bf16[16,192,256]{2,1,0:T(8,128)(2,1)S(1)} %all_to_all.33.out_ref, s32[512,8]{1,0:T(8,128)S(1)} %bitcast.51, f32[128,256]{1,0:T(8,128)S(1)} %get-tuple-element.60.hidden_ref), custom_call_target="tpu_custom_call" | custom-call | tf_op jit(solution)/shard_map/combine_rows/pallas_call | solution.py:292
  159.4 18.0 %all_to_all.34 = bf16[128,4,256]{2,1,0:T(4,128)(2,1)S(1)} all-to-all(bf16[128,4,256]{2,1,0:T(4,128)(2,1)S(1)} %combine_rows.1), channel_id=1, replica_groups=mesh['z'=4,'x'=4,'y'=4,'c'=2] {'z','x','y','c'}, dimensions={0} | all-to-all | bytes 524288 | tf_op jit(solution)/shard_map/all_to_all | solution.py:550
  (58 shorter events, 9.3 us)
Async XLA Ops:
  0.0 26.9 %copy-start = (bf16[7168,32]{0,1:T(8,128)(2,1)S(1)}, bf16[7168,32]{0,1:T(8,128)(2,1)}, u32[]{:S(2)}) copy-start(bf16[7168,32]{0,1:T(8,128)(2,1)} %param.25) | copy-start | bytes 1376260
  0.0 0.7 copy-start.3
  4.3 8.8 %copy-start.4 = (bf16[4,7168]{1,0:T(4,128)(2,1)S(1)}, bf16[4,7168]{1,0:T(4,128)(2,1)}, u32[]{:S(2)}) copy-start(bf16[4,7168]{1,0:T(4,128)(2,1)} %param.21) | copy-start | bytes 172036
  4.3 42.6 %all-to-all-start = ((bf16[32,64,576]{2,1,0:T(8,128)(2,1)}), bf16[32,64,576]{2,1,0:T(8,128)(2,1)S(1)}, u32[]{:S(2)}, u32[]{:S(2)}) async-start(bf16[32,64,576]{2,1,0:T(8,128)(2,1)} %spread.1), calls=%async_computation | async-start | bytes 5242880 | tf_op jit(solution)/shard_map/all_to_all | solution.py:482
  13.8 7.6 %copy-start.5 = (s32[512,8]{0,1:T(8,128)S(1)}, s32[512,8]{0,1:T(8,128)}, u32[]{:S(2)}) copy-start(s32[512,8]{0,1:T(8,128)} %param.26) | copy-start | bytes 49156
  13.8 8.8 %copy-start.6 = (s32[1,3]{1,0:T(1,128)S(1)}, s32[1,3]{1,0:T(1,128)}, u32[]{:S(2)}) copy-start(s32[1,3]{1,0:T(1,128)} %param.18) | copy-start | bytes 40
  13.8 8.8 %copy-start.2 = (bf16[4,576]{1,0:T(4,128)(2,1)S(1)}, bf16[4,576]{1,0:T(4,128)(2,1)}, u32[]{:S(2)}) copy-start(bf16[4,576]{1,0:T(4,128)(2,1)} %entry_ref.1) | copy-start | bytes 13828
  20.5 13.9 %collective-permute-start.2 = (bf16[256,3584]{1,0:T(8,128)(2,1)}, bf16[256,3584]{1,0:T(8,128)(2,1)}, u32[]{:S(2)}, u32[]{:S(2)}) collective-permute-start(bf16[256,3584]{1,0:T(8,128)(2,1)} %get-tuple-element.35), channel_id=1, source_target_pairs={{0,1},{1,0},{2,3},{3,2},{4,5},{5,4},{6,7},{7,6},{8,9},{9,8},{10,11... | collective-permute-start | bytes 5505032 | tf_op jit(solution)/shard_map/ppermute | solution.py:453
  20.9 26.1 %collective-permute-start.1 = (bf16[2,3584,256]{2,1,0:T(8,128)(2,1)}, bf16[2,3584,256]{2,1,0:T(8,128)(2,1)}, u32[]{:S(2)}, u32[]{:S(2)}) collective-permute-start(bf16[2,3584,256]{2,1,0:T(8,128)(2,1)} %get-tuple-element.34), channel_id=1, source_target_pairs={{0,1},{1,0},{2,3},{3,2},{4,5},{5,4},{6,7},{7,6},{8,9},{9,8},{10,11... | collective-permute-start | bytes 11010056 | tf_op jit(solution)/shard_map/ppermute | solution.py:453
  21.1 25.8 %collective-permute-start = (bf16[528,3584]{1,0:T(8,128)(2,1)}, bf16[528,3584]{1,0:T(8,128)(2,1)}, u32[]{:S(2)}, u32[]{:S(2)}) collective-permute-start(bf16[528,3584]{1,0:T(8,128)(2,1)} %get-tuple-element.33), channel_id=1, source_target_pairs={{0,1},{1,0},{2,3},{3,2},{4,5},{5,4},{6,7},{7,6},{8,9},{9,8},{10,11... | collective-permute-start | bytes 11354120 | tf_op jit(solution)/shard_map/ppermute | solution.py:453
  68.5 1.4 collective-permute-start.3
  91.4 8.8 %collective-permute-start.6 = (bf16[128,256]{1,0:T(8,128)(2,1)S(1)}, bf16[128,256]{1,0:T(8,128)(2,1)S(1)}, u32[]{:S(2)}, u32[]{:S(2)}) collective-permute-start(bf16[128,256]{1,0:T(8,128)(2,1)S(1)} %get-tuple-element.50.after_ref.refs_0_), channel_id=1, source_target_pairs={{0,96},{32,0},{64,32},{96,64},{1,97},{33,1},{65,33},{97,65},{2,98}... | collective-permute-start | bytes 196616 | tf_op jit(solution)/shard_map/ppermute | solution.py:540
  95.2 5.0 %collective-permute-start.5 = (bf16[128,256]{1,0:T(8,128)(2,1)S(1)}, bf16[128,256]{1,0:T(8,128)(2,1)S(1)}, u32[]{:S(2)}, u32[]{:S(2)}) collective-permute-start(bf16[128,256]{1,0:T(8,128)(2,1)S(1)} %get-tuple-element.50.after_ref.refs_0_), channel_id=1, source_target_pairs={{0,64},{32,96},{64,0},{96,32},{1,65},{33,97},{65,1},{97,33},{2,66}... | collective-permute-start | bytes 196616 | tf_op jit(solution)/shard_map/ppermute | solution.py:540
  95.2 5.0 %collective-permute-start.4 = (bf16[128,256]{1,0:T(8,128)(2,1)S(1)}, bf16[128,256]{1,0:T(8,128)(2,1)S(1)}, u32[]{:S(2)}, u32[]{:S(2)}) collective-permute-start(bf16[128,256]{1,0:T(8,128)(2,1)S(1)} %get-tuple-element.50.after_ref.refs_0_), channel_id=1, source_target_pairs={{0,32},{32,64},{64,96},{96,0},{1,33},{33,65},{65,97},{97,1},{2,34}... | collective-permute-start | bytes 196616 | tf_op jit(solution)/shard_map/ppermute | solution.py:540
  125.0 6.6 %collective-permute-start.7 = (bf16[192,1152]{1,0:T(8,128)(2,1)S(1)}, bf16[192,1152]{1,0:T(8,128)(2,1)S(1)}, u32[]{:S(2)}, u32[]{:S(2)}) collective-permute-start(bf16[192,1152]{1,0:T(8,128)(2,1)S(1)} %get-tuple-element.57), channel_id=1, source_target_pairs={{0,1},{1,0},{2,3},{3,2},{4,5},{5,4},{6,7},{7,6},{8,9},{9,8},{10,11... | collective-permute-start | bytes 1327112 | tf_op jit(solution)/shard_map/ppermute | solution.py:453
  131.6 46.8 %copy-start.1 = (bf16[7168,32]{0,1:T(8,128)(2,1)S(1)}, bf16[7168,32]{0,1:T(8,128)(2,1)}, u32[]{:S(2)}) copy-start(bf16[7168,32]{0,1:T(8,128)(2,1)} %param.25) | copy-start | bytes 1376260

commit v4 on v3

--- a/solution.py
+++ b/solution.py
@@ -66,30 +66,61 @@
     return context.astype(BF16)
 
 
-def spread_kernel(owners_ref, cache_ref, out_ref, held_ref, in_sem, out_sem):
-    arrive = [pltpu.make_async_copy(cache_ref.at[p], held_ref.at[p], in_sem.at[p]) for p in range(NDEV)]
+def pack_chunk(ref, at, part):
+    rows, most = part.shape[0], part.shape[0] * 3 // 4
+    rest = part[:, 128:]
+    ref[at, :rows, :] = part[:, :128].astype(ref.dtype)
+    ref[at, rows:, :96] = rest[:most].astype(ref.dtype)
+    tail = jnp.concatenate([rest[most:, 32 * i : 32 * (i + 1)] for i in range(3)], axis=0)
+    ref[at, rows:, 96:] = tail.astype(ref.dtype)
+
+
+def unpack_chunk(packed):
+    rows = packed.shape[0] * 4 // 7
+    most, few = rows * 3 // 4, rows // 4
+    rest = packed[rows:, :96]
+    tail = [packed[rows + few * i : rows + few * (i + 1), 96:] for i in range(3)]
+    rest = jnp.concatenate([rest, jnp.concatenate(tail, axis=1)], axis=0)
+    return jnp.concatenate([packed[:rows], rest], axis=1)
+
+
+def spread_kernel(owners_ref, cache_ref, out_ref, held_ref, packed_ref, in_sem, out_sem):
+    batch = NDEV // in_sem.shape[0]
+    tokens, half = cache_ref.shape[1], cache_ref.shape[1] // 2
+    arrive = []
+    for b in range(in_sem.shape[0]):
+        at = pl.ds(b * batch, batch)
+        arrive.append(pltpu.make_async_copy(cache_ref.at[at], held_ref.at[at], in_sem.at[b]))
     leave = [
-        pltpu.make_async_copy(held_ref.at[p], out_ref.at[owners_ref[0, p]], out_sem.at[p]) for p in range(NDEV)
+        pltpu.make_async_copy(packed_ref.at[p], out_ref.at[owners_ref[0, p]], out_sem.at[p])
+        for p in range(NDEV)
     ]
     start_all(arrive)
     for p in range(NDEV):
-        arrive[p].wait()
+        if p % batch == 0:
+            arrive[p // batch].wait()
+        for j in range(LAT // 128):
+            packed_ref[p, j * tokens : (j + 1) * tokens, :] = held_ref[p, :, j * 128 : (j + 1) * 128]
+        tail = jnp.concatenate([held_ref[p, :half, LAT:], held_ref[p, half:, LAT:]], axis=1)
+        packed_ref[p, LAT // 128 * tokens :, :] = tail
         leave[p].start()
     for p in range(NDEV):
         leave[p].wait()
 
 
 def spread(owners, cache):
+    packed = (NDEV, cache.shape[1] * cache.shape[2] // 128, 128)
     return pl.pallas_call(
         spread_kernel,
         in_specs=[SCALAR, ANYWHERE],
         out_specs=ANYWHERE,
         scratch_shapes=[
             pltpu.VMEM(cache.shape, cache.dtype),
-            pltpu.SemaphoreType.DMA((NDEV,)),
+            pltpu.VMEM(packed, cache.dtype),
+            pltpu.SemaphoreType.DMA((8,)),
             pltpu.SemaphoreType.DMA((NDEV,)),
         ],
-        out_shape=pltpu.HBM(cache.shape, cache.dtype),
+        out_shape=pltpu.HBM(packed, cache.dtype),
         compiler_params=pltpu.CompilerParams(vmem_limit_bytes=SMALL),
         name="spread",
     )(owners, in_hbm(cache))
@@ -112,11 +143,22 @@
     )
     start_all((query_copy, old_copy, uv_copy) + w_copies)
     scale_factor = (NOPE + ROPE) ** (-0.5)
-    cache = cache_ref[...].reshape(-1, cache_ref.shape[-1])
+    sources, tokens = cache_ref.shape[0], cache_ref.shape[1] * 128 // query_ref.shape[0]
+    tiles = [cache_ref[:, j * tokens : (j + 1) * tokens, :].reshape(-1, 128) for j in range(LAT // 128)]
+    cache = jnp.concatenate(tiles, axis=1)
+    rope = cache_ref[:, LAT // 128 * tokens :, :].reshape(-1, 128)
     entry = entry_ref[:1, :]
     query_copy.wait()
     query = query_ref[...]
-    scores = jnp.dot(cache, query, preferred_element_type=F32) * scale_factor
+    tail = query[LAT:, :]
+    blank = jnp.zeros_like(tail)
+    tail = jnp.concatenate(
+        [jnp.concatenate([tail, blank], axis=0), jnp.concatenate([blank, tail], axis=0)], axis=1
+    )
+    extra = jnp.dot(rope, tail, preferred_element_type=F32)
+    extra = [extra[:, h * heads_all : (h + 1) * heads_all].reshape(sources, -1, heads_all) for h in range(2)]
+    scores = jnp.dot(cache, query[:LAT, :], preferred_element_type=F32)
+    scores = (scores + jnp.concatenate(extra, axis=1).reshape(scores.shape)) * scale_factor
     own_score = jnp.dot(entry, query, preferred_element_type=F32) * scale_factor
     maximum = jnp.maximum(jnp.max(scores, axis=0, keepdims=True), own_score)
     exponent = jnp.exp(scores - maximum)
@@ -125,7 +167,7 @@
     weights = (exponent / totals).astype(BF16)
     own_weight = (own_exponent / totals).astype(BF16)
     over_rows = (((0,), (0,)), ((), ()))
-    context = lax.dot_general(weights, cache[:, :LAT], over_rows, preferred_element_type=F32)
+    context = lax.dot_general(weights, cache, over_rows, preferred_element_type=F32)
     context = context + lax.dot_general(own_weight, entry[:, :LAT], over_rows, preferred_element_type=F32)
     all_ref[:heads_all, :] = context.astype(BF16)
     rows, block = out_ref.shape[0], out_ref.shape[0] // NDEV
@@ -194,8 +236,7 @@
             )
             at += left.shape[1]
         for g in range(GROUP):
-            out_ref[i * GROUP + g, :, :CHUNK] = acc[:, g * CHUNK : (g + 1) * CHUNK].astype(BF16)
-            out_ref[i * GROUP + g, :, CHUNK:] = jnp.zeros((ROWS, LANES - CHUNK), BF16)
+            pack_chunk(out_ref, i * GROUP + g, acc[:, g * CHUNK : (g + 1) * CHUNK])
 
 
 def project(own, got, place, w_out):
@@ -203,7 +244,7 @@
         project_kernel,
         in_specs=[WHOLE] * 4,
         out_specs=WHOLE,
-        out_shape=kept((NXY, ROWS, LANES), BF16),
+        out_shape=kept((NXY, ROWS * CHUNK // 128, 128), BF16),
         compiler_params=pltpu.CompilerParams(vmem_limit_bytes=SMALL),
         name="project",
     )(own, got, place, w_out)
@@ -213,12 +254,12 @@
     total = part_ref[0].astype(F32)
     for source in range(1, part_ref.shape[0]):
         total = total + part_ref[source].astype(F32)
-    total = total.astype(BF16)
+    total = unpack_chunk(total.astype(BF16))
     to = lax.broadcasted_iota(jnp.int32, (ROWS, ROWS), 0)
     order = to % (ROWS // rows_dev) * rows_dev + to // (ROWS // rows_dev)
     order = (lax.broadcasted_iota(jnp.int32, (ROWS, ROWS), 1) == order).astype(BF16)
     hidden_ref[...] = jnp.dot(order, total, preferred_element_type=F32)
-    hidden = total[:, :CHUNK].astype(F32)
+    hidden = total.astype(F32)
     square = jnp.sum(hidden * hidden, axis=1, keepdims=True)
     scaled = (hidden * gain_ref[...]).astype(BF16)
     logits = jnp.dot(scaled, router_ref[...], preferred_element_type=F32)
@@ -240,7 +281,7 @@
 def pack_rows(part, gain, router, ids, rows_dev):
     return pl.pallas_call(
         functools.partial(rows_kernel, rows_dev),
-        out_shape=[kept((ROWS, LANES), BF16), kept((ROWS, LANES), F32)],
+        out_shape=[kept((ROWS, LANES), BF16), kept((ROWS, CHUNK), F32)],
         compiler_params=pltpu.CompilerParams(vmem_limit_bytes=SMALL),
         name="pack_rows",
     )(part, gain, router, ids)
@@ -272,11 +313,11 @@
 
 def combine_kernel(plane_ref, out_ref, ranks_ref, hidden_ref, rows_ref, acc_ref):
     slot = lax.broadcasted_iota(jnp.int32, (ALL_ROWS, CAP), 1)
-    acc = jnp.zeros((ALL_ROWS, LANES), F32)
+    acc = jnp.zeros((ALL_ROWS, CHUNK), F32)
     for e in range(EXP_G):
         table = (ranks_ref[:, e : e + 1] == slot).astype(BF16)
-        acc = acc + jnp.dot(table, out_ref[2 * e], preferred_element_type=F32)
-        acc = acc + jnp.dot(table, out_ref[2 * e + 1], preferred_element_type=F32)
+        for source in (2 * e, 2 * e + 1):
+            acc = acc + jnp.dot(table, unpack_chunk(out_ref[source]), preferred_element_type=F32)
     acc_ref[...] = acc
     span, count = rows_ref.shape[0], rows_ref.shape[1]
     own = ROWS // count
@@ -293,8 +334,8 @@
         combine_kernel,
         in_specs=[pl.BlockSpec(memory_space=pltpu.SMEM), vmem, vmem, vmem],
         out_specs=vmem,
-        out_shape=kept((ALL_ROWS // count, count, LANES), BF16),
-        scratch_shapes=[pltpu.VMEM((ALL_ROWS, LANES), F32)],
+        out_shape=kept((ALL_ROWS // count, count, CHUNK), BF16),
+        scratch_shapes=[pltpu.VMEM((ALL_ROWS, CHUNK), F32)],
         compiler_params=pltpu.CompilerParams(vmem_limit_bytes=SMALL),
         name="combine_rows",
     )(plane, out, ranks, hidden)
@@ -434,8 +475,7 @@
     for i in range(STEPS):
         acc = jnp.dot(act, w_ref[:, i * BLK : (i + 1) * BLK], preferred_element_type=F32) * gates
         for g in range(GROUP):
-            out_ref[i * GROUP + g, :, :CHUNK] = acc[:, g * CHUNK : (g + 1) * CHUNK].astype(BF16)
-            out_ref[i * GROUP + g, :, CHUNK:] = jnp.zeros((CAP, LANES - CHUNK), BF16)
+            pack_chunk(out_ref, i * GROUP + g, acc[:, g * CHUNK : (g + 1) * CHUNK])
 
 
 def down(own, got, mine, w):
@@ -443,7 +483,7 @@
         down_kernel,
         in_specs=[WHOLE] * 4,
         out_specs=WHOLE,
-        out_shape=kept((NXY, CAP, LANES), BF16),
+        out_shape=kept((NXY, CAP * CHUNK // 128, 128), BF16),
         compiler_params=pltpu.CompilerParams(vmem_limit_bytes=SMALL),
         name="down",
     )(own, got, mine, w)
@@ -548,7 +588,7 @@
 
     total = combine_rows(plane_index, out, owner_ranks, hidden, rows_dev)
     total = lax.all_to_all(total, ("z", "x", "y", "c"), 0, 0, tiled=True)
-    total = jnp.sum(total.reshape(NZ, NXY, NC, rows_dev, LANES)[..., :CHUNK].astype(F32), axis=0)
+    total = jnp.sum(total.reshape(NZ, NXY, NC, rows_dev, CHUNK).astype(F32), axis=0)
     return total.transpose(2, 1, 0, 3).reshape(rows_dev, D).astype(BF16)
 
 

time: 179 us -> 173 us (0.966)
  blocking collectives: 99.3 us -> 95.4 us
  waiting for transfers between devices: 15.3 us -> 12.6 us
    all_to_all x1, waiting for transfers between devices: 12.5 us -> 9.79 us  [per_device(): lax.all_to_all(spread(assignment, prompt_cache), ('x', 'y', 'c'), 0, 0, t...]
    all_to_all x1, blocking collectives: 24.6 us -> 22.3 us  [per_device(): out = lax.all_to_all(out, ('x', 'y'), 0, 0, tiled=True)]
  transfers between devices with their start and end apart: 9 -> 9, of which waited for: 3 -> 4; matrix products, arithmetic and copies ran while one was open for 8% -> 8% of each run, Pallas kernels for 6% -> 6%
where the time goes in v4:
time: 173 us; the launch traced here: 172 us
  blocking collectives  95.4 us (55%)
  Pallas kernels  28.9 us (17%)
  starting transfers between devices  19.4 us (11%)
  waiting for transfers between devices  12.6 us (7%)
  matrix products  7.8 us (5%)
  local copies, waits for them, and re-layouts  4.88 us (3%)
  other arithmetic  2.62 us (2%)
    all_to_all x1, blocking collectives, per_device(): out = lax.all_to_all(out, ('x', 'y'), 0, 0, tiled=True)  22.3 us
    all_to_all x1, blocking collectives, per_device(): slotted = lax.all_to_all(slotted, ('x', 'y'), 0, 0, tiled=True)  22.1 us
    all_to_all x1, blocking collectives, per_device(): total = lax.all_to_all(total, ('z', 'x', 'y', 'c'), 0, 0, tiled=True)  18.2 us
    all_to_all x1, blocking collectives, per_device(): partial = lax.all_to_all(partial, ('x', 'y'), 0, 0, tiled=True)  17.5 us
    all_to_all x1, blocking collectives, per_device(): lax.all_to_all(context.reshape(NDEV, -1, LAT), ('x', 'y', 'c'), 0, 0, til...  15.3 us
    all_to_all x1, waiting for transfers between devices, per_device(): lax.all_to_all(spread(assignment, prompt_cache), ('x', 'y', 'c'), 0, 0, t...  9.79 us
    all_to_all x1, starting transfers between devices, per_device(): lax.all_to_all(spread(assignment, prompt_cache), ('x', 'y', 'c'), 0, 0, t...  8.73 us
    pallas_call x1, Pallas kernels, give_weights(): pl.pallas_call(give_kernel, in_specs=[SCALAR] + [ANYWHERE] * 5, out_specs...  6.73 us
  transfers between devices with their start and end apart: 9, of which 4 were waited for; matrix products, arithmetic and copies ran while one was open for 8% of the time, Pallas kernels for 6%

profile of v4, /device:TPU:1, one launch (start us, length us, event | category | flops | bytes accessed | tf_op | source)
XLA Modules:
  0.0 171.9 jit_solution(6789843790889112910)
XLA Ops:
  0.7 3.4 %spread.1 = bf16[32,288,128]{2,1,0:T(8,128)(2,1)} custom-call(s32[1,32]{1,0:T(1,128)S(1)} %copy-done.3, bf16[32,64,576]{2,1,0:T(8,128)(2,1)} %cache_ref.1), custom_call_target="tpu_custom_call" | custom-call | tf_op jit(solution)/shard_map/spread/pallas_call | solution.py:113
  4.2 8.7 %all-to-all-start = ((bf16[32,288,128]{2,1,0:T(8,128)(2,1)}), bf16[32,288,128]{2,1,0:T(8,128)(2,1)S(1)}, u32[]{:S(2)}, u32[]{:S(2)}) async-start(bf16[32,288,128]{2,1,0:T(8,128)(2,1)} %spread.1), calls=%async_computation | async-start | bytes 4718592 | tf_op jit(solution)/shard_map/all_to_all | solution.py:522
  13.7 6.7 %give_weights.1 = (bf16[528,3584]{1,0:T(8,128)(2,1)}, bf16[2,3584,256]{2,1,0:T(8,128)(2,1)}, bf16[256,3584]{1,0:T(8,128)(2,1)}) custom-call(s32[1]{0:T(128)S(6)} %sub.49.half_ref, bf16[512,7168]{1,0:T(8,128)(2,1)} %w_hbm.1, bf16[16,7168]{1,0:T(8,128)(2,1)} %pad.4.res_hbm, bf16[1,7168,256]{2,1,0:T(8,128)(2,1)} %gate_hbm.3, bf16[1,7168,256]{2,1,0:T(8,128)(2,1)} %up_hbm.3, ...), custom_call_target="tpu_custom_call" | custom-call | tf_op jit(solution)/shard_map/give_weights/pallas_call | solution.py:371
  23.7 3.1 %fusion.26 = (f32[3,128]{1,0:T(4,128)S(1)}, f32[3,128,512]{2,1,0:T(8,128)}) fusion(bf16[4,128,576]{1,2,0:T(8,128)(2,1)} %param.19, bf16[3,512,576]{1,2,0:T(8,128)(2,1)} %param.17, pred[3,512]{1,0:T(4,128)(4,1)S(1)} %iota_compare_fusion.6), kind=kOutput, calls=%fused_computation.53 | convolution fusion | flops 227081856 | bytes 3148800 | tf_op jit(solution)/shard_map/vmap(hc,kc->hk)/dot_general | solution.py:54
  27.8 1.4 fusion.11
  29.6 1.6 slice_bitcast_fusion.query_hbm
  31.2 3.1 %fusion.6 = bf16[3,128,512]{2,1,0:T(8,128)(2,1)} fusion(bf16[3,512,576]{1,2,0:T(8,128)(2,1)} %param.17, f32[3,128,512]{2,1,0:T(8,128)} %get-tuple-element.64, f32[3,512]{1,0:T(4,128)S(1)} %slice_convert_fusion, f32[3,128]{1,0:T(4,128)S(1)} %get-tuple-element.62, f32[3,128]{1,0:T(4,128)S(1)} %get-tuple-element.61, f32[3,128]{1,0:T(4,128)S(1)} %fusion.21), kind=kOutput, calls=%fused_computation.6 | convolution fusion | flops 202506240 | bytes 2763264 | tf_op jit(solution)/shard_map/vmap(hk,kl->hl)/dot_general | solution.py:64
  34.3 9.8 %all-to-all-done.cache_ref = bf16[32,288,128]{2,1,0:T(8,128)(2,1)S(1)} async-done(((bf16[32,288,128]{2,1,0:T(8,128)(2,1)}), bf16[32,288,128]{2,1,0:T(8,128)(2,1)S(1)}, u32[]{:S(2)}, u32[]{:S(2)}) %all-to-all-start) | async-done | bytes 2359328 | tf_op jit(solution)/shard_map/all_to_all | solution.py:522
  44.1 3.9 %prompt_attention.1 = (bf16[512,512]{1,0:T(8,128)(2,1)S(1)}, bf16[4,512,128]{2,1,0:T(8,128)(2,1)S(1)}, bf16[1056,3584]{1,0:T(8,128)(2,1)S(1)}) custom-call(s32[1]{0:T(128)} %bitcast.15.half_ref, bf16[576,128]{1,0:T(8,128)(2,1)} %slice_bitcast_fusion.query_hbm, bf16[32,288,128]{2,1,0:T(8,128)(2,1)S(1)} %all-to-all-done.cache_ref, ...), custom_call_target="tpu_custom_call" | custom-call | tf_op jit(solution)/shard_map/prompt_attention/pallas_call | solution.py:187
  48.0 15.3 %all_to_all.30 = bf16[32,16,512]{2,1,0:T(8,128)(2,1)S(1)} all-to-all(bf16[32,16,512]{2,1,0:T(8,128)(2,1)S(1)} %bitcast.52), channel_id=1, replica_groups=mesh['z'=4,'x'=4,'y'=4,'c'=2] {'x','y','c'}, dimensions={0} | all-to-all | bytes 1048576 | tf_op jit(solution)/shard_map/all_to_all | solution.py:569
  63.2 1.7 head_values.1.own_ref
  65.0 1.3 collective-permute-done.3.got_ref
  66.4 1.9 %project.1 = bf16[16,224,128]{2,1,0:T(8,128)(2,1)S(1)} custom-call(bf16[128,512]{1,0:T(8,128)(2,1)S(1)} %head_values.1.own_ref, bf16[128,512]{1,0:T(8,128)(2,1)S(1)} %collective-permute-done.3.got_ref, bf16[2,128,16]{2,1,0:T(8,128)(2,1)S(1)} %fusion.17.place_ref, bf16[1056,3584]{1,0:T(8,128)(2,1)S(1)} %get-tuple-element.46.w_ref), custom_call_target="tpu_custom_call" | custom-call | tf_op jit(solution)/shard_map/project/pallas_call | solution.py:243
  68.3 17.5 %all_to_all.31.part_ref = bf16[16,224,128]{2,1,0:T(8,128)(2,1)S(1)} all-to-all(bf16[16,224,128]{2,1,0:T(8,128)(2,1)S(1)} %project.1), channel_id=1, replica_groups=mesh['z'=4,'x'=4,'y'=4,'c'=2] {'x','y'}, dimensions={0} | all-to-all | bytes 1835008 | tf_op jit(solution)/shard_map/all_to_all | solution.py:574
  86.8 3.9 %collective-permute-start.6 = (bf16[128,256]{1,0:T(8,128)(2,1)S(1)}, bf16[128,256]{1,0:T(8,128)(2,1)S(1)}, u32[]{:S(2)}, u32[]{:S(2)}) collective-permute-start(bf16[128,256]{1,0:T(8,128)(2,1)S(1)} %get-tuple-element.50.after_ref.refs_0_), channel_id=1, source_target_pairs={{0,96},{32,0},{64,32},{96,64},{1,97},{33,1},{65,33},{97,65},{2,98}... | collective-permute-start | bytes 196616 | tf_op jit(solution)/shard_map/ppermute | solution.py:580
  91.3 4.2 %fetch_experts.1 = (bf16[3584,1024]{1,0:T(8,128)(2,1)S(1)}, bf16[512,3584]{1,0:T(8,128)(2,1)S(1)}) custom-call(bf16[128,256]{1,0:T(8,128)(2,1)S(1)} %get-tuple-element.50.after_ref.refs_0_, s32[1]{0:T(128)} %bitcast.15.half_ref, bf16[1,7168,256]{2,1,0:T(8,128)(2,1)} %gate_hbm.3, bf16[1,7168,256]{2,1,0:T(8,128)(2,1)} %up_hbm.3, ...), custom_call_target="tpu_custom_call" | custom-call | bytes 22020096 | tf_op jit(solution)/shard_map/fetch_experts/pallas_call | solution.py:413
  96.2 22.1 %all_to_all.32.y_ref = bf16[16,192,256]{2,1,0:T(8,128)(2,1)S(1)} all-to-all(bf16[16,192,256]{2,1,0:T(8,128)(2,1)S(1)} %slot_rows.1), channel_id=1, replica_groups=mesh['z'=4,'x'=4,'y'=4,'c'=2] {'x','y'}, dimensions={0} | all-to-all | bytes 3145728 | tf_op jit(solution)/shard_map/all_to_all | solution.py:583
  118.4 1.8 %gate_up.1 = (f32[192,1152]{1,0:T(8,128)S(1)}, bf16[192,1152]{1,0:T(8,128)(2,1)S(1)}) custom-call(bf16[16,192,256]{2,1,0:T(8,128)(2,1)S(1)} %all_to_all.32.y_ref, bf16[3584,1024]{1,0:T(8,128)(2,1)S(1)} %get-tuple-element.55.w_ref), custom_call_target="tpu_custom_call" | custom-call | tf_op jit(solution)/shard_map/gate_up/pallas_call | solution.py:444
  120.1 5.2 %collective-permute-start.7 = (bf16[192,1152]{1,0:T(8,128)(2,1)S(1)}, bf16[192,1152]{1,0:T(8,128)(2,1)S(1)}, u32[]{:S(2)}, u32[]{:S(2)}) collective-permute-start(bf16[192,1152]{1,0:T(8,128)(2,1)S(1)} %get-tuple-element.57), channel_id=1, source_target_pairs={{0,1},{1,0},{2,3},{3,2},{4,5},{5,4},{6,7},{7,6},{8,9},{9,8},{10,11... | collective-permute-start | bytes 1327112 | tf_op jit(solution)/shard_map/ppermute | solution.py:493
  125.3 1.4 collective-permute-done.7.got_ref
  126.7 1.7 down.1
  128.4 22.3 %all_to_all.33.out_ref = bf16[16,336,128]{2,1,0:T(8,128)(2,1)S(1)} all-to-all(bf16[16,336,128]{2,1,0:T(8,128)(2,1)S(1)} %down.1), channel_id=1, replica_groups=mesh['z'=4,'x'=4,'y'=4,'c'=2] {'x','y'}, dimensions={0} | all-to-all | bytes 2752512 | tf_op jit(solution)/shard_map/all_to_all | solution.py:587
  150.7 2.0 %combine_rows.1 = bf16[128,4,224]{2,1,0:T(4,128)(2,1)S(1)} custom-call(s32[1]{0:T(128)} %bitcast.16.plane_ref, bf16[16,336,128]{2,1,0:T(8,128)(2,1)S(1)} %all_to_all.33.out_ref, s32[512,8]{1,0:T(8,128)S(1)} %bitcast.51, f32[128,224]{1,0:T(8,128)S(1)} %get-tuple-element.60.hidden_ref), custom_call_target="tpu_custom_call" | custom-call | tf_op jit(solution)/shard_map/combine_rows/pallas_call | solution.py:333
  152.7 18.2 %all_to_all.34 = bf16[128,4,224]{2,1,0:T(4,128)(2,1)S(1)} all-to-all(bf16[128,4,224]{2,1,0:T(4,128)(2,1)S(1)} %combine_rows.1), channel_id=1, replica_groups=mesh['z'=4,'x'=4,'y'=4,'c'=2] {'z','x','y','c'}, dimensions={0} | all-to-all | bytes 458752 | tf_op jit(solution)/shard_map/all_to_all | solution.py:590
  (58 shorter events, 9.3 us)
Async XLA Ops:
  0.0 26.8 %copy-start = (bf16[7168,32]{0,1:T(8,128)(2,1)S(1)}, bf16[7168,32]{0,1:T(8,128)(2,1)}, u32[]{:S(2)}) copy-start(bf16[7168,32]{0,1:T(8,128)(2,1)} %param.25) | copy-start | bytes 1376260
  0.0 0.7 copy-start.3
  4.2 8.8 %copy-start.4 = (bf16[4,7168]{1,0:T(4,128)(2,1)S(1)}, bf16[4,7168]{1,0:T(4,128)(2,1)}, u32[]{:S(2)}) copy-start(bf16[4,7168]{1,0:T(4,128)(2,1)} %param.21) | copy-start | bytes 172036
  4.2 39.9 %all-to-all-start = ((bf16[32,288,128]{2,1,0:T(8,128)(2,1)}), bf16[32,288,128]{2,1,0:T(8,128)(2,1)S(1)}, u32[]{:S(2)}, u32[]{:S(2)}) async-start(bf16[32,288,128]{2,1,0:T(8,128)(2,1)} %spread.1), calls=%async_computation | async-start | bytes 4718592 | tf_op jit(solution)/shard_map/all_to_all | solution.py:522
  13.7 7.6 %copy-start.5 = (s32[512,8]{0,1:T(8,128)S(1)}, s32[512,8]{0,1:T(8,128)}, u32[]{:S(2)}) copy-start(s32[512,8]{0,1:T(8,128)} %param.26) | copy-start | bytes 49156
  13.7 8.8 %copy-start.6 = (s32[1,3]{1,0:T(1,128)S(1)}, s32[1,3]{1,0:T(1,128)}, u32[]{:S(2)}) copy-start(s32[1,3]{1,0:T(1,128)} %param.18) | copy-start | bytes 40
  13.7 8.9 %copy-start.2 = (bf16[4,576]{1,0:T(4,128)(2,1)S(1)}, bf16[4,576]{1,0:T(4,128)(2,1)}, u32[]{:S(2)}) copy-start(bf16[4,576]{1,0:T(4,128)(2,1)} %entry_ref.1) | copy-start | bytes 13828
  20.4 13.9 %collective-permute-start.2 = (bf16[256,3584]{1,0:T(8,128)(2,1)}, bf16[256,3584]{1,0:T(8,128)(2,1)}, u32[]{:S(2)}, u32[]{:S(2)}) collective-permute-start(bf16[256,3584]{1,0:T(8,128)(2,1)} %get-tuple-element.35), channel_id=1, source_target_pairs={{0,1},{1,0},{2,3},{3,2},{4,5},{5,4},{6,7},{7,6},{8,9},{9,8},{10,11... | collective-permute-start | bytes 5505032 | tf_op jit(solution)/shard_map/ppermute | solution.py:493
  20.7 23.3 %collective-permute-start.1 = (bf16[2,3584,256]{2,1,0:T(8,128)(2,1)}, bf16[2,3584,256]{2,1,0:T(8,128)(2,1)}, u32[]{:S(2)}, u32[]{:S(2)}) collective-permute-start(bf16[2,3584,256]{2,1,0:T(8,128)(2,1)} %get-tuple-element.34), channel_id=1, source_target_pairs={{0,1},{1,0},{2,3},{3,2},{4,5},{5,4},{6,7},{7,6},{8,9},{9,8},{10,11... | collective-permute-start | bytes 11010056 | tf_op jit(solution)/shard_map/ppermute | solution.py:493
  21.0 23.1 %collective-permute-start = (bf16[528,3584]{1,0:T(8,128)(2,1)}, bf16[528,3584]{1,0:T(8,128)(2,1)}, u32[]{:S(2)}, u32[]{:S(2)}) collective-permute-start(bf16[528,3584]{1,0:T(8,128)(2,1)} %get-tuple-element.33), channel_id=1, source_target_pairs={{0,1},{1,0},{2,3},{3,2},{4,5},{5,4},{6,7},{7,6},{8,9},{9,8},{10,11... | collective-permute-start | bytes 11354120 | tf_op jit(solution)/shard_map/ppermute | solution.py:493
  64.9 1.4 collective-permute-start.3
  86.8 8.8 %collective-permute-start.6 = (bf16[128,256]{1,0:T(8,128)(2,1)S(1)}, bf16[128,256]{1,0:T(8,128)(2,1)S(1)}, u32[]{:S(2)}, u32[]{:S(2)}) collective-permute-start(bf16[128,256]{1,0:T(8,128)(2,1)S(1)} %get-tuple-element.50.after_ref.refs_0_), channel_id=1, source_target_pairs={{0,96},{32,0},{64,32},{96,64},{1,97},{33,1},{65,33},{97,65},{2,98}... | collective-permute-start | bytes 196616 | tf_op jit(solution)/shard_map/ppermute | solution.py:580
  90.6 5.0 %collective-permute-start.5 = (bf16[128,256]{1,0:T(8,128)(2,1)S(1)}, bf16[128,256]{1,0:T(8,128)(2,1)S(1)}, u32[]{:S(2)}, u32[]{:S(2)}) collective-permute-start(bf16[128,256]{1,0:T(8,128)(2,1)S(1)} %get-tuple-element.50.after_ref.refs_0_), channel_id=1, source_target_pairs={{0,64},{32,96},{64,0},{96,32},{1,65},{33,97},{65,1},{97,33},{2,66}... | collective-permute-start | bytes 196616 | tf_op jit(solution)/shard_map/ppermute | solution.py:580
  90.6 5.0 %collective-permute-start.4 = (bf16[128,256]{1,0:T(8,128)(2,1)S(1)}, bf16[128,256]{1,0:T(8,128)(2,1)S(1)}, u32[]{:S(2)}, u32[]{:S(2)}) collective-permute-start(bf16[128,256]{1,0:T(8,128)(2,1)S(1)} %get-tuple-element.50.after_ref.refs_0_), channel_id=1, source_target_pairs={{0,32},{32,64},{64,96},{96,0},{1,33},{33,65},{65,97},{97,1},{2,34}... | collective-permute-start | bytes 196616 | tf_op jit(solution)/shard_map/ppermute | solution.py:580
  120.1 6.6 %collective-permute-start.7 = (bf16[192,1152]{1,0:T(8,128)(2,1)S(1)}, bf16[192,1152]{1,0:T(8,128)(2,1)S(1)}, u32[]{:S(2)}, u32[]{:S(2)}) collective-permute-start(bf16[192,1152]{1,0:T(8,128)(2,1)S(1)} %get-tuple-element.57), channel_id=1, source_target_pairs={{0,1},{1,0},{2,3},{3,2},{4,5},{5,4},{6,7},{7,6},{8,9},{9,8},{10,11... | collective-permute-start | bytes 1327112 | tf_op jit(solution)/shard_map/ppermute | solution.py:493
  126.7 45.1 %copy-start.1 = (bf16[7168,32]{0,1:T(8,128)(2,1)S(1)}, bf16[7168,32]{0,1:T(8,128)(2,1)}, u32[]{:S(2)}) copy-start(bf16[7168,32]{0,1:T(8,128)(2,1)} %param.25) | copy-start | bytes 1376260

commit v5 on v4

--- a/solution.py
+++ b/solution.py
@@ -18,6 +18,7 @@
 EXP_G = 8
 CHUNK = D // NDEV
 HALF = D // 2
+PARTS = 4
 LANES = 256
 GROUP = 4
 BLK = CHUNK * GROUP
@@ -84,18 +85,21 @@
     return jnp.concatenate([packed[:rows], rest], axis=1)
 
 
-def spread_kernel(owners_ref, cache_ref, out_ref, held_ref, packed_ref, in_sem, out_sem):
+def spread_kernel(owners_hbm, cache_ref, out_ref, owners_ref, held_ref, packed_ref, owner_sem, in_sem, out_sem):
+    owners_copy = pltpu.make_async_copy(owners_hbm, owners_ref, owner_sem)
+    owners_copy.start()
     batch = NDEV // in_sem.shape[0]
     tokens, half = cache_ref.shape[1], cache_ref.shape[1] // 2
     arrive = []
     for b in range(in_sem.shape[0]):
         at = pl.ds(b * batch, batch)
         arrive.append(pltpu.make_async_copy(cache_ref.at[at], held_ref.at[at], in_sem.at[b]))
+    start_all(arrive)
+    owners_copy.wait()
     leave = [
         pltpu.make_async_copy(packed_ref.at[p], out_ref.at[owners_ref[0, p]], out_sem.at[p])
         for p in range(NDEV)
     ]
-    start_all(arrive)
     for p in range(NDEV):
         if p % batch == 0:
             arrive[p // batch].wait()
@@ -112,36 +116,46 @@
     packed = (NDEV, cache.shape[1] * cache.shape[2] // 128, 128)
     return pl.pallas_call(
         spread_kernel,
-        in_specs=[SCALAR, ANYWHERE],
+        in_specs=[ANYWHERE, ANYWHERE],
         out_specs=ANYWHERE,
         scratch_shapes=[
+            pltpu.SMEM(owners.shape, owners.dtype),
             pltpu.VMEM(cache.shape, cache.dtype),
             pltpu.VMEM(packed, cache.dtype),
+            pltpu.SemaphoreType.DMA,
             pltpu.SemaphoreType.DMA((8,)),
             pltpu.SemaphoreType.DMA((NDEV,)),
         ],
         out_shape=pltpu.HBM(packed, cache.dtype),
         compiler_params=pltpu.CompilerParams(vmem_limit_bytes=SMALL),
         name="spread",
-    )(owners, in_hbm(cache))
+    )(in_hbm(owners), in_hbm(cache))
 
 
 def prompt_kernel(
     half_ref, query_hbm, cache_ref, entry_ref, old_hbm, uv_hbm, w_hbm, res_hbm, got_hbm,
-    out_ref, uv_ref, w_ref, all_ref, query_ref, sems,
+    out_ref, uv_ref, w_ref, old_ref, query_ref, sems,
 ):
     heads_all = query_hbm.shape[1]
     query_copy = pltpu.make_async_copy(query_hbm, query_ref, sems.at[0])
-    old_copy = pltpu.make_async_copy(old_hbm, all_ref.at[pl.ds(heads_all, old_hbm.shape[0]), :], sems.at[1])
+    old_copy = pltpu.make_async_copy(old_hbm, old_ref, sems.at[1])
     uv_copy = pltpu.make_async_copy(uv_hbm, uv_ref, sems.at[2])
     depth = w_hbm.shape[0]
     at = pl.ds(pl.multiple_of(half_ref[0] * HALF, 128), HALF)
-    w_copies = (
-        pltpu.make_async_copy(w_hbm.at[:, at], w_ref.at[pl.ds(0, depth), :], sems.at[3]),
-        pltpu.make_async_copy(res_hbm.at[:, at], w_ref.at[pl.ds(depth, 16), :], sems.at[4]),
-        pltpu.make_async_copy(got_hbm, w_ref.at[pl.ds(depth + 16, depth + 16), :], sems.at[5]),
-    )
-    start_all((query_copy, old_copy, uv_copy) + w_copies)
+    w_copies = [pltpu.make_async_copy(res_hbm.at[:, at], w_ref.at[pl.ds(depth, 16), :], sems.at[3])]
+    span = depth // PARTS
+    for n in range(PARTS):
+        rows = pl.ds(n * span, span)
+        w_copies.append(pltpu.make_async_copy(w_hbm.at[rows, at], w_ref.at[rows, :], sems.at[4 + n]))
+        span_got = span + 16 if n == PARTS - 1 else span
+        w_copies.append(
+            pltpu.make_async_copy(
+                got_hbm.at[pl.ds(n * span, span_got), :],
+                w_ref.at[pl.ds(depth + 16 + n * span, span_got), :],
+                sems.at[4 + PARTS + n],
+            )
+        )
+    start_all([query_copy, old_copy, uv_copy] + w_copies)
     scale_factor = (NOPE + ROPE) ** (-0.5)
     sources, tokens = cache_ref.shape[0], cache_ref.shape[1] * 128 // query_ref.shape[0]
     tiles = [cache_ref[:, j * tokens : (j + 1) * tokens, :].reshape(-1, 128) for j in range(LAT // 128)]
@@ -164,26 +178,27 @@
     exponent = jnp.exp(scores - maximum)
     own_exponent = jnp.exp(own_score - maximum)
     totals = jnp.sum(exponent, axis=0, keepdims=True) + own_exponent
-    weights = (exponent / totals).astype(BF16)
-    own_weight = (own_exponent / totals).astype(BF16)
+    inverse = 1.0 / totals
+    weights = (exponent * inverse).astype(BF16)
+    own_weight = (own_exponent * inverse).astype(BF16)
     over_rows = (((0,), (0,)), ((), ()))
     context = lax.dot_general(weights, cache, over_rows, preferred_element_type=F32)
     context = context + lax.dot_general(own_weight, entry[:, :LAT], over_rows, preferred_element_type=F32)
-    all_ref[:heads_all, :] = context.astype(BF16)
     rows, block = out_ref.shape[0], out_ref.shape[0] // NDEV
     heads = heads_all // NDEV
-    to = lax.broadcasted_iota(jnp.int32, (rows, rows), 0)
-    source = (to % block) // heads * heads_all + to // block * heads + to % heads
-    order = (lax.broadcasted_iota(jnp.int32, (rows, rows), 1) == source).astype(BF16)
+    to = lax.broadcasted_iota(jnp.int32, (rows, heads_all), 0)
+    source = jnp.where(to % block < heads, to // block * heads + to % block, -1)
+    order = (lax.broadcasted_iota(jnp.int32, (rows, heads_all), 1) == source).astype(BF16)
+    placed = jnp.dot(order, context.astype(BF16), preferred_element_type=F32)
     old_copy.wait()
-    out_ref[...] = jnp.dot(order, all_ref[...], preferred_element_type=F32).astype(BF16)
+    out_ref[...] = (placed + old_ref[...].astype(F32)).astype(BF16)
     uv_copy.wait()
     for copy in w_copies:
         copy.wait()
 
 
 def prompt_attention(half, query, cache, entry, old, w_uv, w_out, res, got):
-    rows = query.shape[1] + old.shape[0]
+    rows = old.shape[0]
     return pl.pallas_call(
         prompt_kernel,
         in_specs=[SCALAR, ANYWHERE, WHOLE, WHOLE] + [ANYWHERE] * 5,
@@ -194,7 +209,7 @@
         scratch_shapes=[
             pltpu.VMEM((rows, LAT), BF16),
             pltpu.VMEM(query.shape, BF16),
-            pltpu.SemaphoreType.DMA((6,)),
+            pltpu.SemaphoreType.DMA((4 + 2 * PARTS,)),
         ],
         compiler_params=pltpu.CompilerParams(vmem_limit_bytes=LARGE),
         name="prompt_attention",
@@ -489,6 +504,25 @@
     )(own, got, mine, w)
 
 
+def finish_kernel(total_ref, out_ref):
+    for c in range(NC):
+        for p in range(NXY):
+            row = sum(total_ref[z * NDEV + p * NC + c].astype(F32) for z in range(NZ))
+            at = (c * NXY + p) * CHUNK
+            out_ref[:, at : at + CHUNK] = row.astype(BF16)
+
+
+def finish(total):
+    return pl.pallas_call(
+        finish_kernel,
+        in_specs=[WHOLE],
+        out_specs=WHOLE,
+        out_shape=jax.ShapeDtypeStruct((total.shape[1], D), BF16),
+        compiler_params=pltpu.CompilerParams(vmem_limit_bytes=SMALL),
+        name="finish",
+    )(total)
+
+
 def swap_cores(values):
     return lax.ppermute(values, "c", [(0, 1), (1, 0)])
 
@@ -553,7 +587,8 @@
     cache_iota = jnp.arange(resident_cache.shape[1], dtype=jnp.int32)
     old_masks = cache_iota[None, :] < resident_len[0][:, None]
     context_old = jax.vmap(attend)(queries[1:], resident_cache, old_masks, new_latent[1:])
-    context_old = context_old.reshape(-1, LAT)
+    context_old = context_old.reshape(rows_dev - 1, NDEV, -1, LAT).transpose(1, 0, 2, 3)
+    context_old = jnp.pad(context_old, ((0, 0), (1, 0), (0, 0), (0, 0))).reshape(-1, LAT)
     held = (
         received, context_old, queries[0].T, step_ranks, owner_ranks, mine, group_ids, gain_chunk,
         router_chunk, place, res, own_half, plane_index, got_out, got_in, got_down,
@@ -588,8 +623,7 @@
 
     total = combine_rows(plane_index, out, owner_ranks, hidden, rows_dev)
     total = lax.all_to_all(total, ("z", "x", "y", "c"), 0, 0, tiled=True)
-    total = jnp.sum(total.reshape(NZ, NXY, NC, rows_dev, CHUNK).astype(F32), axis=0)
-    return total.transpose(2, 1, 0, 3).reshape(rows_dev, D).astype(BF16)
+    return finish(total)
 
 
 def solution(mesh):

time: 173 us -> 171 us (0.988)
  local copies, waits for them, and re-layouts: 4.88 us -> 9.94 us
  waiting for transfers between devices: 12.6 us -> 9.06 us
  matrix products: 7.8 us -> 5.82 us
    all_to_all x1, waiting for transfers between devices: 9.79 us -> 6.25 us  [per_device(): lax.all_to_all(spread(assignment, prompt_cache), ('x', 'y', 'c'), 0, 0, t...]
    reshape x0 -> x3, local copies, waits for them, and re-layouts: none -> 3.19 us  [the longest x1 1.96 us: per_device(): jnp.pad(context_old, ((0, 0), (1, 0), (0, 0), (0, 0))).reshape(-1, LAT)]
    pallas_call x1 -> x2, Pallas kernels: 3.45 us -> 3.72 us  [the longest x1 2.99 us: spread(): pl.pallas_call(spread_kernel, in_specs=[ANYWHERE, ANYWHERE], out_specs=AN...]
  transfers between devices with their start and end apart: 9 -> 9, of which waited for: 4 -> 3; matrix products, arithmetic and copies ran while one was open for 8% -> 10% of each run, Pallas kernels for 6% -> 6%
where the time goes in v5:
time: 171 us; the launch traced here: 170 us
  blocking collectives  95.3 us (56%)
  Pallas kernels  29 us (17%)
  starting transfers between devices  19.5 us (11%)
  local copies, waits for them, and re-layouts  9.94 us (6%)
  waiting for transfers between devices  9.06 us (5%)
  matrix products  5.82 us (3%)
    all_to_all x1, blocking collectives, per_device(): out = lax.all_to_all(out, ('x', 'y'), 0, 0, tiled=True)  22.3 us
    all_to_all x1, blocking collectives, per_device(): slotted = lax.all_to_all(slotted, ('x', 'y'), 0, 0, tiled=True)  22.1 us
    all_to_all x1, blocking collectives, per_device(): total = lax.all_to_all(total, ('z', 'x', 'y', 'c'), 0, 0, tiled=True)  18.1 us
    all_to_all x1, blocking collectives, per_device(): partial = lax.all_to_all(partial, ('x', 'y'), 0, 0, tiled=True)  17.5 us
    all_to_all x1, blocking collectives, per_device(): lax.all_to_all(context.reshape(NDEV, -1, LAT), ('x', 'y', 'c'), 0, 0, til...  15.3 us
    all_to_all x1, starting transfers between devices, per_device(): lax.all_to_all(spread(assignment, prompt_cache), ('x', 'y', 'c'), 0, 0, t...  8.73 us
    pallas_call x1, Pallas kernels, give_weights(): pl.pallas_call(give_kernel, in_specs=[SCALAR] + [ANYWHERE] * 5, out_specs...  6.75 us
    all_to_all x1, waiting for transfers between devices, per_device(): lax.all_to_all(spread(assignment, prompt_cache), ('x', 'y', 'c'), 0, 0, t...  6.25 us
  transfers between devices with their start and end apart: 9, of which 3 were waited for; matrix products, arithmetic and copies ran while one was open for 10% of the time, Pallas kernels for 6%

profile of v5, /device:TPU:1, one launch (start us, length us, event | category | flops | bytes accessed | tf_op | source)
XLA Modules:
  0.0 170.2 jit_solution(8767073051254161493)
XLA Ops:
  0.0 3.0 %spread.1 = bf16[32,288,128]{2,1,0:T(8,128)(2,1)} custom-call(s32[1,32]{1,0:T(1,128)} %owners_hbm.1, bf16[32,64,576]{2,1,0:T(8,128)(2,1)} %cache_ref.1), custom_call_target="tpu_custom_call" | custom-call | tf_op jit(solution)/shard_map/spread/pallas_call | solution.py:117
  3.0 8.7 %all-to-all-start = ((bf16[32,288,128]{2,1,0:T(8,128)(2,1)}), bf16[32,288,128]{2,1,0:T(8,128)(2,1)S(1)}, u32[]{:S(2)}, u32[]{:S(2)}) async-start(bf16[32,288,128]{2,1,0:T(8,128)(2,1)} %spread.1), calls=%async_computation | async-start | bytes 4718592 | tf_op jit(solution)/shard_map/all_to_all | solution.py:556
  12.5 6.8 %give_weights.1 = (bf16[528,3584]{1,0:T(8,128)(2,1)}, bf16[2,3584,256]{2,1,0:T(8,128)(2,1)}, bf16[256,3584]{1,0:T(8,128)(2,1)}) custom-call(s32[1]{0:T(128)S(6)} %sub.49.half_ref, bf16[512,7168]{1,0:T(8,128)(2,1)} %w_hbm.1, bf16[16,7168]{1,0:T(8,128)(2,1)} %pad.9.res_hbm, bf16[1,7168,256]{2,1,0:T(8,128)(2,1)} %gate_hbm.3, bf16[1,7168,256]{2,1,0:T(8,128)(2,1)} %up_hbm.3, ...), custom_call_target="tpu_custom_call" | custom-call | tf_op jit(solution)/shard_map/give_weights/pallas_call | solution.py:386
  20.4 2.1 %fusion.26 = (f32[3,128]{1,0:T(4,128)S(1)}, f32[3,128,512]{2,1,0:T(8,128)S(1)}) fusion(bf16[4,128,576]{1,2,0:T(8,128)(2,1)S(1)} %copy-done.3, bf16[3,512,576]{1,2,0:T(8,128)(2,1)} %param.17, pred[3,512]{1,0:T(4,128)(4,1)S(1)} %iota_compare_fusion.6), kind=kOutput, calls=%fused_computation.54 | convolution fusion | flops 227081856 | bytes 3148800 | tf_op jit(solution)/shard_map/vmap(hc,kc->hk)/dot_general | solution.py:55
  24.2 3.1 %fusion.6 = bf16[3,128,512]{2,1,0:T(8,128)(2,1)} fusion(bf16[3,512,576]{1,2,0:T(8,128)(2,1)} %param.17, f32[3,128,512]{2,1,0:T(8,128)} %copy-done.4, f32[3,512]{1,0:T(4,128)S(1)} %slice_convert_fusion, f32[3,128]{1,0:T(4,128)S(1)} %get-tuple-element.62, f32[3,128]{1,0:T(4,128)S(1)} %get-tuple-element.61, f32[3,128]{1,0:T(4,128)S(1)} %fusion.21), kind=kOutput, calls=%fused_computation.6 | convolution fusion | flops 202506240 | bytes 2763264 | tf_op jit(solution)/shard_map/vmap(hk,kl->hl)/dot_general | solution.py:65
  30.0 2.0 %reshape.134.old_hbm = bf16[512,512]{1,0:T(8,128)(2,1)} reshape(bf16[32,4,4,512]{3,2,1,0:T(4,128)(2,1)} %pad.8) | data formatting | bytes 1048576 | tf_op jit(solution)/shard_map/reshape | solution.py:591
  35.1 1.6 slice_bitcast_fusion.query_hbm
  36.6 6.2 %all-to-all-done.cache_ref = bf16[32,288,128]{2,1,0:T(8,128)(2,1)S(1)} async-done(((bf16[32,288,128]{2,1,0:T(8,128)(2,1)}), bf16[32,288,128]{2,1,0:T(8,128)(2,1)S(1)}, u32[]{:S(2)}, u32[]{:S(2)}) %all-to-all-start) | async-done | bytes 2359328 | tf_op jit(solution)/shard_map/all_to_all | solution.py:556
  42.9 3.7 %prompt_attention.1 = (bf16[512,512]{1,0:T(8,128)(2,1)S(1)}, bf16[4,512,128]{2,1,0:T(8,128)(2,1)S(1)}, bf16[1056,3584]{1,0:T(8,128)(2,1)S(1)}) custom-call(s32[1]{0:T(128)} %bitcast.15.half_ref, bf16[576,128]{1,0:T(8,128)(2,1)} %slice_bitcast_fusion.query_hbm, bf16[32,288,128]{2,1,0:T(8,128)(2,1)S(1)} %all-to-all-done.cache_ref, ...), custom_call_target="tpu_custom_call" | custom-call | tf_op jit(solution)/shard_map/prompt_attention/pallas_call | solution.py:202
  46.6 15.3 %all_to_all.30 = bf16[32,16,512]{2,1,0:T(8,128)(2,1)S(1)} all-to-all(bf16[32,16,512]{2,1,0:T(8,128)(2,1)S(1)} %bitcast.50), channel_id=1, replica_groups=mesh['z'=4,'x'=4,'y'=4,'c'=2] {'x','y','c'}, dimensions={0} | all-to-all | bytes 1048576 | tf_op jit(solution)/shard_map/all_to_all | solution.py:604
  61.8 1.7 head_values.1.own_ref
  63.6 1.3 collective-permute-done.3.got_ref
  65.0 2.0 %project.1 = bf16[16,224,128]{2,1,0:T(8,128)(2,1)S(1)} custom-call(bf16[128,512]{1,0:T(8,128)(2,1)S(1)} %head_values.1.own_ref, bf16[128,512]{1,0:T(8,128)(2,1)S(1)} %collective-permute-done.3.got_ref, bf16[2,128,16]{2,1,0:T(8,128)(2,1)S(1)} %fusion.17.place_ref, bf16[1056,3584]{1,0:T(8,128)(2,1)S(1)} %get-tuple-element.46.w_ref), custom_call_target="tpu_custom_call" | custom-call | tf_op jit(solution)/shard_map/project/pallas_call | solution.py:258
  67.0 17.5 %all_to_all.31.part_ref = bf16[16,224,128]{2,1,0:T(8,128)(2,1)S(1)} all-to-all(bf16[16,224,128]{2,1,0:T(8,128)(2,1)S(1)} %project.1), channel_id=1, replica_groups=mesh['z'=4,'x'=4,'y'=4,'c'=2] {'x','y'}, dimensions={0} | all-to-all | bytes 1835008 | tf_op jit(solution)/shard_map/all_to_all | solution.py:609
  85.4 3.8 %collective-permute-start.6 = (bf16[128,256]{1,0:T(8,128)(2,1)S(1)}, bf16[128,256]{1,0:T(8,128)(2,1)S(1)}, u32[]{:S(2)}, u32[]{:S(2)}) collective-permute-start(bf16[128,256]{1,0:T(8,128)(2,1)S(1)} %get-tuple-element.50.after_ref.refs_0_), channel_id=1, source_target_pairs={{0,96},{32,0},{64,32},{96,64},{1,97},{33,1},{65,33},{97,65},{2,98}... | collective-permute-start | bytes 196616 | tf_op jit(solution)/shard_map/ppermute | solution.py:615
  90.1 4.2 %fetch_experts.1 = (bf16[3584,1024]{1,0:T(8,128)(2,1)S(1)}, bf16[512,3584]{1,0:T(8,128)(2,1)S(1)}) custom-call(bf16[128,256]{1,0:T(8,128)(2,1)S(1)} %get-tuple-element.50.after_ref.refs_0_, s32[1]{0:T(128)} %bitcast.15.half_ref, bf16[1,7168,256]{2,1,0:T(8,128)(2,1)} %gate_hbm.3, bf16[1,7168,256]{2,1,0:T(8,128)(2,1)} %up_hbm.3, ...), custom_call_target="tpu_custom_call" | custom-call | bytes 22020096 | tf_op jit(solution)/shard_map/fetch_experts/pallas_call | solution.py:428
  95.0 22.1 %all_to_all.32.y_ref = bf16[16,192,256]{2,1,0:T(8,128)(2,1)S(1)} all-to-all(bf16[16,192,256]{2,1,0:T(8,128)(2,1)S(1)} %slot_rows.1), channel_id=1, replica_groups=mesh['z'=4,'x'=4,'y'=4,'c'=2] {'x','y'}, dimensions={0} | all-to-all | bytes 3145728 | tf_op jit(solution)/shard_map/all_to_all | solution.py:618
  117.1 1.8 %gate_up.1 = (f32[192,1152]{1,0:T(8,128)S(1)}, bf16[192,1152]{1,0:T(8,128)(2,1)S(1)}) custom-call(bf16[16,192,256]{2,1,0:T(8,128)(2,1)S(1)} %all_to_all.32.y_ref, bf16[3584,1024]{1,0:T(8,128)(2,1)S(1)} %get-tuple-element.55.w_ref), custom_call_target="tpu_custom_call" | custom-call | tf_op jit(solution)/shard_map/gate_up/pallas_call | solution.py:459
  118.9 5.2 %collective-permute-start.7 = (bf16[192,1152]{1,0:T(8,128)(2,1)S(1)}, bf16[192,1152]{1,0:T(8,128)(2,1)S(1)}, u32[]{:S(2)}, u32[]{:S(2)}) collective-permute-start(bf16[192,1152]{1,0:T(8,128)(2,1)S(1)} %get-tuple-element.57), channel_id=1, source_target_pairs={{0,1},{1,0},{2,3},{3,2},{4,5},{5,4},{6,7},{7,6},{8,9},{9,8},{10,11... | collective-permute-start | bytes 1327112 | tf_op jit(solution)/shard_map/ppermute | solution.py:527
  124.1 1.4 collective-permute-done.7.got_ref
  125.5 1.7 down.1
  127.2 22.3 %all_to_all.33.out_ref = bf16[16,336,128]{2,1,0:T(8,128)(2,1)S(1)} all-to-all(bf16[16,336,128]{2,1,0:T(8,128)(2,1)S(1)} %down.1), channel_id=1, replica_groups=mesh['z'=4,'x'=4,'y'=4,'c'=2] {'x','y'}, dimensions={0} | all-to-all | bytes 2752512 | tf_op jit(solution)/shard_map/all_to_all | solution.py:622
  149.4 2.0 %combine_rows.1 = bf16[128,4,224]{2,1,0:T(4,128)(2,1)S(1)} custom-call(s32[1]{0:T(128)} %bitcast.16.plane_ref, bf16[16,336,128]{2,1,0:T(8,128)(2,1)S(1)} %all_to_all.33.out_ref, s32[512,8]{1,0:T(8,128)S(1)} %bitcast.49, f32[128,224]{1,0:T(8,128)S(1)} %get-tuple-element.60.hidden_ref), custom_call_target="tpu_custom_call" | custom-call | tf_op jit(solution)/shard_map/combine_rows/pallas_call | solution.py:348
  151.5 18.1 %all_to_all.34.total_ref = bf16[128,4,224]{2,1,0:T(4,128)(2,1)S(1)} all-to-all(bf16[128,4,224]{2,1,0:T(4,128)(2,1)S(1)} %combine_rows.1), channel_id=1, replica_groups=mesh['z'=4,'x'=4,'y'=4,'c'=2] {'z','x','y','c'}, dimensions={0} | all-to-all | bytes 458752 | tf_op jit(solution)/shard_map/all_to_all | solution.py:625
  (64 shorter events, 12.4 us)
Async XLA Ops:
  0.0 24.0 %copy-start = (bf16[7168,32]{0,1:T(8,128)(2,1)S(1)}, bf16[7168,32]{0,1:T(8,128)(2,1)}, u32[]{:S(2)}) copy-start(bf16[7168,32]{0,1:T(8,128)(2,1)} %param.25) | copy-start | bytes 1376260
  3.0 8.8 %copy-start.5 = (bf16[4,7168]{1,0:T(4,128)(2,1)S(1)}, bf16[4,7168]{1,0:T(4,128)(2,1)}, u32[]{:S(2)}) copy-start(bf16[4,7168]{1,0:T(4,128)(2,1)} %param.21) | copy-start | bytes 172036
  3.0 39.9 %all-to-all-start = ((bf16[32,288,128]{2,1,0:T(8,128)(2,1)}), bf16[32,288,128]{2,1,0:T(8,128)(2,1)S(1)}, u32[]{:S(2)}, u32[]{:S(2)}) async-start(bf16[32,288,128]{2,1,0:T(8,128)(2,1)} %spread.1), calls=%async_computation | async-start | bytes 4718592 | tf_op jit(solution)/shard_map/all_to_all | solution.py:556
  12.5 7.6 %copy-start.8 = (s32[1,3]{1,0:T(1,128)S(1)}, s32[1,3]{1,0:T(1,128)}, u32[]{:S(2)}) copy-start(s32[1,3]{1,0:T(1,128)} %param.18) | copy-start | bytes 40
  12.5 7.7 %copy-start.2 = (bf16[4,576]{1,0:T(4,128)(2,1)S(1)}, bf16[4,576]{1,0:T(4,128)(2,1)}, u32[]{:S(2)}) copy-start(bf16[4,576]{1,0:T(4,128)(2,1)} %entry_ref.1) | copy-start | bytes 13828
  12.5 7.7 %copy-start.3 = (bf16[4,128,576]{1,2,0:T(8,128)(2,1)S(1)}, bf16[4,128,576]{1,2,0:T(8,128)(2,1)}, u32[]{:S(2)}) copy-start(bf16[4,128,576]{1,2,0:T(8,128)(2,1)} %param.19) | copy-start | bytes 1769476
  12.5 7.9 %copy-start.6 = (s32[512,8]{0,1:T(8,128)S(1)}, s32[512,8]{0,1:T(8,128)}, u32[]{:S(2)}) copy-start(s32[512,8]{0,1:T(8,128)} %param.26) | copy-start | bytes 49156
  19.3 17.4 %collective-permute-start.2 = (bf16[256,3584]{1,0:T(8,128)(2,1)}, bf16[256,3584]{1,0:T(8,128)(2,1)}, u32[]{:S(2)}, u32[]{:S(2)}) collective-permute-start(bf16[256,3584]{1,0:T(8,128)(2,1)} %get-tuple-element.35), channel_id=1, source_target_pairs={{0,1},{1,0},{2,3},{3,2},{4,5},{5,4},{6,7},{7,6},{8,9},{9,8},{10,11... | collective-permute-start | bytes 5505032 | tf_op jit(solution)/shard_map/ppermute | solution.py:527
  19.6 23.3 %collective-permute-start.1 = (bf16[2,3584,256]{2,1,0:T(8,128)(2,1)}, bf16[2,3584,256]{2,1,0:T(8,128)(2,1)}, u32[]{:S(2)}, u32[]{:S(2)}) collective-permute-start(bf16[2,3584,256]{2,1,0:T(8,128)(2,1)} %get-tuple-element.34), channel_id=1, source_target_pairs={{0,1},{1,0},{2,3},{3,2},{4,5},{5,4},{6,7},{7,6},{8,9},{9,8},{10,11... | collective-permute-start | bytes 11010056 | tf_op jit(solution)/shard_map/ppermute | solution.py:527
  19.8 23.0 %collective-permute-start = (bf16[528,3584]{1,0:T(8,128)(2,1)}, bf16[528,3584]{1,0:T(8,128)(2,1)}, u32[]{:S(2)}, u32[]{:S(2)}) collective-permute-start(bf16[528,3584]{1,0:T(8,128)(2,1)} %get-tuple-element.33), channel_id=1, source_target_pairs={{0,1},{1,0},{2,3},{3,2},{4,5},{5,4},{6,7},{7,6},{8,9},{9,8},{10,11... | collective-permute-start | bytes 11354120 | tf_op jit(solution)/shard_map/ppermute | solution.py:527
  22.6 0.9 copy-start.4
  24.1 3.4 %copy-start.7 = (s32[512,32]{0,1:T(8,128)}, s32[512,32]{0,1:T(8,128)S(1)}, u32[]{:S(2)}) copy-start(s32[512,32]{0,1:T(8,128)S(1)} %fusion.9) | copy-start | bytes 196612
  63.5 1.4 collective-permute-start.3
  85.4 8.9 %collective-permute-start.6 = (bf16[128,256]{1,0:T(8,128)(2,1)S(1)}, bf16[128,256]{1,0:T(8,128)(2,1)S(1)}, u32[]{:S(2)}, u32[]{:S(2)}) collective-permute-start(bf16[128,256]{1,0:T(8,128)(2,1)S(1)} %get-tuple-element.50.after_ref.refs_0_), channel_id=1, source_target_pairs={{0,96},{32,0},{64,32},{96,64},{1,97},{33,1},{65,33},{97,65},{2,98}... | collective-permute-start | bytes 196616 | tf_op jit(solution)/shard_map/ppermute | solution.py:615
  89.2 5.1 %collective-permute-start.5 = (bf16[128,256]{1,0:T(8,128)(2,1)S(1)}, bf16[128,256]{1,0:T(8,128)(2,1)S(1)}, u32[]{:S(2)}, u32[]{:S(2)}) collective-permute-start(bf16[128,256]{1,0:T(8,128)(2,1)S(1)} %get-tuple-element.50.after_ref.refs_0_), channel_id=1, source_target_pairs={{0,64},{32,96},{64,0},{96,32},{1,65},{33,97},{65,1},{97,33},{2,66}... | collective-permute-start | bytes 196616 | tf_op jit(solution)/shard_map/ppermute | solution.py:615
  89.4 5.0 %collective-permute-start.4 = (bf16[128,256]{1,0:T(8,128)(2,1)S(1)}, bf16[128,256]{1,0:T(8,128)(2,1)S(1)}, u32[]{:S(2)}, u32[]{:S(2)}) collective-permute-start(bf16[128,256]{1,0:T(8,128)(2,1)S(1)} %get-tuple-element.50.after_ref.refs_0_), channel_id=1, source_target_pairs={{0,32},{32,64},{64,96},{96,0},{1,33},{33,65},{65,97},{97,1},{2,34}... | collective-permute-start | bytes 196616 | tf_op jit(solution)/shard_map/ppermute | solution.py:615
  118.9 6.6 %collective-permute-start.7 = (bf16[192,1152]{1,0:T(8,128)(2,1)S(1)}, bf16[192,1152]{1,0:T(8,128)(2,1)S(1)}, u32[]{:S(2)}, u32[]{:S(2)}) collective-permute-start(bf16[192,1152]{1,0:T(8,128)(2,1)S(1)} %get-tuple-element.57), channel_id=1, source_target_pairs={{0,1},{1,0},{2,3},{3,2},{4,5},{5,4},{6,7},{7,6},{8,9},{9,8},{10,11... | collective-permute-start | bytes 1327112 | tf_op jit(solution)/shard_map/ppermute | solution.py:527
  125.5 44.8 %copy-start.1 = (bf16[7168,32]{0,1:T(8,128)(2,1)S(1)}, bf16[7168,32]{0,1:T(8,128)(2,1)}, u32[]{:S(2)}) copy-start(bf16[7168,32]{0,1:T(8,128)(2,1)} %param.25) | copy-start | bytes 1376260

commit v6 on v5

--- a/solution.py
+++ b/solution.py
@@ -221,12 +221,15 @@
     context = context_ref[...]
     pick = lax.broadcasted_iota(jnp.int32, (ROWS, rows), 1) // heads
     pick = (pick == lax.broadcasted_iota(jnp.int32, (ROWS, rows), 0)).astype(BF16)
-    head = lax.broadcasted_iota(jnp.int32, (rows, uv_ref.shape[2]), 0) % heads
-    for h in range(heads):
-        values = jnp.dot(context, uv_ref[h], preferred_element_type=F32)
-        values = jnp.where(head == h, values, 0.0).astype(BF16)
+    width = uv_ref.shape[2]
+    row_head = lax.broadcasted_iota(jnp.int32, (rows, 2 * width), 0) % heads
+    lane_head = lax.broadcasted_iota(jnp.int32, (rows, 2 * width), 1) // width
+    for h in range(0, heads, 2):
+        values = jnp.concatenate([uv_ref[h], uv_ref[h + 1]], axis=1)
+        values = jnp.dot(context, values, preferred_element_type=F32)
+        values = jnp.where(row_head == lane_head + h, values, 0.0).astype(BF16)
         values = jnp.dot(pick, values, preferred_element_type=F32).astype(BF16)
-        attn_ref[:, h * values.shape[1] : (h + 1) * values.shape[1]] = values
+        attn_ref[:, h * width : (h + 2) * width] = values
 
 
 def head_values(context, w_uv):
@@ -331,8 +334,8 @@
     acc = jnp.zeros((ALL_ROWS, CHUNK), F32)
     for e in range(EXP_G):
         table = (ranks_ref[:, e : e + 1] == slot).astype(BF16)
-        for source in (2 * e, 2 * e + 1):
-            acc = acc + jnp.dot(table, unpack_chunk(out_ref[source]), preferred_element_type=F32)
+        both = out_ref[2 * e].astype(F32) + out_ref[2 * e + 1].astype(F32)
+        acc = acc + jnp.dot(table, unpack_chunk(both.astype(BF16)), preferred_element_type=F32)
     acc_ref[...] = acc
     span, count = rows_ref.shape[0], rows_ref.shape[1]
     own = ROWS // count

time: 171 us -> 170 us (level)
  transfers between devices with their start and end apart: 9 -> 9, of which waited for: 3 -> 4; matrix products, arithmetic and copies ran while one was open for 10% -> 10% of each run, Pallas kernels for 6% -> 7%
where the time goes in v6:
time: 170 us; the launch traced here: 169 us
  blocking collectives  95.4 us (56%)
  Pallas kernels  27.8 us (16%)
  starting transfers between devices  19.4 us (11%)
  local copies, waits for them, and re-layouts  9.94 us (6%)
  waiting for transfers between devices  9.06 us (5%)
  matrix products  5.82 us (3%)
    all_to_all x1, blocking collectives, per_device(): out = lax.all_to_all(out, ('x', 'y'), 0, 0, tiled=True)  22.3 us
    all_to_all x1, blocking collectives, per_device(): slotted = lax.all_to_all(slotted, ('x', 'y'), 0, 0, tiled=True)  22.1 us
    all_to_all x1, blocking collectives, per_device(): total = lax.all_to_all(total, ('z', 'x', 'y', 'c'), 0, 0, tiled=True)  18.2 us
    all_to_all x1, blocking collectives, per_device(): partial = lax.all_to_all(partial, ('x', 'y'), 0, 0, tiled=True)  17.6 us
    all_to_all x1, blocking collectives, per_device(): lax.all_to_all(context.reshape(NDEV, -1, LAT), ('x', 'y', 'c'), 0, 0, til...  15.3 us
    all_to_all x1, starting transfers between devices, per_device(): lax.all_to_all(spread(assignment, prompt_cache), ('x', 'y', 'c'), 0, 0, t...  8.73 us
    pallas_call x1, Pallas kernels, give_weights(): pl.pallas_call(give_kernel, in_specs=[SCALAR] + [ANYWHERE] * 5, out_specs...  6.75 us
    all_to_all x1, waiting for transfers between devices, per_device(): lax.all_to_all(spread(assignment, prompt_cache), ('x', 'y', 'c'), 0, 0, t...  6.25 us
  transfers between devices with their start and end apart: 9, of which 4 were waited for; matrix products, arithmetic and copies ran while one was open for 10% of the time, Pallas kernels for 7%

profile of v6, /device:TPU:1, one launch (start us, length us, event | category | flops | bytes accessed | tf_op | source)
XLA Modules:
  0.0 169.1 jit_solution(10851197259724344669)
XLA Ops:
  0.0 3.0 %spread.1 = bf16[32,288,128]{2,1,0:T(8,128)(2,1)} custom-call(s32[1,32]{1,0:T(1,128)} %owners_hbm.1, bf16[32,64,576]{2,1,0:T(8,128)(2,1)} %cache_ref.1), custom_call_target="tpu_custom_call" | custom-call | tf_op jit(solution)/shard_map/spread/pallas_call | solution.py:117
  3.0 8.7 %all-to-all-start = ((bf16[32,288,128]{2,1,0:T(8,128)(2,1)}), bf16[32,288,128]{2,1,0:T(8,128)(2,1)S(1)}, u32[]{:S(2)}, u32[]{:S(2)}) async-start(bf16[32,288,128]{2,1,0:T(8,128)(2,1)} %spread.1), calls=%async_computation | async-start | bytes 4718592 | tf_op jit(solution)/shard_map/all_to_all | solution.py:559
  12.5 6.8 %give_weights.1 = (bf16[528,3584]{1,0:T(8,128)(2,1)}, bf16[2,3584,256]{2,1,0:T(8,128)(2,1)}, bf16[256,3584]{1,0:T(8,128)(2,1)}) custom-call(s32[1]{0:T(128)S(6)} %sub.49.half_ref, bf16[512,7168]{1,0:T(8,128)(2,1)} %w_hbm.1, bf16[16,7168]{1,0:T(8,128)(2,1)} %pad.9.res_hbm, bf16[1,7168,256]{2,1,0:T(8,128)(2,1)} %gate_hbm.3, bf16[1,7168,256]{2,1,0:T(8,128)(2,1)} %up_hbm.3, ...), custom_call_target="tpu_custom_call" | custom-call | tf_op jit(solution)/shard_map/give_weights/pallas_call | solution.py:389
  20.4 2.1 %fusion.26 = (f32[3,128]{1,0:T(4,128)S(1)}, f32[3,128,512]{2,1,0:T(8,128)S(1)}) fusion(bf16[4,128,576]{1,2,0:T(8,128)(2,1)S(1)} %copy-done.3, bf16[3,512,576]{1,2,0:T(8,128)(2,1)} %param.17, pred[3,512]{1,0:T(4,128)(4,1)S(1)} %iota_compare_fusion.6), kind=kOutput, calls=%fused_computation.54 | convolution fusion | flops 227081856 | bytes 3148800 | tf_op jit(solution)/shard_map/vmap(hc,kc->hk)/dot_general | solution.py:55
  24.1 3.1 %fusion.6 = bf16[3,128,512]{2,1,0:T(8,128)(2,1)} fusion(bf16[3,512,576]{1,2,0:T(8,128)(2,1)} %param.17, f32[3,128,512]{2,1,0:T(8,128)} %copy-done.4, f32[3,512]{1,0:T(4,128)S(1)} %slice_convert_fusion, f32[3,128]{1,0:T(4,128)S(1)} %get-tuple-element.62, f32[3,128]{1,0:T(4,128)S(1)} %get-tuple-element.61, f32[3,128]{1,0:T(4,128)S(1)} %fusion.21), kind=kOutput, calls=%fused_computation.6 | convolution fusion | flops 202506240 | bytes 2763264 | tf_op jit(solution)/shard_map/vmap(hk,kl->hl)/dot_general | solution.py:65
  27.6 1.1 reshape.133
  29.9 2.0 %reshape.134.old_hbm = bf16[512,512]{1,0:T(8,128)(2,1)} reshape(bf16[32,4,4,512]{3,2,1,0:T(4,128)(2,1)} %pad.8) | data formatting | bytes 1048576 | tf_op jit(solution)/shard_map/reshape | solution.py:594
  35.0 1.6 slice_bitcast_fusion.query_hbm
  36.6 6.2 %all-to-all-done.cache_ref = bf16[32,288,128]{2,1,0:T(8,128)(2,1)S(1)} async-done(((bf16[32,288,128]{2,1,0:T(8,128)(2,1)}), bf16[32,288,128]{2,1,0:T(8,128)(2,1)S(1)}, u32[]{:S(2)}, u32[]{:S(2)}) %all-to-all-start) | async-done | bytes 2359328 | tf_op jit(solution)/shard_map/all_to_all | solution.py:559
  42.9 3.7 %prompt_attention.1 = (bf16[512,512]{1,0:T(8,128)(2,1)S(1)}, bf16[4,512,128]{2,1,0:T(8,128)(2,1)S(1)}, bf16[1056,3584]{1,0:T(8,128)(2,1)S(1)}) custom-call(s32[1]{0:T(128)} %bitcast.15.half_ref, bf16[576,128]{1,0:T(8,128)(2,1)} %slice_bitcast_fusion.query_hbm, bf16[32,288,128]{2,1,0:T(8,128)(2,1)S(1)} %all-to-all-done.cache_ref, ...), custom_call_target="tpu_custom_call" | custom-call | tf_op jit(solution)/shard_map/prompt_attention/pallas_call | solution.py:202
  46.5 15.3 %all_to_all.30 = bf16[32,16,512]{2,1,0:T(8,128)(2,1)S(1)} all-to-all(bf16[32,16,512]{2,1,0:T(8,128)(2,1)S(1)} %bitcast.50), channel_id=1, replica_groups=mesh['z'=4,'x'=4,'y'=4,'c'=2] {'x','y','c'}, dimensions={0} | all-to-all | bytes 1048576 | tf_op jit(solution)/shard_map/all_to_all | solution.py:607
  62.9 1.3 collective-permute-done.3.got_ref
  64.2 2.0 %project.1 = bf16[16,224,128]{2,1,0:T(8,128)(2,1)S(1)} custom-call(bf16[128,512]{1,0:T(8,128)(2,1)S(1)} %head_values.1.own_ref, bf16[128,512]{1,0:T(8,128)(2,1)S(1)} %collective-permute-done.3.got_ref, bf16[2,128,16]{2,1,0:T(8,128)(2,1)S(1)} %fusion.17.place_ref, bf16[1056,3584]{1,0:T(8,128)(2,1)S(1)} %get-tuple-element.46.w_ref), custom_call_target="tpu_custom_call" | custom-call | tf_op jit(solution)/shard_map/project/pallas_call | solution.py:261
  66.2 17.6 %all_to_all.31.part_ref = bf16[16,224,128]{2,1,0:T(8,128)(2,1)S(1)} all-to-all(bf16[16,224,128]{2,1,0:T(8,128)(2,1)S(1)} %project.1), channel_id=1, replica_groups=mesh['z'=4,'x'=4,'y'=4,'c'=2] {'x','y'}, dimensions={0} | all-to-all | bytes 1835008 | tf_op jit(solution)/shard_map/all_to_all | solution.py:612
  84.7 3.8 %collective-permute-start.6 = (bf16[128,256]{1,0:T(8,128)(2,1)S(1)}, bf16[128,256]{1,0:T(8,128)(2,1)S(1)}, u32[]{:S(2)}, u32[]{:S(2)}) collective-permute-start(bf16[128,256]{1,0:T(8,128)(2,1)S(1)} %get-tuple-element.50.after_ref.refs_0_), channel_id=1, source_target_pairs={{0,96},{32,0},{64,32},{96,64},{1,97},{33,1},{65,33},{97,65},{2,98}... | collective-permute-start | bytes 196616 | tf_op jit(solution)/shard_map/ppermute | solution.py:618
  89.2 4.2 %fetch_experts.1 = (bf16[3584,1024]{1,0:T(8,128)(2,1)S(1)}, bf16[512,3584]{1,0:T(8,128)(2,1)S(1)}) custom-call(bf16[128,256]{1,0:T(8,128)(2,1)S(1)} %get-tuple-element.50.after_ref.refs_0_, s32[1]{0:T(128)} %bitcast.15.half_ref, bf16[1,7168,256]{2,1,0:T(8,128)(2,1)} %gate_hbm.3, bf16[1,7168,256]{2,1,0:T(8,128)(2,1)} %up_hbm.3, ...), custom_call_target="tpu_custom_call" | custom-call | bytes 22020096 | tf_op jit(solution)/shard_map/fetch_experts/pallas_call | solution.py:431
  94.1 22.1 %all_to_all.32.y_ref = bf16[16,192,256]{2,1,0:T(8,128)(2,1)S(1)} all-to-all(bf16[16,192,256]{2,1,0:T(8,128)(2,1)S(1)} %slot_rows.1), channel_id=1, replica_groups=mesh['z'=4,'x'=4,'y'=4,'c'=2] {'x','y'}, dimensions={0} | all-to-all | bytes 3145728 | tf_op jit(solution)/shard_map/all_to_all | solution.py:621
  116.3 1.8 %gate_up.1 = (f32[192,1152]{1,0:T(8,128)S(1)}, bf16[192,1152]{1,0:T(8,128)(2,1)S(1)}) custom-call(bf16[16,192,256]{2,1,0:T(8,128)(2,1)S(1)} %all_to_all.32.y_ref, bf16[3584,1024]{1,0:T(8,128)(2,1)S(1)} %get-tuple-element.55.w_ref), custom_call_target="tpu_custom_call" | custom-call | tf_op jit(solution)/shard_map/gate_up/pallas_call | solution.py:462
  118.0 5.2 %collective-permute-start.7 = (bf16[192,1152]{1,0:T(8,128)(2,1)S(1)}, bf16[192,1152]{1,0:T(8,128)(2,1)S(1)}, u32[]{:S(2)}, u32[]{:S(2)}) collective-permute-start(bf16[192,1152]{1,0:T(8,128)(2,1)S(1)} %get-tuple-element.57), channel_id=1, source_target_pairs={{0,1},{1,0},{2,3},{3,2},{4,5},{5,4},{6,7},{7,6},{8,9},{9,8},{10,11... | collective-permute-start | bytes 1327112 | tf_op jit(solution)/shard_map/ppermute | solution.py:530
  123.2 1.4 collective-permute-done.7.got_ref
  124.6 1.7 down.1
  126.3 22.3 %all_to_all.33.out_ref = bf16[16,336,128]{2,1,0:T(8,128)(2,1)S(1)} all-to-all(bf16[16,336,128]{2,1,0:T(8,128)(2,1)S(1)} %down.1), channel_id=1, replica_groups=mesh['z'=4,'x'=4,'y'=4,'c'=2] {'x','y'}, dimensions={0} | all-to-all | bytes 2752512 | tf_op jit(solution)/shard_map/all_to_all | solution.py:625
  148.6 1.6 combine_rows.1
  150.2 18.2 %all_to_all.34.total_ref = bf16[128,4,224]{2,1,0:T(4,128)(2,1)S(1)} all-to-all(bf16[128,4,224]{2,1,0:T(4,128)(2,1)S(1)} %combine_rows.1), channel_id=1, replica_groups=mesh['z'=4,'x'=4,'y'=4,'c'=2] {'z','x','y','c'}, dimensions={0} | all-to-all | bytes 458752 | tf_op jit(solution)/shard_map/all_to_all | solution.py:628
  (64 shorter events, 12.2 us)
Async XLA Ops:
  0.0 24.0 %copy-start = (bf16[7168,32]{0,1:T(8,128)(2,1)S(1)}, bf16[7168,32]{0,1:T(8,128)(2,1)}, u32[]{:S(2)}) copy-start(bf16[7168,32]{0,1:T(8,128)(2,1)} %param.25) | copy-start | bytes 1376260
  3.0 8.8 %copy-start.5 = (bf16[4,7168]{1,0:T(4,128)(2,1)S(1)}, bf16[4,7168]{1,0:T(4,128)(2,1)}, u32[]{:S(2)}) copy-start(bf16[4,7168]{1,0:T(4,128)(2,1)} %param.21) | copy-start | bytes 172036
  3.0 39.9 %all-to-all-start = ((bf16[32,288,128]{2,1,0:T(8,128)(2,1)}), bf16[32,288,128]{2,1,0:T(8,128)(2,1)S(1)}, u32[]{:S(2)}, u32[]{:S(2)}) async-start(bf16[32,288,128]{2,1,0:T(8,128)(2,1)} %spread.1), calls=%async_computation | async-start | bytes 4718592 | tf_op jit(solution)/shard_map/all_to_all | solution.py:559
  12.5 7.6 %copy-start.8 = (s32[1,3]{1,0:T(1,128)S(1)}, s32[1,3]{1,0:T(1,128)}, u32[]{:S(2)}) copy-start(s32[1,3]{1,0:T(1,128)} %param.18) | copy-start | bytes 40
  12.5 7.7 %copy-start.2 = (bf16[4,576]{1,0:T(4,128)(2,1)S(1)}, bf16[4,576]{1,0:T(4,128)(2,1)}, u32[]{:S(2)}) copy-start(bf16[4,576]{1,0:T(4,128)(2,1)} %entry_ref.1) | copy-start | bytes 13828
  12.5 7.7 %copy-start.3 = (bf16[4,128,576]{1,2,0:T(8,128)(2,1)S(1)}, bf16[4,128,576]{1,2,0:T(8,128)(2,1)}, u32[]{:S(2)}) copy-start(bf16[4,128,576]{1,2,0:T(8,128)(2,1)} %param.19) | copy-start | bytes 1769476
  12.5 7.9 %copy-start.6 = (s32[512,8]{0,1:T(8,128)S(1)}, s32[512,8]{0,1:T(8,128)}, u32[]{:S(2)}) copy-start(s32[512,8]{0,1:T(8,128)} %param.26) | copy-start | bytes 49156
  19.2 17.4 %collective-permute-start.2 = (bf16[256,3584]{1,0:T(8,128)(2,1)}, bf16[256,3584]{1,0:T(8,128)(2,1)}, u32[]{:S(2)}, u32[]{:S(2)}) collective-permute-start(bf16[256,3584]{1,0:T(8,128)(2,1)} %get-tuple-element.35), channel_id=1, source_target_pairs={{0,1},{1,0},{2,3},{3,2},{4,5},{5,4},{6,7},{7,6},{8,9},{9,8},{10,11... | collective-permute-start | bytes 5505032 | tf_op jit(solution)/shard_map/ppermute | solution.py:530
  19.5 23.3 %collective-permute-start.1 = (bf16[2,3584,256]{2,1,0:T(8,128)(2,1)}, bf16[2,3584,256]{2,1,0:T(8,128)(2,1)}, u32[]{:S(2)}, u32[]{:S(2)}) collective-permute-start(bf16[2,3584,256]{2,1,0:T(8,128)(2,1)} %get-tuple-element.34), channel_id=1, source_target_pairs={{0,1},{1,0},{2,3},{3,2},{4,5},{5,4},{6,7},{7,6},{8,9},{9,8},{10,11... | collective-permute-start | bytes 11010056 | tf_op jit(solution)/shard_map/ppermute | solution.py:530
  19.8 23.0 %collective-permute-start = (bf16[528,3584]{1,0:T(8,128)(2,1)}, bf16[528,3584]{1,0:T(8,128)(2,1)}, u32[]{:S(2)}, u32[]{:S(2)}) collective-permute-start(bf16[528,3584]{1,0:T(8,128)(2,1)} %get-tuple-element.33), channel_id=1, source_target_pairs={{0,1},{1,0},{2,3},{3,2},{4,5},{5,4},{6,7},{7,6},{8,9},{9,8},{10,11... | collective-permute-start | bytes 11354120 | tf_op jit(solution)/shard_map/ppermute | solution.py:530
  22.5 0.9 copy-start.4
  24.0 3.4 %copy-start.7 = (s32[512,32]{0,1:T(8,128)}, s32[512,32]{0,1:T(8,128)S(1)}, u32[]{:S(2)}) copy-start(s32[512,32]{0,1:T(8,128)S(1)} %fusion.9) | copy-start | bytes 196612
  62.8 1.4 collective-permute-start.3
  84.7 8.8 %collective-permute-start.6 = (bf16[128,256]{1,0:T(8,128)(2,1)S(1)}, bf16[128,256]{1,0:T(8,128)(2,1)S(1)}, u32[]{:S(2)}, u32[]{:S(2)}) collective-permute-start(bf16[128,256]{1,0:T(8,128)(2,1)S(1)} %get-tuple-element.50.after_ref.refs_0_), channel_id=1, source_target_pairs={{0,96},{32,0},{64,32},{96,64},{1,97},{33,1},{65,33},{97,65},{2,98}... | collective-permute-start | bytes 196616 | tf_op jit(solution)/shard_map/ppermute | solution.py:618
  88.5 5.0 %collective-permute-start.5 = (bf16[128,256]{1,0:T(8,128)(2,1)S(1)}, bf16[128,256]{1,0:T(8,128)(2,1)S(1)}, u32[]{:S(2)}, u32[]{:S(2)}) collective-permute-start(bf16[128,256]{1,0:T(8,128)(2,1)S(1)} %get-tuple-element.50.after_ref.refs_0_), channel_id=1, source_target_pairs={{0,64},{32,96},{64,0},{96,32},{1,65},{33,97},{65,1},{97,33},{2,66}... | collective-permute-start | bytes 196616 | tf_op jit(solution)/shard_map/ppermute | solution.py:618
  88.5 5.0 %collective-permute-start.4 = (bf16[128,256]{1,0:T(8,128)(2,1)S(1)}, bf16[128,256]{1,0:T(8,128)(2,1)S(1)}, u32[]{:S(2)}, u32[]{:S(2)}) collective-permute-start(bf16[128,256]{1,0:T(8,128)(2,1)S(1)} %get-tuple-element.50.after_ref.refs_0_), channel_id=1, source_target_pairs={{0,32},{32,64},{64,96},{96,0},{1,33},{33,65},{65,97},{97,1},{2,34}... | collective-permute-start | bytes 196616 | tf_op jit(solution)/shard_map/ppermute | solution.py:618
  118.0 6.6 %collective-permute-start.7 = (bf16[192,1152]{1,0:T(8,128)(2,1)S(1)}, bf16[192,1152]{1,0:T(8,128)(2,1)S(1)}, u32[]{:S(2)}, u32[]{:S(2)}) collective-permute-start(bf16[192,1152]{1,0:T(8,128)(2,1)S(1)} %get-tuple-element.57), channel_id=1, source_target_pairs={{0,1},{1,0},{2,3},{3,2},{4,5},{5,4},{6,7},{7,6},{8,9},{9,8},{10,11... | collective-permute-start | bytes 1327112 | tf_op jit(solution)/shard_map/ppermute | solution.py:530
  124.6 44.5 %copy-start.1 = (bf16[7168,32]{0,1:T(8,128)(2,1)S(1)}, bf16[7168,32]{0,1:T(8,128)(2,1)}, u32[]{:S(2)}) copy-start(bf16[7168,32]{0,1:T(8,128)(2,1)} %param.25) | copy-start | bytes 1376260

commit v7 on v6

--- a/solution.py
+++ b/solution.py
@@ -142,19 +142,21 @@
     uv_copy = pltpu.make_async_copy(uv_hbm, uv_ref, sems.at[2])
     depth = w_hbm.shape[0]
     at = pl.ds(pl.multiple_of(half_ref[0] * HALF, 128), HALF)
-    w_copies = [pltpu.make_async_copy(res_hbm.at[:, at], w_ref.at[pl.ds(depth, 16), :], sems.at[3])]
+    w_copies = [pltpu.make_async_copy(res_hbm.at[:, at], w_ref.at[pl.ds(2 * depth, 16), :], sems.at[3])]
     span = depth // PARTS
     for n in range(PARTS):
         rows = pl.ds(n * span, span)
         w_copies.append(pltpu.make_async_copy(w_hbm.at[rows, at], w_ref.at[rows, :], sems.at[4 + n]))
-        span_got = span + 16 if n == PARTS - 1 else span
         w_copies.append(
             pltpu.make_async_copy(
-                got_hbm.at[pl.ds(n * span, span_got), :],
-                w_ref.at[pl.ds(depth + 16 + n * span, span_got), :],
-                sems.at[4 + PARTS + n],
+                got_hbm.at[rows, :], w_ref.at[pl.ds(depth + n * span, span), :], sems.at[4 + PARTS + n]
             )
         )
+    w_copies.append(
+        pltpu.make_async_copy(
+            got_hbm.at[pl.ds(depth, 16), :], w_ref.at[pl.ds(2 * depth + 16, 16), :], sems.at[4 + 2 * PARTS]
+        )
+    )
     start_all([query_copy, old_copy, uv_copy] + w_copies)
     scale_factor = (NOPE + ROPE) ** (-0.5)
     sources, tokens = cache_ref.shape[0], cache_ref.shape[1] * 128 // query_ref.shape[0]
@@ -209,7 +211,7 @@
         scratch_shapes=[
             pltpu.VMEM((rows, LAT), BF16),
             pltpu.VMEM(query.shape, BF16),
-            pltpu.SemaphoreType.DMA((4 + 2 * PARTS,)),
+            pltpu.SemaphoreType.DMA((5 + 2 * PARTS,)),
         ],
         compiler_params=pltpu.CompilerParams(vmem_limit_bytes=LARGE),
         name="prompt_attention",
@@ -244,8 +246,7 @@
 
 
 def project_kernel(own_ref, got_ref, place_ref, w_ref, out_ref):
-    depth = own_ref.shape[1]
-    lhs = (own_ref[...], place_ref[0], got_ref[...], place_ref[1])
+    lhs = (own_ref[...], got_ref[...], jnp.concatenate([place_ref[0], place_ref[1]], axis=1))
     for i in range(STEPS):
         at, acc = 0, jnp.zeros((ROWS, BLK), F32)
         for left in lhs:

time: 170 us -> 170 us (level)
  no operation moved by 1% of the time
where the time goes in v7:
time: 170 us; the launch traced here: 169 us
  blocking collectives  95.4 us (56%)
  Pallas kernels  27.6 us (16%)
  starting transfers between devices  19.3 us (11%)
  local copies, waits for them, and re-layouts  9.94 us (6%)
  waiting for transfers between devices  9.08 us (5%)
  matrix products  5.82 us (3%)
    all_to_all x1, blocking collectives, per_device(): out = lax.all_to_all(out, ('x', 'y'), 0, 0, tiled=True)  22.3 us
    all_to_all x1, blocking collectives, per_device(): slotted = lax.all_to_all(slotted, ('x', 'y'), 0, 0, tiled=True)  22.1 us
    all_to_all x1, blocking collectives, per_device(): total = lax.all_to_all(total, ('z', 'x', 'y', 'c'), 0, 0, tiled=True)  18.2 us
    all_to_all x1, blocking collectives, per_device(): partial = lax.all_to_all(partial, ('x', 'y'), 0, 0, tiled=True)  17.6 us
    all_to_all x1, blocking collectives, per_device(): lax.all_to_all(context.reshape(NDEV, -1, LAT), ('x', 'y', 'c'), 0, 0, til...  15.3 us
    all_to_all x1, starting transfers between devices, per_device(): lax.all_to_all(spread(assignment, prompt_cache), ('x', 'y', 'c'), 0, 0, t...  8.73 us
    pallas_call x1, Pallas kernels, give_weights(): pl.pallas_call(give_kernel, in_specs=[SCALAR] + [ANYWHERE] * 5, out_specs...  6.75 us
    all_to_all x1, waiting for transfers between devices, per_device(): lax.all_to_all(spread(assignment, prompt_cache), ('x', 'y', 'c'), 0, 0, t...  6.25 us
  transfers between devices with their start and end apart: 9, of which 4 were waited for; matrix products, arithmetic and copies ran while one was open for 10% of the time, Pallas kernels for 7%

profile of v7, /device:TPU:1, one launch (start us, length us, event | category | flops | bytes accessed | tf_op | source)
XLA Modules:
  0.0 168.9 jit_solution(16375049998614886274)
XLA Ops:
  0.0 3.0 %spread.1 = bf16[32,288,128]{2,1,0:T(8,128)(2,1)} custom-call(s32[1,32]{1,0:T(1,128)} %owners_hbm.1, bf16[32,64,576]{2,1,0:T(8,128)(2,1)} %cache_ref.1), custom_call_target="tpu_custom_call" | custom-call | tf_op jit(solution)/shard_map/spread/pallas_call | solution.py:117
  3.0 8.7 %all-to-all-start = ((bf16[32,288,128]{2,1,0:T(8,128)(2,1)}), bf16[32,288,128]{2,1,0:T(8,128)(2,1)S(1)}, u32[]{:S(2)}, u32[]{:S(2)}) async-start(bf16[32,288,128]{2,1,0:T(8,128)(2,1)} %spread.1), calls=%async_computation | async-start | bytes 4718592 | tf_op jit(solution)/shard_map/all_to_all | solution.py:560
  12.5 6.8 %give_weights.1 = (bf16[528,3584]{1,0:T(8,128)(2,1)}, bf16[2,3584,256]{2,1,0:T(8,128)(2,1)}, bf16[256,3584]{1,0:T(8,128)(2,1)}) custom-call(s32[1]{0:T(128)S(6)} %sub.49.half_ref, bf16[512,7168]{1,0:T(8,128)(2,1)} %w_hbm.1, bf16[16,7168]{1,0:T(8,128)(2,1)} %pad.9.res_hbm, bf16[1,7168,256]{2,1,0:T(8,128)(2,1)} %gate_hbm.3, bf16[1,7168,256]{2,1,0:T(8,128)(2,1)} %up_hbm.3, ...), custom_call_target="tpu_custom_call" | custom-call | tf_op jit(solution)/shard_map/give_weights/pallas_call | solution.py:390
  20.4 2.1 %fusion.26 = (f32[3,128]{1,0:T(4,128)S(1)}, f32[3,128,512]{2,1,0:T(8,128)S(1)}) fusion(bf16[4,128,576]{1,2,0:T(8,128)(2,1)S(1)} %copy-done.3, bf16[3,512,576]{1,2,0:T(8,128)(2,1)} %param.17, pred[3,512]{1,0:T(4,128)(4,1)S(1)} %iota_compare_fusion.6), kind=kOutput, calls=%fused_computation.54 | convolution fusion | flops 227081856 | bytes 3148800 | tf_op jit(solution)/shard_map/vmap(hc,kc->hk)/dot_general | solution.py:55
  24.2 3.1 %fusion.6 = bf16[3,128,512]{2,1,0:T(8,128)(2,1)} fusion(bf16[3,512,576]{1,2,0:T(8,128)(2,1)} %param.17, f32[3,128,512]{2,1,0:T(8,128)} %copy-done.4, f32[3,512]{1,0:T(4,128)S(1)} %slice_convert_fusion, f32[3,128]{1,0:T(4,128)S(1)} %get-tuple-element.62, f32[3,128]{1,0:T(4,128)S(1)} %get-tuple-element.61, f32[3,128]{1,0:T(4,128)S(1)} %fusion.21), kind=kOutput, calls=%fused_computation.6 | convolution fusion | flops 202506240 | bytes 2763264 | tf_op jit(solution)/shard_map/vmap(hk,kl->hl)/dot_general | solution.py:65
  27.6 1.1 reshape.133
  30.0 2.0 %reshape.134.old_hbm = bf16[512,512]{1,0:T(8,128)(2,1)} reshape(bf16[32,4,4,512]{3,2,1,0:T(4,128)(2,1)} %pad.8) | data formatting | bytes 1048576 | tf_op jit(solution)/shard_map/reshape | solution.py:595
  35.1 1.6 slice_bitcast_fusion.query_hbm
  36.6 6.2 %all-to-all-done.cache_ref = bf16[32,288,128]{2,1,0:T(8,128)(2,1)S(1)} async-done(((bf16[32,288,128]{2,1,0:T(8,128)(2,1)}), bf16[32,288,128]{2,1,0:T(8,128)(2,1)S(1)}, u32[]{:S(2)}, u32[]{:S(2)}) %all-to-all-start) | async-done | bytes 2359328 | tf_op jit(solution)/shard_map/all_to_all | solution.py:560
  42.9 3.6 %prompt_attention.1 = (bf16[512,512]{1,0:T(8,128)(2,1)S(1)}, bf16[4,512,128]{2,1,0:T(8,128)(2,1)S(1)}, bf16[1056,3584]{1,0:T(8,128)(2,1)S(1)}) custom-call(s32[1]{0:T(128)} %bitcast.15.half_ref, bf16[576,128]{1,0:T(8,128)(2,1)} %slice_bitcast_fusion.query_hbm, bf16[32,288,128]{2,1,0:T(8,128)(2,1)S(1)} %all-to-all-done.cache_ref, ...), custom_call_target="tpu_custom_call" | custom-call | tf_op jit(solution)/shard_map/prompt_attention/pallas_call | solution.py:204
  46.5 15.3 %all_to_all.30 = bf16[32,16,512]{2,1,0:T(8,128)(2,1)S(1)} all-to-all(bf16[32,16,512]{2,1,0:T(8,128)(2,1)S(1)} %bitcast.50), channel_id=1, replica_groups=mesh['z'=4,'x'=4,'y'=4,'c'=2] {'x','y','c'}, dimensions={0} | all-to-all | bytes 1048576 | tf_op jit(solution)/shard_map/all_to_all | solution.py:608
  62.9 1.3 collective-permute-done.3.got_ref
  64.2 1.8 %project.1 = bf16[16,224,128]{2,1,0:T(8,128)(2,1)S(1)} custom-call(bf16[128,512]{1,0:T(8,128)(2,1)S(1)} %head_values.1.own_ref, bf16[128,512]{1,0:T(8,128)(2,1)S(1)} %collective-permute-done.3.got_ref, bf16[2,128,16]{2,1,0:T(8,128)(2,1)S(1)} %fusion.17.place_ref, bf16[1056,3584]{1,0:T(8,128)(2,1)S(1)} %get-tuple-element.46.w_ref), custom_call_target="tpu_custom_call" | custom-call | tf_op jit(solution)/shard_map/project/pallas_call | solution.py:262
  66.0 17.6 %all_to_all.31.part_ref = bf16[16,224,128]{2,1,0:T(8,128)(2,1)S(1)} all-to-all(bf16[16,224,128]{2,1,0:T(8,128)(2,1)S(1)} %project.1), channel_id=1, replica_groups=mesh['z'=4,'x'=4,'y'=4,'c'=2] {'x','y'}, dimensions={0} | all-to-all | bytes 1835008 | tf_op jit(solution)/shard_map/all_to_all | solution.py:613
  84.5 3.8 %collective-permute-start.6 = (bf16[128,256]{1,0:T(8,128)(2,1)S(1)}, bf16[128,256]{1,0:T(8,128)(2,1)S(1)}, u32[]{:S(2)}, u32[]{:S(2)}) collective-permute-start(bf16[128,256]{1,0:T(8,128)(2,1)S(1)} %get-tuple-element.50.after_ref.refs_0_), channel_id=1, source_target_pairs={{0,96},{32,0},{64,32},{96,64},{1,97},{33,1},{65,33},{97,65},{2,98}... | collective-permute-start | bytes 196616 | tf_op jit(solution)/shard_map/ppermute | solution.py:619
  89.0 4.2 %fetch_experts.1 = (bf16[3584,1024]{1,0:T(8,128)(2,1)S(1)}, bf16[512,3584]{1,0:T(8,128)(2,1)S(1)}) custom-call(bf16[128,256]{1,0:T(8,128)(2,1)S(1)} %get-tuple-element.50.after_ref.refs_0_, s32[1]{0:T(128)} %bitcast.15.half_ref, bf16[1,7168,256]{2,1,0:T(8,128)(2,1)} %gate_hbm.3, bf16[1,7168,256]{2,1,0:T(8,128)(2,1)} %up_hbm.3, ...), custom_call_target="tpu_custom_call" | custom-call | bytes 22020096 | tf_op jit(solution)/shard_map/fetch_experts/pallas_call | solution.py:432
  93.9 22.1 %all_to_all.32.y_ref = bf16[16,192,256]{2,1,0:T(8,128)(2,1)S(1)} all-to-all(bf16[16,192,256]{2,1,0:T(8,128)(2,1)S(1)} %slot_rows.1), channel_id=1, replica_groups=mesh['z'=4,'x'=4,'y'=4,'c'=2] {'x','y'}, dimensions={0} | all-to-all | bytes 3145728 | tf_op jit(solution)/shard_map/all_to_all | solution.py:622
  116.0 1.8 %gate_up.1 = (f32[192,1152]{1,0:T(8,128)S(1)}, bf16[192,1152]{1,0:T(8,128)(2,1)S(1)}) custom-call(bf16[16,192,256]{2,1,0:T(8,128)(2,1)S(1)} %all_to_all.32.y_ref, bf16[3584,1024]{1,0:T(8,128)(2,1)S(1)} %get-tuple-element.55.w_ref), custom_call_target="tpu_custom_call" | custom-call | tf_op jit(solution)/shard_map/gate_up/pallas_call | solution.py:463
  117.8 5.2 %collective-permute-start.7 = (bf16[192,1152]{1,0:T(8,128)(2,1)S(1)}, bf16[192,1152]{1,0:T(8,128)(2,1)S(1)}, u32[]{:S(2)}, u32[]{:S(2)}) collective-permute-start(bf16[192,1152]{1,0:T(8,128)(2,1)S(1)} %get-tuple-element.57), channel_id=1, source_target_pairs={{0,1},{1,0},{2,3},{3,2},{4,5},{5,4},{6,7},{7,6},{8,9},{9,8},{10,11... | collective-permute-start | bytes 1327112 | tf_op jit(solution)/shard_map/ppermute | solution.py:531
  123.0 1.4 collective-permute-done.7.got_ref
  124.4 1.7 down.1
  126.1 22.3 %all_to_all.33.out_ref = bf16[16,336,128]{2,1,0:T(8,128)(2,1)S(1)} all-to-all(bf16[16,336,128]{2,1,0:T(8,128)(2,1)S(1)} %down.1), channel_id=1, replica_groups=mesh['z'=4,'x'=4,'y'=4,'c'=2] {'x','y'}, dimensions={0} | all-to-all | bytes 2752512 | tf_op jit(solution)/shard_map/all_to_all | solution.py:626
  148.3 1.6 combine_rows.1
  149.9 18.2 %all_to_all.34.total_ref = bf16[128,4,224]{2,1,0:T(4,128)(2,1)S(1)} all-to-all(bf16[128,4,224]{2,1,0:T(4,128)(2,1)S(1)} %combine_rows.1), channel_id=1, replica_groups=mesh['z'=4,'x'=4,'y'=4,'c'=2] {'z','x','y','c'}, dimensions={0} | all-to-all | bytes 458752 | tf_op jit(solution)/shard_map/all_to_all | solution.py:629
  (64 shorter events, 12.2 us)
Async XLA Ops:
  0.0 24.0 %copy-start = (bf16[7168,32]{0,1:T(8,128)(2,1)S(1)}, bf16[7168,32]{0,1:T(8,128)(2,1)}, u32[]{:S(2)}) copy-start(bf16[7168,32]{0,1:T(8,128)(2,1)} %param.25) | copy-start | bytes 1376260
  3.0 8.8 %copy-start.5 = (bf16[4,7168]{1,0:T(4,128)(2,1)S(1)}, bf16[4,7168]{1,0:T(4,128)(2,1)}, u32[]{:S(2)}) copy-start(bf16[4,7168]{1,0:T(4,128)(2,1)} %param.21) | copy-start | bytes 172036
  3.0 39.9 %all-to-all-start = ((bf16[32,288,128]{2,1,0:T(8,128)(2,1)}), bf16[32,288,128]{2,1,0:T(8,128)(2,1)S(1)}, u32[]{:S(2)}, u32[]{:S(2)}) async-start(bf16[32,288,128]{2,1,0:T(8,128)(2,1)} %spread.1), calls=%async_computation | async-start | bytes 4718592 | tf_op jit(solution)/shard_map/all_to_all | solution.py:560
  12.5 7.6 %copy-start.8 = (s32[1,3]{1,0:T(1,128)S(1)}, s32[1,3]{1,0:T(1,128)}, u32[]{:S(2)}) copy-start(s32[1,3]{1,0:T(1,128)} %param.18) | copy-start | bytes 40
  12.5 7.7 %copy-start.2 = (bf16[4,576]{1,0:T(4,128)(2,1)S(1)}, bf16[4,576]{1,0:T(4,128)(2,1)}, u32[]{:S(2)}) copy-start(bf16[4,576]{1,0:T(4,128)(2,1)} %entry_ref.1) | copy-start | bytes 13828
  12.5 7.7 %copy-start.3 = (bf16[4,128,576]{1,2,0:T(8,128)(2,1)S(1)}, bf16[4,128,576]{1,2,0:T(8,128)(2,1)}, u32[]{:S(2)}) copy-start(bf16[4,128,576]{1,2,0:T(8,128)(2,1)} %param.19) | copy-start | bytes 1769476
  12.5 7.9 %copy-start.6 = (s32[512,8]{0,1:T(8,128)S(1)}, s32[512,8]{0,1:T(8,128)}, u32[]{:S(2)}) copy-start(s32[512,8]{0,1:T(8,128)} %param.26) | copy-start | bytes 49156
  19.2 17.4 %collective-permute-start.2 = (bf16[256,3584]{1,0:T(8,128)(2,1)}, bf16[256,3584]{1,0:T(8,128)(2,1)}, u32[]{:S(2)}, u32[]{:S(2)}) collective-permute-start(bf16[256,3584]{1,0:T(8,128)(2,1)} %get-tuple-element.35), channel_id=1, source_target_pairs={{0,1},{1,0},{2,3},{3,2},{4,5},{5,4},{6,7},{7,6},{8,9},{9,8},{10,11... | collective-permute-start | bytes 5505032 | tf_op jit(solution)/shard_map/ppermute | solution.py:531
  19.6 23.3 %collective-permute-start.1 = (bf16[2,3584,256]{2,1,0:T(8,128)(2,1)}, bf16[2,3584,256]{2,1,0:T(8,128)(2,1)}, u32[]{:S(2)}, u32[]{:S(2)}) collective-permute-start(bf16[2,3584,256]{2,1,0:T(8,128)(2,1)} %get-tuple-element.34), channel_id=1, source_target_pairs={{0,1},{1,0},{2,3},{3,2},{4,5},{5,4},{6,7},{7,6},{8,9},{9,8},{10,11... | collective-permute-start | bytes 11010056 | tf_op jit(solution)/shard_map/ppermute | solution.py:531
  19.8 23.0 %collective-permute-start = (bf16[528,3584]{1,0:T(8,128)(2,1)}, bf16[528,3584]{1,0:T(8,128)(2,1)}, u32[]{:S(2)}, u32[]{:S(2)}) collective-permute-start(bf16[528,3584]{1,0:T(8,128)(2,1)} %get-tuple-element.33), channel_id=1, source_target_pairs={{0,1},{1,0},{2,3},{3,2},{4,5},{5,4},{6,7},{7,6},{8,9},{9,8},{10,11... | collective-permute-start | bytes 11354120 | tf_op jit(solution)/shard_map/ppermute | solution.py:531
  22.5 0.9 copy-start.4
  24.0 3.4 %copy-start.7 = (s32[512,32]{0,1:T(8,128)}, s32[512,32]{0,1:T(8,128)S(1)}, u32[]{:S(2)}) copy-start(s32[512,32]{0,1:T(8,128)S(1)} %fusion.9) | copy-start | bytes 196612
  62.8 1.4 collective-permute-start.3
  84.5 8.8 %collective-permute-start.6 = (bf16[128,256]{1,0:T(8,128)(2,1)S(1)}, bf16[128,256]{1,0:T(8,128)(2,1)S(1)}, u32[]{:S(2)}, u32[]{:S(2)}) collective-permute-start(bf16[128,256]{1,0:T(8,128)(2,1)S(1)} %get-tuple-element.50.after_ref.refs_0_), channel_id=1, source_target_pairs={{0,96},{32,0},{64,32},{96,64},{1,97},{33,1},{65,33},{97,65},{2,98}... | collective-permute-start | bytes 196616 | tf_op jit(solution)/shard_map/ppermute | solution.py:619
  88.3 5.0 %collective-permute-start.5 = (bf16[128,256]{1,0:T(8,128)(2,1)S(1)}, bf16[128,256]{1,0:T(8,128)(2,1)S(1)}, u32[]{:S(2)}, u32[]{:S(2)}) collective-permute-start(bf16[128,256]{1,0:T(8,128)(2,1)S(1)} %get-tuple-element.50.after_ref.refs_0_), channel_id=1, source_target_pairs={{0,64},{32,96},{64,0},{96,32},{1,65},{33,97},{65,1},{97,33},{2,66}... | collective-permute-start | bytes 196616 | tf_op jit(solution)/shard_map/ppermute | solution.py:619
  88.3 5.0 %collective-permute-start.4 = (bf16[128,256]{1,0:T(8,128)(2,1)S(1)}, bf16[128,256]{1,0:T(8,128)(2,1)S(1)}, u32[]{:S(2)}, u32[]{:S(2)}) collective-permute-start(bf16[128,256]{1,0:T(8,128)(2,1)S(1)} %get-tuple-element.50.after_ref.refs_0_), channel_id=1, source_target_pairs={{0,32},{32,64},{64,96},{96,0},{1,33},{33,65},{65,97},{97,1},{2,34}... | collective-permute-start | bytes 196616 | tf_op jit(solution)/shard_map/ppermute | solution.py:619
  117.8 6.6 %collective-permute-start.7 = (bf16[192,1152]{1,0:T(8,128)(2,1)S(1)}, bf16[192,1152]{1,0:T(8,128)(2,1)S(1)}, u32[]{:S(2)}, u32[]{:S(2)}) collective-permute-start(bf16[192,1152]{1,0:T(8,128)(2,1)S(1)} %get-tuple-element.57), channel_id=1, source_target_pairs={{0,1},{1,0},{2,3},{3,2},{4,5},{5,4},{6,7},{7,6},{8,9},{9,8},{10,11... | collective-permute-start | bytes 1327112 | tf_op jit(solution)/shard_map/ppermute | solution.py:531
  124.4 44.5 %copy-start.1 = (bf16[7168,32]{0,1:T(8,128)(2,1)S(1)}, bf16[7168,32]{0,1:T(8,128)(2,1)}, u32[]{:S(2)}) copy-start(bf16[7168,32]{0,1:T(8,128)(2,1)} %param.25) | copy-start | bytes 1376260
